TPU v7x, 32 devices: a whole 2x2x4 slice. The times are simulated.
32 devices in a mesh: shard: 2 (over y), loop: 16 (over z, x, core).
Axes of the slice: x: 2, y: 2, z: 4, core: 2. Of those that a mesh axis runs over, the one named last changes fastest.
Arguments:
- hidden: bfloat16 [61440, 768], P(('shard', 'loop')), may hold values from -6 to 6
- segment: int32 [61440], P(('shard', 'loop')), may hold values from 0 to 8, as said below
- counts: int32 [256], P(('shard', 'loop')), may hold values from 1 to 720, as said below
- w_proj: bfloat16 [768, 128], replicated, may hold values from -0.21875 to 0.21875
- seeds: bfloat16 [256, 32, 128], P('loop', 'shard'), may hold values from -6 to 6
Outputs:
- scores: float32 [256, 256], P(('shard', 'loop'))
Inputs may be any that keep to these rules, and one draw needn't show every extreme that they name: On every device one document has exactly 720 tokens, and a device's counts sum to less than 1920. `segment`: within a device, document k occupies counts of that document consecutive slots, documents in order of k from the first slot; all later slots hold 8, and every device has at least one such slot.
All inputs are finite; a program needn't handle non-finite values.
Results may differ from a plain program's by a relative error of at most 0.00055.
Values may be sent and summed in bfloat16 or wider, within the bound.
No kernel may reach another device: no remote copies, remote signals or barrier semaphores. Data moves between devices by JAX's collectives and lax.ppermute only.
A program may use at most 64 MiB of HBM per device.

v0:
```python
import jax
import jax.numpy as jnp
from jax import lax
from jax.sharding import PartitionSpec as P

BETA = 16.0
EPS = 1e-06


def unit_rows(values):
    values = values.astype(jnp.float32)
    return (values * lax.rsqrt(jnp.sum(values * values, axis=-1, keepdims=True) + EPS)).astype(
        jnp.bfloat16
    )


def body(hidden, segment, counts, w_proj, seeds):
    projected = jnp.dot(hidden, w_proj, preferred_element_type=jnp.float32)
    doc_vectors = unit_rows(projected)
    doc_count = counts.shape[0]
    member = (segment[None, :] == jnp.arange(doc_count, dtype=jnp.int32)[:, None]).astype(
        jnp.bfloat16
    )
    lengths = counts.astype(jnp.float32)[:, None]
    own_seeds = lax.all_gather(unit_rows(seeds), "shard", axis=1, tiled=True)
    group = own_seeds.shape[0]
    qtokens = own_seeds.shape[1]
    width = own_seeds.shape[2]

    def score_group(block):
        flat = block.reshape(group * qtokens, width)
        sims = lax.dot_general(
            doc_vectors, flat, (((1,), (1,)), ((), ())), preferred_element_type=jnp.float32
        )
        weights = jnp.exp(BETA * sims)
        upper = weights.astype(jnp.bfloat16)
        lower = (weights - upper.astype(jnp.float32)).astype(jnp.bfloat16)
        mass = jnp.dot(member, upper, preferred_element_type=jnp.float32) + jnp.dot(
            member, lower, preferred_element_type=jnp.float32
        )
        logs = jnp.log(mass / lengths).reshape(doc_count, group, qtokens)
        return jnp.mean(logs, axis=-1)

    piece = lax.all_gather(own_seeds, "loop", axis=0, tiled=True)
    groups_here = piece.shape[0] // group
    result = lax.map(score_group, piece.reshape(groups_here, group, qtokens, width))
    return jnp.transpose(result, (1, 0, 2)).reshape(doc_count, groups_here * group)


def solution(mesh):
    in_specs = (
        P(("shard", "loop"), None),
        P(("shard", "loop")),
        P(("shard", "loop")),
        P(),
        P("loop", "shard", None),
    )
    out_specs = P(("shard", "loop"), None)
    return jax.shard_map(body, mesh=mesh, in_specs=in_specs, out_specs=out_specs, check_vma=False)
```

profile of v0, /device:TPU:0, one launch (start us, length us, event | category | flops | bytes accessed | tf_op | source)
XLA Modules:
  0.0 125.8 jit_solution(5875091822637708876)
XLA Ops:
  6.5 1.1 fusion.26
  7.7 0.9 fusion.27
  8.6 6.0 %all_gather.6 = bf16[16,32,128]{2,1,0:T(8,128)(2,1)} all-gather(bf16[16,16,128]{2,1,0:T(8,128)(2,1)S(1)} %fusion.27), channel_id=1, replica_groups=mesh['shard'=2,'loop'=16] {'shard'}, dimensions={1}, use_global_device_ids=true | all-gather | bytes 196608 | tf_op jit(solution)/shard_map/all_gather | solution.py:25
  14.6 2.0 %multiply_reduce_fusion = (f32[1920]{0:T(1024)S(1)}, f32[1920,128]{0,1:T(8,128)S(1)}) fusion(bf16[1920,768]{1,0:T(8,128)(2,1)S(1)} %copy-done, bf16[768,128]{1,0:T(8,128)(2,1)} %param.10), kind=kOutput, calls=%fused_computation.21 | convolution fusion | flops 377976960 | bytes 4136448 | tf_op jit(solution)/shard_map/dot_general | solution.py:18
  16.6 0.8 multiply_convert_fusion
  17.5 1.3 %copy.8 = bf16[1920,128]{1,0:T(8,128)(2,1)S(1)} copy(bf16[1920,128]{0,1:T(8,128)(2,1)} %multiply_convert_fusion) | data formatting | bytes 983040
  18.8 39.2 %all-gather.2.cloned.1.call-done = bf16[256,32,128]{2,1,0:T(8,128)(2,1)} async-done(((bf16[16,32,128]{2,1,0:T(8,128)(2,1)}), bf16[256,32,128]{2,1,0:T(8,128)(2,1)}) %all-gather.2.cloned.1.call-update) | async-done | bytes 2097168 | tf_op jit(solution)/shard_map/all_gather | solution.py:44
  57.9 59.4 %while.11 = (s32[]{:T(128)}, f32[16,8,16]{2,1,0:T(8,128)}, bf16[16,16,32,128]{3,2,1,0:T(8,128)(2,1)}, bf16[1920,128]{1,0:T(8,128)(2,1)S(1)}, f32[8,1]{0,1:T(1,12...) while((s32[]{:T(128)}, f32[16,8,16]{2,1,0:T(8,128)}, bf16[16,16,32,128]{3,2,1,0:T(8,128)(2,1)}, ...), condition=%wide.region_4.5_spmd.clone, body=%wide.region_2.4_spmd.clone.sunk | while | flops 290070528 | bytes 12800637 | solution.py:46
  57.9 0.9 constant_dynamic-slice_fusion.2
  60.2 0.7 fusion.48
  61.7 0.9 constant_dynamic-slice_fusion.2
  63.9 0.7 fusion.48
  65.4 0.9 constant_dynamic-slice_fusion.2
  69.1 0.9 constant_dynamic-slice_fusion.2
  72.8 0.9 constant_dynamic-slice_fusion.2
  76.5 0.9 constant_dynamic-slice_fusion.2
  80.2 0.9 constant_dynamic-slice_fusion.2
  82.4 0.7 fusion.48
  83.9 0.9 constant_dynamic-slice_fusion.2
  87.7 0.9 constant_dynamic-slice_fusion.2
  89.9 0.7 fusion.48
  91.4 0.9 constant_dynamic-slice_fusion.2
  93.6 0.7 fusion.48
  95.1 0.9 constant_dynamic-slice_fusion.2
  98.8 0.9 constant_dynamic-slice_fusion.2
  102.5 0.9 constant_dynamic-slice_fusion.2
  106.2 0.9 constant_dynamic-slice_fusion.2
  110.0 0.9 constant_dynamic-slice_fusion.2
  112.2 0.7 fusion.48
  113.7 0.9 constant_dynamic-slice_fusion.2
  115.9 0.7 fusion.48
  117.4 0.9 copy.9
  (102 shorter events, 40.4 us)
Async XLA Ops:
  6.5 8.1 %copy-start = (bf16[1920,768]{1,0:T(8,128)(2,1)S(1)}, bf16[1920,768]{1,0:T(8,128)(2,1)}, u32[]{:S(2)}) copy-start(bf16[1920,768]{1,0:T(8,128)(2,1)} %param.7) | copy-start | bytes 8847364
  6.5 12.2 %copy-start.2 = (s32[8]{0:T(128)S(1)}, s32[8]{0:T(128)}, u32[]{:S(2)}) copy-start(s32[8]{0:T(128)} %param.9) | copy-start | bytes 100
  6.5 51.4 %copy-start.1 = (s32[1920]{0:T(1024)S(1)}, s32[1920]{0:T(1024)}, u32[]{:S(2)}) copy-start(s32[1920]{0:T(1024)} %param.8) | copy-start | bytes 23044
  6.5 51.4 %all-gather.2.cloned.1.call-start = ((), (), s32[]{:S(2)}) async-start(), calls=%async_computation | async-start | bytes 2228224 | tf_op jit(solution)/shard_map/all_gather | solution.py:44
Sparse Core Ops, SparseCore 0:
  14.7 43.1 all-gather.1
where the time goes:
time: 126 us
  waiting for transfers between devices  39.2 us (31%)
  matrix products  34 us (27%)
  local copies, waits for them, and re-layouts  18.9 us (15%)
  other arithmetic  14 us (11%)
  between operations  13.5 us (11%)
  blocking collectives  5.97 us (5%)
    all_gather x1, waiting for transfers between devices, body(): piece = lax.all_gather(own_seeds, 'loop', axis=0, tiled=True)  39.2 us
    dynamic_slice x16, local copies, waits for them, and re-layouts, body(): lax.map(score_group, piece.reshape(groups_here, group, qtokens, width))  14.6 us
    dot_general x16, matrix products, score_group(): jnp.dot(member, lower, preferred_element_type=jnp.float32)  11.2 us
    dot_general x16, matrix products, score_group(): lax.dot_general(doc_vectors, flat, (((1,), (1,)), ((), ())), preferred_el...  10.8 us
    dot_general x16, matrix products, score_group(): jnp.dot(member, upper, preferred_element_type=jnp.float32)  10.1 us
    dynamic_update_slice x16, other arithmetic, body(): lax.map(score_group, piece.reshape(groups_here, group, qtokens, width))  9.57 us
    all_gather x1, blocking collectives, body(): own_seeds = lax.all_gather(unit_rows(seeds), 'shard', axis=1, tiled=True)  5.97 us
  transfers between devices with their start and end apart: 1, of which 1 were waited for; matrix products, arithmetic and copies ran while one was open for 3% of the time, Pallas kernels for 0%

commit v1 on v0

v1 whole, which is shorter than its diff:
```python
import functools

import jax
import jax.numpy as jnp
from jax import lax
from jax.experimental import pallas as pl
from jax.experimental.pallas import tpu as pltpu
from jax.sharding import PartitionSpec as P

BETA = 16.0
EPS = 1e-06
LOG2E = 1.4426950408889634
GROUP = 16
PIECE = 256
SMEM = pl.BlockSpec(memory_space=pltpu.SMEM)
VMEM = pl.BlockSpec(memory_space=pltpu.VMEM)


def unit_rows(values):
    values = values.astype(jnp.float32)
    return (values * lax.rsqrt(jnp.sum(values * values, axis=-1, keepdims=True) + EPS)).astype(
        jnp.bfloat16
    )


def params(mib):
    return pltpu.CompilerParams(vmem_limit_bytes=mib * 2**20)


def docs_kernel(counts, hidden, w_proj, rows_out, slot, keep, vectors):
    docs = counts.shape[0]
    rows = hidden.shape[0]
    groups = slot.shape[0]
    step = 384 if rows % 384 == 0 else rows
    for lo in range(0, rows, step):
        projected = jnp.dot(
            hidden[lo : lo + step, :], w_proj[...], preferred_element_type=jnp.float32
        )
        vectors[lo : lo + step, :] = unit_rows(projected).astype(jnp.float32)
    vectors[rows:, :] = jnp.zeros_like(vectors[rows:, :])
    tail = docs * GROUP
    rows_out[tail:, :] = jnp.zeros_like(rows_out[tail:, :])

    def fill(g, carry):
        slot[g] = docs
        keep[g] = 0.0
        return carry

    lax.fori_loop(0, groups, fill, 0, unroll=8)
    start = jnp.int32(0)
    first = jnp.int32(0)
    for d in range(docs):
        count = counts[d]
        full = count // GROUP

        def move(k, carry, d=d, start=start, first=first):
            g = first + k
            block = vectors[pl.ds(start + k * GROUP, GROUP), :]
            rows_out[pl.ds(pl.multiple_of(tail + g * GROUP, GROUP), GROUP), :] = block.astype(
                jnp.bfloat16
            )
            slot[g] = d
            keep[g] = jnp.where(k == 0, 0.0, 1.0)
            return carry

        lax.fori_loop(0, full, move, 0)
        block = vectors[pl.ds(start + full * GROUP, GROUP), :]
        rows_out[d * GROUP : (d + 1) * GROUP, :] = block.astype(jnp.bfloat16)
        start = start + count
        first = first + full


def regroup_documents(hidden, counts, w_proj):
    rows, docs = hidden.shape[0], counts.shape[0]
    width = w_proj.shape[1]
    groups = rows // GROUP
    return pl.pallas_call(
        docs_kernel,
        out_shape=(
            jax.ShapeDtypeStruct((docs * GROUP + rows, width), jnp.bfloat16),
            jax.ShapeDtypeStruct((groups,), jnp.int32),
            jax.ShapeDtypeStruct((groups,), jnp.float32),
        ),
        in_specs=[SMEM, VMEM, VMEM],
        out_specs=(VMEM, SMEM, SMEM),
        scratch_shapes=[pltpu.VMEM((rows + GROUP, width), jnp.float32)],
        compiler_params=params(16),
        name="documents",
    )(counts, hidden, w_proj)


def unit_kernel(*refs):
    *pieces, out = refs
    for i, piece in enumerate(pieces):
        values = piece[...].reshape(PIECE, piece.shape[-1])
        out[i * PIECE : (i + 1) * PIECE, :] = unit_rows(values)


def unit_pieces(*pieces):
    return pl.pallas_call(
        unit_kernel,
        out_shape=jax.ShapeDtypeStruct((len(pieces) * PIECE, pieces[0].shape[-1]), jnp.bfloat16),
        in_specs=[VMEM] * len(pieces),
        out_specs=VMEM,
        compiler_params=params(8),
        name="unit_pieces",
    )(*pieces)


def mass_kernel(places, counts, slot, keep, rows, *refs):
    *chunks, mass, open_sums, tail_sums = refs
    chunks = chunks[-len(places) :]
    docs = counts.shape[0]
    groups = slot.shape[0]
    tail = docs * GROUP

    def weights(block, tokens):
        sims = lax.dot_general(
            block, tokens, (((1,), (1,)), ((), ())), preferred_element_type=jnp.float32
        )
        return jnp.exp2(sims * (BETA * LOG2E))

    for chunk, place in zip(chunks, places):
        tokens = chunk[...]
        wide = tokens.shape[0]
        open_sums[...] = jnp.zeros_like(open_sums)
        block = weights(rows[:tail, :], tokens)
        place8 = lax.broadcasted_iota(jnp.int32, (GROUP // 2, wide), 0)
        for d in range(docs):
            left = counts[d] % GROUP
            lo = d * GROUP
            mid, hi = lo + GROUP // 2, lo + GROUP
            tail_sums[d] = jnp.where(place8 < left, block[lo:mid], 0.0) + jnp.where(
                place8 + GROUP // 2 < left, block[mid:hi], 0.0
            )
        total = jnp.zeros((GROUP // 2, wide), jnp.float32)
        step = 32 if groups % 32 == 0 else 24 if groups % 24 == 0 else groups
        for base in range(0, groups, step):
            block = weights(rows[tail + base * GROUP : tail + (base + step) * GROUP, :], tokens)
            for j in range(step):
                lo = j * GROUP
                mid, hi = lo + GROUP // 2, lo + GROUP
                total = total * keep[base + j] + (block[lo:mid] + block[mid:hi])
                open_sums[slot[base + j]] = total
        sums = jnp.sum(open_sums[:docs] + tail_sums[...], axis=1)
        for i, at in enumerate(place):
            mass[at] = sums[:, i * PIECE : (i + 1) * PIECE]


def add_masses(counts, slot, keep, rows, mass, chunks, places, pieces):
    docs = counts.shape[0]
    wide = chunks[0].shape[0]
    half = GROUP // 2
    before = () if mass is None else (mass,)
    return pl.pallas_call(
        functools.partial(mass_kernel, places),
        out_shape=jax.ShapeDtypeStruct((pieces, docs, PIECE), jnp.float32),
        in_specs=[SMEM, SMEM, SMEM] + [VMEM] * (1 + len(before) + len(chunks)),
        out_specs=VMEM,
        input_output_aliases={4: 0} if before else {},
        scratch_shapes=[
            pltpu.VMEM((docs + 1, half, wide), jnp.float32),
            pltpu.VMEM((docs, half, wide), jnp.float32),
        ],
        compiler_params=params(24),
        name="masses",
    )(counts, slot, keep, rows, *before, *chunks)


def score_kernel(parts, tokens, own, counts, mass, scores):
    pieces, docs, _ = mass.shape
    groups = pieces // parts
    queries = PIECE // tokens
    per_tile = 128 // queries
    lengths = jnp.concatenate(
        [jnp.full((1, PIECE), counts[d].astype(jnp.float32)) for d in range(docs)], axis=0
    )
    logs = []
    for group in range(groups):
        relative = group ^ own[0]
        total = jnp.log(mass[relative * parts] / lengths)
        for part in range(1, parts):
            total = total + jnp.log(mass[relative * parts + part] / lengths)
        logs.append(total)
    place = lax.broadcasted_iota(jnp.int32, (PIECE, 128), 0) // tokens
    column = lax.broadcasted_iota(jnp.int32, (PIECE, 128), 1)
    tiles = groups // per_tile
    total = jnp.zeros((tiles * docs, 128), jnp.float32)
    for i in range(per_tile):
        pick = (column == place + i * queries).astype(jnp.bfloat16)
        rest = jnp.concatenate([logs[tile * per_tile + i] for tile in range(tiles)], axis=0)
        for _ in range(3):
            head = rest.astype(jnp.bfloat16)
            total = total + jnp.dot(head, pick, preferred_element_type=jnp.float32)
            rest = rest - head.astype(jnp.float32)
    total = total * (1.0 / (tokens * parts))
    for tile in range(tiles):
        scores[:, tile * 128 : (tile + 1) * 128] = total[tile * docs : (tile + 1) * docs]


def score(parts, tokens, own, counts, mass):
    pieces, docs, _ = mass.shape
    queries = pieces // parts * (PIECE // tokens)
    return pl.pallas_call(
        functools.partial(score_kernel, parts, tokens),
        out_shape=jax.ShapeDtypeStruct((docs, queries), jnp.float32),
        in_specs=[SMEM, SMEM, VMEM],
        out_specs=VMEM,
        compiler_params=params(8),
        name="scores",
    )(own, counts, mass)


def swap(values, mask, devices):
    return lax.ppermute(values, ("shard", "loop"), [(i, i ^ mask) for i in range(devices)])


def pair_body(hidden, segment, counts, w_proj, seeds):
    devices = 32
    core, x, z, far, y = 1, 2, 4, 8, 16
    send = functools.partial(swap, devices=devices)
    raw = [seeds, send(seeds, z), send(seeds, far), send(seeds, z | far)]
    rows, slot, keep = regroup_documents(hidden, counts, w_proj)
    own = unit_pieces(*raw)
    a, b = own[: 2 * PIECE], own[2 * PIECE :]
    ax, by = send(a, x), send(b, y)
    ay, bx = send(a, y), send(b, x)
    axy, byx = send(ax, y), send(by, x)
    mass = None
    for va, vb, ma, mb in (
        (a, b, 0, 0),
        (ax, by, x, y),
        (ay, bx, y, x),
        (axy, byx, x | y, x | y),
    ):
        places = (pair_places(ma, 0, z), pair_places(mb, far, z | far))
        mass = add_masses(counts, slot, keep, rows, mass, (va, vb), places, devices)
        places = (pair_places(ma | core, 0, z), pair_places(mb | core, far, z | far))
        chunks = (send(va, core), send(vb, core))
        mass = add_masses(counts, slot, keep, rows, mass, chunks, places, devices)
    mine = lax.axis_index("loop").astype(jnp.int32).reshape(1)
    return score(2, 16, mine, counts, mass)


def pair_places(mask, *along_z):
    return tuple(((mask & 15) ^ bits) * 2 + (mask >> 4) for bits in along_z)


def whole_body(hidden, segment, counts, w_proj, seeds):
    own = lax.all_gather(unit_rows(seeds), "shard", axis=1, tiled=True)
    every = lax.all_gather(own, "loop", axis=0, tiled=True)
    tokens = every.shape[1]
    every = every.reshape(-1, every.shape[-1])
    pieces = every.shape[0] // PIECE
    rows, slot, keep = regroup_documents(hidden, counts, w_proj)
    mass = None
    for first in range(0, pieces, 4):
        chunks = tuple(every[i * PIECE : (i + 2) * PIECE] for i in (first, first + 2))
        places = ((first, first + 1), (first + 2, first + 3))
        mass = add_masses(counts, slot, keep, rows, mass, chunks, places, pieces)
    return score(1, tokens, jnp.zeros((1,), jnp.int32), counts, mass)


def solution(mesh):
    in_specs = (
        P(("shard", "loop"), None),
        P(("shard", "loop")),
        P(("shard", "loop")),
        P(),
        P("loop", "shard", None),
    )
    out_specs = P(("shard", "loop"), None)
    paired = mesh.shape["shard"] == 2 and mesh.shape["loop"] == 16
    body = pair_body if paired else whole_body
    return jax.shard_map(body, mesh=mesh, in_specs=in_specs, out_specs=out_specs, check_vma=False)
```

time: 126 us -> 50.3 us (0.40)
  matrix products: 34 us -> 0 us
  waiting for transfers between devices: 39.2 us -> 11.7 us
  Pallas kernels: 0 us -> 20.1 us
  local copies, waits for them, and re-layouts: 18.9 us -> 4.28 us
  other arithmetic: 14 us -> 0 us
  starting transfers between devices: 0.01 us -> 13.9 us
  between operations: 13.5 us -> 0.16 us
  blocking collectives: 5.97 us -> 0 us
    all_gather x1 -> x0, waiting for transfers between devices: 39.2 us -> none  [body(): piece = lax.all_gather(own_seeds, 'loop', axis=0, tiled=True)]
    dot_general x49 -> x0, matrix products: 34 us -> none  [the longest x16 11.2 us: score_group(): jnp.dot(member, lower, preferred_element_type=jnp.float32)]
    pallas_call x0 -> x11, Pallas kernels: none -> 20.1 us  [the longest x8 14.9 us: add_masses(): pl.pallas_call(functools.partial(mass_kernel, places), out_shape=jax.Shap...]
    dynamic_slice x16 -> x0, local copies, waits for them, and re-layouts: 14.6 us -> none  [body(): lax.map(score_group, piece.reshape(groups_here, group, qtokens, width))]
    ppermute x0 -> x17, starting transfers between devices: none -> 13.9 us  [swap(): lax.ppermute(values, ('shard', 'loop'), [(i, i ^ mask) for i in range(dev...]
    ppermute x0 -> x17, waiting for transfers between devices: none -> 11.7 us  [swap(): lax.ppermute(values, ('shard', 'loop'), [(i, i ^ mask) for i in range(dev...]
    dynamic_update_slice x16 -> x0, other arithmetic: 9.57 us -> none  [body(): lax.map(score_group, piece.reshape(groups_here, group, qtokens, width))]
    all_gather x1 -> x0, blocking collectives: 5.97 us -> none  [body(): own_seeds = lax.all_gather(unit_rows(seeds), 'shard', axis=1, tiled=True)]
  transfers between devices with their start and end apart: 1 -> 17, of which waited for: 1 -> 7; matrix products, arithmetic and copies ran while one was open for 3% -> 0% of each run, Pallas kernels for 0% -> 33%
where the time goes in v1:
time: 50.3 us; the launch traced here: 50.1 us
  Pallas kernels  20.1 us (40%)
  starting transfers between devices  13.9 us (28%)
  waiting for transfers between devices  11.7 us (23%)
  local copies, waits for them, and re-layouts  4.28 us (9%)
    pallas_call x8, Pallas kernels, add_masses(): pl.pallas_call(functools.partial(mass_kernel, places), out_shape=jax.Shap...  14.9 us
    ppermute x17, starting transfers between devices, swap(): lax.ppermute(values, ('shard', 'loop'), [(i, i ^ mask) for i in range(dev...  13.9 us
    ppermute x17, waiting for transfers between devices, swap(): lax.ppermute(values, ('shard', 'loop'), [(i, i ^ mask) for i in range(dev...  11.7 us
    unnamed x10, local copies, waits for them, and re-layouts  4.26 us
    pallas_call x1, Pallas kernels, regroup_documents(): pl.pallas_call(docs_kernel, out_shape=(jax.ShapeDtypeStruct((docs * GROUP...  3.49 us
    pallas_call x1, Pallas kernels, score(): pl.pallas_call(functools.partial(score_kernel, parts, tokens), out_shape=...  1.49 us
  transfers between devices with their start and end apart: 17, of which 7 were waited for; matrix products, arithmetic and copies ran while one was open for 0% of the time, Pallas kernels for 33%

profile of v1, /device:TPU:0, one launch (start us, length us, event | category | flops | bytes accessed | tf_op | source)
XLA Modules:
  0.0 50.1 jit_solution(11077648919106679)
XLA Ops:
  0.0 3.0 %collective-permute-start = (bf16[16,16,128]{2,1,0:T(8,128)(2,1)}, bf16[16,16,128]{2,1,0:T(8,128)(2,1)S(1)}, u32[]{:S(2)}, u32[]{:S(2)}) collective-permute-start(bf16[16,16,128]{2,1,0:T(8,128)(2,1)} %refs_0_.1), channel_id=1, source_target_pairs={{0,4},{1,5},{2,6},{3,7},{4,0},{5,1},{6,2},{7,3},{8,12},{9,13},{10,... | collective-permute-start | bytes 196616 | tf_op jit(solution)/shard_map/ppermute | solution.py:215
  3.0 2.6 %collective-permute-start.1 = (bf16[16,16,128]{2,1,0:T(8,128)(2,1)}, bf16[16,16,128]{2,1,0:T(8,128)(2,1)S(1)}, u32[]{:S(2)}, u32[]{:S(2)}) collective-permute-start(bf16[16,16,128]{2,1,0:T(8,128)(2,1)} %refs_0_.1), channel_id=1, source_target_pairs={{0,8},{1,9},{2,10},{3,11},{4,12},{5,13},{6,14},{7,15},{8,0},{9,1},... | collective-permute-start | bytes 196616 | tf_op jit(solution)/shard_map/ppermute | solution.py:215
  5.6 4.9 %collective-permute-done.1.refs_2_ = bf16[16,16,128]{2,1,0:T(8,128)(2,1)S(1)} collective-permute-done((bf16[16,16,128]{2,1,0:T(8,128)(2,1)}, bf16[16,16,128]{2,1,0:T(8,128)(2,1)S(1)}, u32[]{:S(2)}, u32[]{:S(2)}) %collective-permute-start.1) | collective-permute-done | bytes 65568 | tf_op jit(solution)/shard_map/ppermute | solution.py:215
  10.5 1.4 %collective-permute-done.2.refs_3_ = bf16[16,16,128]{2,1,0:T(8,128)(2,1)S(1)} collective-permute-done((bf16[16,16,128]{2,1,0:T(8,128)(2,1)}, bf16[16,16,128]{2,1,0:T(8,128)(2,1)S(1)}, u32[]{:S(2)}, u32[]{:S(2)}) %collective-permute-start.2) | collective-permute-done | bytes 65568 | tf_op jit(solution)/shard_map/ppermute | solution.py:215
  11.9 0.8 %copy-done.2 = bf16[16,16,128]{2,1,0:T(8,128)(2,1)S(1)} copy-done((bf16[16,16,128]{2,1,0:T(8,128)(2,1)S(1)}, bf16[16,16,128]{2,1,0:T(8,128)(2,1)}, u32[]{:S(2)}) %copy-start.2) | copy-done | bytes 65560
  12.8 0.2 unit_pieces.1
  13.1 1.6 %collective-permute-start.5 = (bf16[512,128]{1,0:T(8,128)(2,1)S(1)}, bf16[512,128]{1,0:T(8,128)(2,1)S(1)}, u32[]{:S(2)}, u32[]{:S(2)}) collective-permute-start(bf16[512,128]{1,0:T(8,128)(2,1)S(1)} %get-tuple-element.12.refs_0_), channel_id=1, source_target_pairs={{0,2},{1,3},{2,0},{3,1},{4,6},{5,7},{6,4},{7,5},{8,10},{9,11},{10,... | collective-permute-start | bytes 393224 | tf_op jit(solution)/shard_map/ppermute | solution.py:215
  14.6 0.2 collective-permute-start.4
  14.8 1.5 %collective-permute-start.6 = (bf16[512,128]{1,0:T(8,128)(2,1)S(1)}, bf16[512,128]{1,0:T(8,128)(2,1)S(1)}, u32[]{:S(2)}, u32[]{:S(2)}) collective-permute-start(bf16[512,128]{1,0:T(8,128)(2,1)S(1)} %get-tuple-element.11.refs_1_), channel_id=1, source_target_pairs={{0,16},{1,17},{2,18},{3,19},{4,20},{5,21},{6,22},{7,23},{8,24},{9,... | collective-permute-start | bytes 393224 | tf_op jit(solution)/shard_map/ppermute | solution.py:215
  16.3 0.5 %collective-permute-start.10 = (bf16[512,128]{1,0:T(8,128)(2,1)S(1)}, bf16[512,128]{1,0:T(8,128)(2,1)S(1)}, u32[]{:S(2)}, u32[]{:S(2)}) collective-permute-start(bf16[512,128]{1,0:T(8,128)(2,1)S(1)} %get-tuple-element.11.refs_1_), channel_id=1, source_target_pairs={{0,2},{1,3},{2,0},{3,1},{4,6},{5,7},{6,4},{7,5},{8,10},{9,11},{10,... | collective-permute-start | bytes 393224 | tf_op jit(solution)/shard_map/ppermute | solution.py:215
  16.9 0.5 %collective-permute-start.9 = (bf16[512,128]{1,0:T(8,128)(2,1)S(1)}, bf16[512,128]{1,0:T(8,128)(2,1)S(1)}, u32[]{:S(2)}, u32[]{:S(2)}) collective-permute-start(bf16[512,128]{1,0:T(8,128)(2,1)S(1)} %get-tuple-element.12.refs_0_), channel_id=1, source_target_pairs={{0,16},{1,17},{2,18},{3,19},{4,20},{5,21},{6,22},{7,23},{8,24},{9,... | collective-permute-start | bytes 393224 | tf_op jit(solution)/shard_map/ppermute | solution.py:215
  17.4 1.6 %collective-permute-done.5.refs_1_ = bf16[512,128]{1,0:T(8,128)(2,1)S(1)} collective-permute-done((bf16[512,128]{1,0:T(8,128)(2,1)S(1)}, bf16[512,128]{1,0:T(8,128)(2,1)S(1)}, u32[]{:S(2)}, u32[]{:S(2)}) %collective-permute-start.5) | collective-permute-done | bytes 131104 | tf_op jit(solution)/shard_map/ppermute | solution.py:215
  19.0 2.0 %collective-permute-start.13 = (bf16[512,128]{1,0:T(8,128)(2,1)S(1)}, bf16[512,128]{1,0:T(8,128)(2,1)S(1)}, u32[]{:S(2)}, u32[]{:S(2)}) collective-permute-start(bf16[512,128]{1,0:T(8,128)(2,1)S(1)} %collective-permute-done.5.refs_1_), channel_id=1, source_target_pairs={{0,16},{1,17},{2,18},{3,19},{4,20},{5,21},{6,22},{7,23},{8,24},{9,... | collective-permute-start | bytes 393224 | tf_op jit(solution)/shard_map/ppermute | solution.py:215
  21.0 0.1 collective-permute-done.6.refs_2_
  21.1 1.3 %collective-permute-start.14 = (bf16[512,128]{1,0:T(8,128)(2,1)S(1)}, bf16[512,128]{1,0:T(8,128)(2,1)S(1)}, u32[]{:S(2)}, u32[]{:S(2)}) collective-permute-start(bf16[512,128]{1,0:T(8,128)(2,1)S(1)} %collective-permute-done.6.refs_2_), channel_id=1, source_target_pairs={{0,2},{1,3},{2,0},{3,1},{4,6},{5,7},{6,4},{7,5},{8,10},{9,11},{10,... | collective-permute-start | bytes 393224 | tf_op jit(solution)/shard_map/ppermute | solution.py:215
  22.5 1.5 %collective-permute-done.9.refs_1_ = bf16[512,128]{1,0:T(8,128)(2,1)S(1)} collective-permute-done((bf16[512,128]{1,0:T(8,128)(2,1)S(1)}, bf16[512,128]{1,0:T(8,128)(2,1)S(1)}, u32[]{:S(2)}, u32[]{:S(2)}) %collective-permute-start.9) | collective-permute-done | bytes 131104 | tf_op jit(solution)/shard_map/ppermute | solution.py:215
  23.9 0.5 %collective-permute-start.12 = (bf16[512,128]{1,0:T(8,128)(2,1)S(1)}, bf16[512,128]{1,0:T(8,128)(2,1)S(1)}, u32[]{:S(2)}, u32[]{:S(2)}) collective-permute-start(bf16[512,128]{1,0:T(8,128)(2,1)S(1)} %collective-permute-done.10.refs_2_), channel_id=1, source_target_pairs={{0,1},{1,0},{2,3},{3,2},{4,5},{5,4},{6,7},{7,6},{8,9},{9,8},{10,11... | collective-permute-start | bytes 393224 | tf_op jit(solution)/shard_map/ppermute | solution.py:215
  24.5 1.7 %collective-permute-done.13.refs_1_ = bf16[512,128]{1,0:T(8,128)(2,1)S(1)} collective-permute-done((bf16[512,128]{1,0:T(8,128)(2,1)S(1)}, bf16[512,128]{1,0:T(8,128)(2,1)S(1)}, u32[]{:S(2)}, u32[]{:S(2)}) %collective-permute-start.13) | collective-permute-done | bytes 131104 | tf_op jit(solution)/shard_map/ppermute | solution.py:215
  26.2 0.4 collective-permute-done.14.refs_2_
  26.7 1.8 %copy-done = bf16[1920,768]{1,0:T(8,128)(2,1)S(1)} copy-done((bf16[1920,768]{1,0:T(8,128)(2,1)S(1)}, bf16[1920,768]{1,0:T(8,128)(2,1)}, u32[]{:S(2)}) %copy-start) | copy-done | bytes 2949144
  28.5 0.9 %copy-done.1 = bf16[768,128]{1,0:T(8,128)(2,1)S(1)} copy-done((bf16[768,128]{1,0:T(8,128)(2,1)S(1)}, bf16[768,128]{1,0:T(8,128)(2,1)}, u32[]{:S(2)}) %copy-start.1) | copy-done | bytes 196632
  29.5 0.7 %copy-done.3 = s32[8]{0:T(128)S(1)} copy-done((s32[8]{0:T(128)S(1)}, s32[8]{0:T(128)}, u32[]{:S(2)}) %copy-start.3) | copy-done | bytes 56
  30.1 3.5 %documents.1 = (bf16[2048,128]{1,0:T(8,128)(2,1)S(1)}, s32[120]{0:T(128)S(1)}, f32[120]{0:T(128)S(1)}) custom-call(s32[8]{0:T(128)S(1)} %copy-done.3, bf16[1920,768]{1,0:T(8,128)(2,1)S(1)} %copy-done, bf16[768,128]{1,0:T(8,128)(2,1)S(1)} %copy-done.1), custom_call_target="tpu_custom_call" | custom-call | tf_op jit(solution)/shard_map/documents/pallas_call | solution.py:77
  33.6 1.9 %masses.8.refs_0_ = f32[32,8,256]{2,1,0:T(8,128)S(1)} custom-call(s32[8]{0:T(128)S(1)} %copy-done.4, s32[120]{0:T(128)S(1)} %get-tuple-element.8.slot, f32[120]{0:T(128)S(1)} %get-tuple-element.9.keep, bf16[2048,128]{1,0:T(8,128)(2,1)S(1)} %get-tuple-element.10.rows, bf16[512,128]{1,0:T(8,128)(2,1)S(1)} %get-tuple-element.12.refs_0_, ...), custom_call_target="tpu_custom_call" | custom-call | tf_op jit(solution)/shard_map/masses/pallas_call | solution.py:155
  35.5 1.9 %masses.9.refs_0_ = f32[32,8,256]{2,1,0:T(8,128)S(1)} custom-call(s32[8]{0:T(128)S(1)} %copy-done.4, s32[120]{0:T(128)S(1)} %get-tuple-element.8.slot, f32[120]{0:T(128)S(1)} %get-tuple-element.9.keep, bf16[2048,128]{1,0:T(8,128)(2,1)S(1)} %get-tuple-element.10.rows, f32[32,8,256]{2,1,0:T(8,128)S(1)} %masses.8.refs_0_, ...), custom_call_target="tpu_custom_call", output_to_operand_aliasing={{}: (4, {})} | custom-call | tf_op jit(solution)/shard_map/masses/pallas_call | solution.py:155
  37.4 1.9 %masses.10.refs_0_ = f32[32,8,256]{2,1,0:T(8,128)S(1)} custom-call(s32[8]{0:T(128)S(1)} %copy-done.4, s32[120]{0:T(128)S(1)} %get-tuple-element.8.slot, f32[120]{0:T(128)S(1)} %get-tuple-element.9.keep, bf16[2048,128]{1,0:T(8,128)(2,1)S(1)} %get-tuple-element.10.rows, f32[32,8,256]{2,1,0:T(8,128)S(1)} %masses.9.refs_0_, ...), custom_call_target="tpu_custom_call", output_to_operand_aliasing={{}: (4, {})} | custom-call | tf_op jit(solution)/shard_map/masses/pallas_call | solution.py:155
  39.2 1.9 %masses.11.refs_0_ = f32[32,8,256]{2,1,0:T(8,128)S(1)} custom-call(s32[8]{0:T(128)S(1)} %copy-done.4, s32[120]{0:T(128)S(1)} %get-tuple-element.8.slot, f32[120]{0:T(128)S(1)} %get-tuple-element.9.keep, bf16[2048,128]{1,0:T(8,128)(2,1)S(1)} %get-tuple-element.10.rows, f32[32,8,256]{2,1,0:T(8,128)S(1)} %masses.10.refs_0_, ...), custom_call_target="tpu_custom_call", output_to_operand_aliasing={{}: (4, {})} | custom-call | tf_op jit(solution)/shard_map/masses/pallas_call | solution.py:155
  41.1 1.9 %masses.12.refs_0_ = f32[32,8,256]{2,1,0:T(8,128)S(1)} custom-call(s32[8]{0:T(128)S(1)} %copy-done.4, s32[120]{0:T(128)S(1)} %get-tuple-element.8.slot, f32[120]{0:T(128)S(1)} %get-tuple-element.9.keep, bf16[2048,128]{1,0:T(8,128)(2,1)S(1)} %get-tuple-element.10.rows, f32[32,8,256]{2,1,0:T(8,128)S(1)} %masses.11.refs_0_, ...), custom_call_target="tpu_custom_call", output_to_operand_aliasing={{}: (4, {})} | custom-call | tf_op jit(solution)/shard_map/masses/pallas_call | solution.py:155
  43.0 1.9 %masses.13.refs_0_ = f32[32,8,256]{2,1,0:T(8,128)S(1)} custom-call(s32[8]{0:T(128)S(1)} %copy-done.4, s32[120]{0:T(128)S(1)} %get-tuple-element.8.slot, f32[120]{0:T(128)S(1)} %get-tuple-element.9.keep, bf16[2048,128]{1,0:T(8,128)(2,1)S(1)} %get-tuple-element.10.rows, f32[32,8,256]{2,1,0:T(8,128)S(1)} %masses.12.refs_0_, ...), custom_call_target="tpu_custom_call", output_to_operand_aliasing={{}: (4, {})} | custom-call | tf_op jit(solution)/shard_map/masses/pallas_call | solution.py:155
  44.9 1.9 %masses.14.refs_0_ = f32[32,8,256]{2,1,0:T(8,128)S(1)} custom-call(s32[8]{0:T(128)S(1)} %copy-done.4, s32[120]{0:T(128)S(1)} %get-tuple-element.8.slot, f32[120]{0:T(128)S(1)} %get-tuple-element.9.keep, bf16[2048,128]{1,0:T(8,128)(2,1)S(1)} %get-tuple-element.10.rows, f32[32,8,256]{2,1,0:T(8,128)S(1)} %masses.13.refs_0_, ...), custom_call_target="tpu_custom_call", output_to_operand_aliasing={{}: (4, {})} | custom-call | tf_op jit(solution)/shard_map/masses/pallas_call | solution.py:155
  46.7 1.9 %masses.15.mass = f32[32,8,256]{2,1,0:T(8,128)S(1)} custom-call(s32[8]{0:T(128)S(1)} %copy-done.4, s32[120]{0:T(128)S(1)} %get-tuple-element.8.slot, f32[120]{0:T(128)S(1)} %get-tuple-element.9.keep, bf16[2048,128]{1,0:T(8,128)(2,1)S(1)} %get-tuple-element.10.rows, f32[32,8,256]{2,1,0:T(8,128)S(1)} %masses.14.refs_0_, ...), custom_call_target="tpu_custom_call", output_to_operand_aliasing={{}: (4, {})} | custom-call | tf_op jit(solution)/shard_map/masses/pallas_call | solution.py:155
  48.6 1.5 %scores.1 = f32[8,256]{1,0:T(8,128)} custom-call(s32[1]{0:T(128)} %bitcast.own, s32[8]{0:T(128)S(1)} %copy-done.4, f32[32,8,256]{2,1,0:T(8,128)S(1)} %masses.15.mass), custom_call_target="tpu_custom_call" | custom-call | tf_op jit(solution)/shard_map/scores/pallas_call | solution.py:204
  (24 shorter events, 0.2 us)
Async XLA Ops:
  0.0 5.6 %collective-permute-start = (bf16[16,16,128]{2,1,0:T(8,128)(2,1)}, bf16[16,16,128]{2,1,0:T(8,128)(2,1)S(1)}, u32[]{:S(2)}, u32[]{:S(2)}) collective-permute-start(bf16[16,16,128]{2,1,0:T(8,128)(2,1)} %refs_0_.1), channel_id=1, source_target_pairs={{0,4},{1,5},{2,6},{3,7},{4,0},{5,1},{6,2},{7,3},{8,12},{9,13},{10,... | collective-permute-start | bytes 196616 | tf_op jit(solution)/shard_map/ppermute | solution.py:215
  3.0 7.5 %collective-permute-start.1 = (bf16[16,16,128]{2,1,0:T(8,128)(2,1)}, bf16[16,16,128]{2,1,0:T(8,128)(2,1)S(1)}, u32[]{:S(2)}, u32[]{:S(2)}) collective-permute-start(bf16[16,16,128]{2,1,0:T(8,128)(2,1)} %refs_0_.1), channel_id=1, source_target_pairs={{0,8},{1,9},{2,10},{3,11},{4,12},{5,13},{6,14},{7,15},{8,0},{9,1},... | collective-permute-start | bytes 196616 | tf_op jit(solution)/shard_map/ppermute | solution.py:215
  5.6 6.3 %collective-permute-start.2 = (bf16[16,16,128]{2,1,0:T(8,128)(2,1)}, bf16[16,16,128]{2,1,0:T(8,128)(2,1)S(1)}, u32[]{:S(2)}, u32[]{:S(2)}) collective-permute-start(bf16[16,16,128]{2,1,0:T(8,128)(2,1)} %refs_0_.1), channel_id=1, source_target_pairs={{0,12},{1,13},{2,14},{3,15},{4,8},{5,9},{6,10},{7,11},{8,4},{9,5},... | collective-permute-start | bytes 196616 | tf_op jit(solution)/shard_map/ppermute | solution.py:215
  11.9 0.8 %copy-start.2 = (bf16[16,16,128]{2,1,0:T(8,128)(2,1)S(1)}, bf16[16,16,128]{2,1,0:T(8,128)(2,1)}, u32[]{:S(2)}) copy-start(bf16[16,16,128]{2,1,0:T(8,128)(2,1)} %refs_0_.1) | copy-start | bytes 196612
  12.8 20.9 %copy-start.4 = (s32[8]{0:T(128)S(1)}, s32[8]{0:T(128)}, u32[]{:S(2)}) copy-start(s32[8]{0:T(128)} %counts.19) | copy-start | bytes 100
  13.0 3.9 %collective-permute-start.3 = (bf16[512,128]{1,0:T(8,128)(2,1)S(1)}, bf16[512,128]{1,0:T(8,128)(2,1)S(1)}, u32[]{:S(2)}, u32[]{:S(2)}) collective-permute-start(bf16[512,128]{1,0:T(8,128)(2,1)S(1)} %get-tuple-element.12.refs_0_), channel_id=1, source_target_pairs={{0,1},{1,0},{2,3},{3,2},{4,5},{5,4},{6,7},{7,6},{8,9},{9,8},{10,11... | collective-permute-start | bytes 393224 | tf_op jit(solution)/shard_map/ppermute | solution.py:215
  13.1 5.9 %collective-permute-start.5 = (bf16[512,128]{1,0:T(8,128)(2,1)S(1)}, bf16[512,128]{1,0:T(8,128)(2,1)S(1)}, u32[]{:S(2)}, u32[]{:S(2)}) collective-permute-start(bf16[512,128]{1,0:T(8,128)(2,1)S(1)} %get-tuple-element.12.refs_0_), channel_id=1, source_target_pairs={{0,2},{1,3},{2,0},{3,1},{4,6},{5,7},{6,4},{7,5},{8,10},{9,11},{10,... | collective-permute-start | bytes 393224 | tf_op jit(solution)/shard_map/ppermute | solution.py:215
  14.6 4.4 %collective-permute-start.4 = (bf16[512,128]{1,0:T(8,128)(2,1)S(1)}, bf16[512,128]{1,0:T(8,128)(2,1)S(1)}, u32[]{:S(2)}, u32[]{:S(2)}) collective-permute-start(bf16[512,128]{1,0:T(8,128)(2,1)S(1)} %get-tuple-element.11.refs_1_), channel_id=1, source_target_pairs={{0,1},{1,0},{2,3},{3,2},{4,5},{5,4},{6,7},{7,6},{8,9},{9,8},{10,11... | collective-permute-start | bytes 393224 | tf_op jit(solution)/shard_map/ppermute | solution.py:215
  14.8 6.3 %collective-permute-start.6 = (bf16[512,128]{1,0:T(8,128)(2,1)S(1)}, bf16[512,128]{1,0:T(8,128)(2,1)S(1)}, u32[]{:S(2)}, u32[]{:S(2)}) collective-permute-start(bf16[512,128]{1,0:T(8,128)(2,1)S(1)} %get-tuple-element.11.refs_1_), channel_id=1, source_target_pairs={{0,16},{1,17},{2,18},{3,19},{4,20},{5,21},{6,22},{7,23},{8,24},{9,... | collective-permute-start | bytes 393224 | tf_op jit(solution)/shard_map/ppermute | solution.py:215
  16.3 6.1 %collective-permute-start.10 = (bf16[512,128]{1,0:T(8,128)(2,1)S(1)}, bf16[512,128]{1,0:T(8,128)(2,1)S(1)}, u32[]{:S(2)}, u32[]{:S(2)}) collective-permute-start(bf16[512,128]{1,0:T(8,128)(2,1)S(1)} %get-tuple-element.11.refs_1_), channel_id=1, source_target_pairs={{0,2},{1,3},{2,0},{3,1},{4,6},{5,7},{6,4},{7,5},{8,10},{9,11},{10,... | collective-permute-start | bytes 393224 | tf_op jit(solution)/shard_map/ppermute | solution.py:215
  16.9 7.1 %collective-permute-start.9 = (bf16[512,128]{1,0:T(8,128)(2,1)S(1)}, bf16[512,128]{1,0:T(8,128)(2,1)S(1)}, u32[]{:S(2)}, u32[]{:S(2)}) collective-permute-start(bf16[512,128]{1,0:T(8,128)(2,1)S(1)} %get-tuple-element.12.refs_0_), channel_id=1, source_target_pairs={{0,16},{1,17},{2,18},{3,19},{4,20},{5,21},{6,22},{7,23},{8,24},{9,... | collective-permute-start | bytes 393224 | tf_op jit(solution)/shard_map/ppermute | solution.py:215
  19.0 4.9 %collective-permute-start.7 = (bf16[512,128]{1,0:T(8,128)(2,1)S(1)}, bf16[512,128]{1,0:T(8,128)(2,1)S(1)}, u32[]{:S(2)}, u32[]{:S(2)}) collective-permute-start(bf16[512,128]{1,0:T(8,128)(2,1)S(1)} %collective-permute-done.5.refs_1_), channel_id=1, source_target_pairs={{0,1},{1,0},{2,3},{3,2},{4,5},{5,4},{6,7},{7,6},{8,9},{9,8},{10,11... | collective-permute-start | bytes 393224 | tf_op jit(solution)/shard_map/ppermute | solution.py:215
  19.0 7.2 %collective-permute-start.13 = (bf16[512,128]{1,0:T(8,128)(2,1)S(1)}, bf16[512,128]{1,0:T(8,128)(2,1)S(1)}, u32[]{:S(2)}, u32[]{:S(2)}) collective-permute-start(bf16[512,128]{1,0:T(8,128)(2,1)S(1)} %collective-permute-done.5.refs_1_), channel_id=1, source_target_pairs={{0,16},{1,17},{2,18},{3,19},{4,20},{5,21},{6,22},{7,23},{8,24},{9,... | collective-permute-start | bytes 393224 | tf_op jit(solution)/shard_map/ppermute | solution.py:215
  21.1 5.5 %collective-permute-start.14 = (bf16[512,128]{1,0:T(8,128)(2,1)S(1)}, bf16[512,128]{1,0:T(8,128)(2,1)S(1)}, u32[]{:S(2)}, u32[]{:S(2)}) collective-permute-start(bf16[512,128]{1,0:T(8,128)(2,1)S(1)} %collective-permute-done.6.refs_2_), channel_id=1, source_target_pairs={{0,2},{1,3},{2,0},{3,1},{4,6},{5,7},{6,4},{7,5},{8,10},{9,11},{10,... | collective-permute-start | bytes 393224 | tf_op jit(solution)/shard_map/ppermute | solution.py:215
  22.5 16.7 %collective-permute-start.8 = (bf16[512,128]{1,0:T(8,128)(2,1)S(1)}, bf16[512,128]{1,0:T(8,128)(2,1)S(1)}, u32[]{:S(2)}, u32[]{:S(2)}) collective-permute-start(bf16[512,128]{1,0:T(8,128)(2,1)S(1)} %collective-permute-done.6.refs_2_), channel_id=1, source_target_pairs={{0,1},{1,0},{2,3},{3,2},{4,5},{5,4},{6,7},{7,6},{8,9},{9,8},{10,11... | collective-permute-start | bytes 393224 | tf_op jit(solution)/shard_map/ppermute | solution.py:215
  23.9 19.0 %collective-permute-start.11 = (bf16[512,128]{1,0:T(8,128)(2,1)S(1)}, bf16[512,128]{1,0:T(8,128)(2,1)S(1)}, u32[]{:S(2)}, u32[]{:S(2)}) collective-permute-start(bf16[512,128]{1,0:T(8,128)(2,1)S(1)} %collective-permute-done.9.refs_1_), channel_id=1, source_target_pairs={{0,1},{1,0},{2,3},{3,2},{4,5},{5,4},{6,7},{7,6},{8,9},{9,8},{10,11... | collective-permute-start | bytes 393224 | tf_op jit(solution)/shard_map/ppermute | solution.py:215
  23.9 19.0 %collective-permute-start.12 = (bf16[512,128]{1,0:T(8,128)(2,1)S(1)}, bf16[512,128]{1,0:T(8,128)(2,1)S(1)}, u32[]{:S(2)}, u32[]{:S(2)}) collective-permute-start(bf16[512,128]{1,0:T(8,128)(2,1)S(1)} %collective-permute-done.10.refs_2_), channel_id=1, source_target_pairs={{0,1},{1,0},{2,3},{3,2},{4,5},{5,4},{6,7},{7,6},{8,9},{9,8},{10,11... | collective-permute-start | bytes 393224 | tf_op jit(solution)/shard_map/ppermute | solution.py:215
  26.2 20.6 %collective-permute-start.15 = (bf16[512,128]{1,0:T(8,128)(2,1)S(1)}, bf16[512,128]{1,0:T(8,128)(2,1)S(1)}, u32[]{:S(2)}, u32[]{:S(2)}) collective-permute-start(bf16[512,128]{1,0:T(8,128)(2,1)S(1)} %collective-permute-done.13.refs_1_), channel_id=1, source_target_pairs={{0,1},{1,0},{2,3},{3,2},{4,5},{5,4},{6,7},{7,6},{8,9},{9,8},{10,11... | collective-permute-start | bytes 393224 | tf_op jit(solution)/shard_map/ppermute | solution.py:215
  26.6 20.1 %collective-permute-start.16 = (bf16[512,128]{1,0:T(8,128)(2,1)S(1)}, bf16[512,128]{1,0:T(8,128)(2,1)S(1)}, u32[]{:S(2)}, u32[]{:S(2)}) collective-permute-start(bf16[512,128]{1,0:T(8,128)(2,1)S(1)} %collective-permute-done.14.refs_2_), channel_id=1, source_target_pairs={{0,1},{1,0},{2,3},{3,2},{4,5},{5,4},{6,7},{7,6},{8,9},{9,8},{10,11... | collective-permute-start | bytes 393224 | tf_op jit(solution)/shard_map/ppermute | solution.py:215
  26.7 1.8 %copy-start = (bf16[1920,768]{1,0:T(8,128)(2,1)S(1)}, bf16[1920,768]{1,0:T(8,128)(2,1)}, u32[]{:S(2)}) copy-start(bf16[1920,768]{1,0:T(8,128)(2,1)} %hidden.1) | copy-start | bytes 8847364
  28.5 0.9 %copy-start.1 = (bf16[768,128]{1,0:T(8,128)(2,1)S(1)}, bf16[768,128]{1,0:T(8,128)(2,1)}, u32[]{:S(2)}) copy-start(bf16[768,128]{1,0:T(8,128)(2,1)} %w_proj.1) | copy-start | bytes 589828
  29.5 0.7 %copy-start.3 = (s32[8]{0:T(128)S(1)}, s32[8]{0:T(128)}, u32[]{:S(2)}) copy-start(s32[8]{0:T(128)} %counts.19) | copy-start | bytes 100

commit v2 on v1

v2 whole, which is shorter than its diff:
```python
import functools

import jax
import jax.numpy as jnp
from jax import lax
from jax.experimental import pallas as pl
from jax.experimental.pallas import tpu as pltpu
from jax.sharding import PartitionSpec as P

BETA = 16.0
EPS = 1e-06
LOG2E = 1.4426950408889634
GROUP = 16
HALF = GROUP // 2
PIECE = 256
LANES = 128
ANY = pl.BlockSpec(memory_space=pl.ANY)
VMEM = pl.BlockSpec(memory_space=pltpu.VMEM)


def unit_rows(values):
    values = values.astype(jnp.float32)
    return (values * lax.rsqrt(jnp.sum(values * values, axis=-1, keepdims=True) + EPS)).astype(
        jnp.bfloat16
    )


def params(mib):
    return pltpu.CompilerParams(vmem_limit_bytes=mib * 2**20)


def cost(micros):
    return pl.CostEstimate(flops=int(micros * 1e9), bytes_accessed=0, transcendentals=0)


def docs_kernel(counts_hbm, hidden, w_proj, rows_out, inside, keep, last, lengths, vectors, counts, sem):
    docs = last.shape[0]
    rows = hidden.shape[0]
    groups = rows // GROUP
    tail = docs * GROUP
    fetch = pltpu.make_async_copy(counts_hbm, counts, sem)
    fetch.start()
    step = 384 if rows % 384 == 0 else rows
    for lo in range(0, rows, step):
        projected = jnp.dot(
            hidden[lo : lo + step, :], w_proj[...], preferred_element_type=jnp.float32
        )
        vectors[lo : lo + step, :] = unit_rows(projected).astype(jnp.float32)
    vectors[rows:, :] = jnp.zeros_like(vectors[rows:, :])
    rows_out[tail:, :] = jnp.zeros_like(rows_out[tail:, :])
    fetch.wait()
    group = lax.broadcasted_iota(jnp.int32, keep.shape, 0)
    document = lax.broadcasted_iota(jnp.int32, last.shape, 0)
    place = lax.broadcasted_iota(jnp.int32, (GROUP, LANES), 0)
    keeps = jnp.ones(keep.shape, jnp.float32)
    lasts = jnp.zeros(last.shape, jnp.int32)
    sizes = jnp.zeros(last.shape, jnp.float32)
    start = jnp.int32(0)
    first = jnp.int32(0)
    for d in range(docs):
        count = counts[d]
        full = count // GROUP

        def move(k, carry, start=start, first=first):
            block = vectors[pl.ds(start + k * GROUP, GROUP), :]
            at = pl.multiple_of(tail + (first + k) * GROUP, GROUP)
            rows_out[pl.ds(at, GROUP), :] = block.astype(jnp.bfloat16)
            return carry

        lax.fori_loop(0, full, move, 0)
        block = vectors[pl.ds(start + full * GROUP, GROUP), :]
        rows_out[d * GROUP : (d + 1) * GROUP, :] = block.astype(jnp.bfloat16)
        inside[d * GROUP : (d + 1) * GROUP, :] = (place < count - full * GROUP).astype(jnp.float32)
        keeps = jnp.where(group == jnp.where(full > 0, first, groups), 0.0, keeps)
        lasts = jnp.where(document == d, jnp.where(full > 0, first + full - 1, groups), lasts)
        sizes = jnp.where(document == d, count.astype(jnp.float32), sizes)
        start = start + count
        first = first + full
    keep[...] = keeps
    last[...] = lasts
    lengths[...] = sizes


def regroup_documents(hidden, counts, w_proj):
    rows, docs = hidden.shape[0], counts.shape[0]
    width = w_proj.shape[1]
    groups = rows // GROUP
    return pl.pallas_call(
        docs_kernel,
        out_shape=(
            jax.ShapeDtypeStruct((docs * GROUP + rows, width), jnp.bfloat16),
            jax.ShapeDtypeStruct((docs * GROUP, LANES), jnp.float32),
            jax.ShapeDtypeStruct((groups, LANES), jnp.float32),
            jax.ShapeDtypeStruct((docs, LANES), jnp.int32),
            jax.ShapeDtypeStruct((docs, LANES), jnp.float32),
        ),
        in_specs=[ANY, VMEM, VMEM],
        out_specs=(VMEM,) * 5,
        scratch_shapes=[
            pltpu.VMEM((rows + GROUP, width), jnp.float32),
            pltpu.SMEM((docs,), jnp.int32),
            pltpu.SemaphoreType.DMA,
        ],
        compiler_params=params(16),
        cost_estimate=cost(3),
        name="documents",
    )(counts, hidden, w_proj)


def unit_kernel(*refs):
    *pieces, out = refs
    for i, piece in enumerate(pieces):
        values = piece[...].reshape(PIECE, piece.shape[-1])
        out[i * PIECE : (i + 1) * PIECE, :] = unit_rows(values)


def unit_pieces(*pieces):
    return pl.pallas_call(
        unit_kernel,
        out_shape=jax.ShapeDtypeStruct((len(pieces) * PIECE, pieces[0].shape[-1]), jnp.bfloat16),
        in_specs=[VMEM] * len(pieces),
        out_specs=VMEM,
        compiler_params=params(8),
        cost_estimate=cost(0.2),
        name="unit_pieces",
    )(*pieces)


def mass_kernel(places, rows, inside, keep, last, *refs):
    *chunks, mass, sums, tail_sums = refs
    chunks = chunks[-len(places) :]
    docs = last.shape[0]
    groups = keep.shape[0]
    tail = docs * GROUP

    def weights(block, tokens):
        sims = lax.dot_general(
            block, tokens, (((1,), (1,)), ((), ())), preferred_element_type=jnp.float32
        )
        return jnp.exp2(sims * (BETA * LOG2E))

    def wide(row, width):
        return jnp.concatenate([row] * (width // LANES), axis=1)

    step = 24 if groups % 24 == 0 else groups
    ends = last[...]
    for c, (chunk, place) in enumerate(zip(chunks, places)):
        tokens = chunk[...]
        width = tokens.shape[0]
        block = weights(rows[:tail, :], tokens)
        for d in range(docs):
            lo = d * GROUP
            mid, hi = lo + HALF, lo + GROUP
            tail_sums[c, d] = block[lo:mid] * wide(inside[lo:mid, :], width) + block[
                mid:hi
            ] * wide(inside[mid:hi, :], width)
        total = jnp.zeros((HALF, width), jnp.float32)
        sums[c, groups] = total
        for base in range(0, groups, step):
            block = weights(rows[tail + base * GROUP : tail + (base + step) * GROUP, :], tokens)
            for j in range(step):
                lo = j * GROUP
                mid, hi = lo + HALF, lo + GROUP
                row = jnp.broadcast_to(keep[base + j : base + j + 1, :], (HALF, LANES))
                total = total * wide(row, width) + (block[lo:mid] + block[mid:hi])
                sums[c, base + j] = total
    for c, (chunk, place) in enumerate(zip(chunks, places)):
        for d in range(docs):
            total = jnp.sum(sums[c, ends[d, 0]] + tail_sums[c, d], axis=0, keepdims=True)
            for i, at in enumerate(place):
                mass[at, d : d + 1, :] = total[:, i * PIECE : (i + 1) * PIECE]


def add_masses(documents, mass, chunks, places, pieces):
    rows, inside, keep, last, _ = documents
    docs, groups = last.shape[0], keep.shape[0]
    count, width = len(chunks), chunks[0].shape[0]
    before = () if mass is None else (mass,)
    return pl.pallas_call(
        functools.partial(mass_kernel, places),
        out_shape=jax.ShapeDtypeStruct((pieces, docs, PIECE), jnp.float32),
        in_specs=[VMEM] * (4 + len(before) + count),
        out_specs=VMEM,
        input_output_aliases={4: 0} if before else {},
        scratch_shapes=[
            pltpu.VMEM((count, groups + 1, HALF, width), jnp.float32),
            pltpu.VMEM((count, docs, HALF, width), jnp.float32),
        ],
        compiler_params=params(28),
        cost_estimate=cost(1.2 * count * width / 1024),
        name="masses",
    )(rows, inside, keep, last, *before, *chunks)


def score_kernel(parts, tokens, relative, lengths, mass, scores):
    pieces, docs, _ = mass.shape
    groups = pieces // parts
    queries = PIECE // tokens
    per_tile = LANES // queries
    tiles = groups // per_tile
    own = lax.axis_index("loop") if relative else 0
    sizes = jnp.concatenate([lengths[...]] * (PIECE // LANES), axis=1)
    place = lax.broadcasted_iota(jnp.int32, (PIECE, LANES), 0) // tokens
    column = lax.broadcasted_iota(jnp.int32, (PIECE, LANES), 1)
    total = jnp.zeros((tiles * docs, LANES), jnp.float32)
    for i in range(per_tile):
        logs = []
        for tile in range(tiles):
            at = ((tile * per_tile + i) ^ own) * parts
            logs.append(sum(jnp.log(mass[at + part] / sizes) for part in range(parts)))
        rest = jnp.concatenate(logs, axis=0)
        pick = (column == place + i * queries).astype(jnp.bfloat16)
        for _ in range(3):
            head = rest.astype(jnp.bfloat16)
            total = total + jnp.dot(head, pick, preferred_element_type=jnp.float32)
            rest = rest - head.astype(jnp.float32)
    total = total * (1.0 / (tokens * parts))
    for tile in range(tiles):
        scores[:, tile * LANES : (tile + 1) * LANES] = total[tile * docs : (tile + 1) * docs]


def score(parts, tokens, relative, lengths, mass):
    pieces, docs, _ = mass.shape
    queries = pieces // parts * (PIECE // tokens)
    return pl.pallas_call(
        functools.partial(score_kernel, parts, tokens, relative),
        out_shape=jax.ShapeDtypeStruct((docs, queries), jnp.float32),
        in_specs=[VMEM, VMEM],
        out_specs=VMEM,
        compiler_params=params(8),
        cost_estimate=cost(1),
        name="scores",
    )(lengths, mass)


def swap(values, mask, devices):
    return lax.ppermute(values, ("shard", "loop"), [(i, i ^ mask) for i in range(devices)])


def pair_places(mask, *along_z):
    return tuple(((mask & 15) ^ bits) * 2 + (mask >> 4) for bits in along_z)


def pair_body(hidden, segment, counts, w_proj, seeds):
    devices = 32
    core, x, z, far, y = 1, 2, 4, 8, 16
    near, away = (0, z), (far, z | far)
    send = functools.partial(swap, devices=devices)
    raw_far = send(seeds, far)
    raw_z = send(seeds, z)
    documents = regroup_documents(hidden, counts, w_proj)
    a = unit_pieces(seeds, raw_z)
    raw_both = send(raw_far, z)
    ax, ay = send(a, x), send(a, y)
    b = unit_pieces(raw_far, raw_both)
    bx, by = send(b, x), send(b, y)
    axy, byx = send(ax, y), send(by, x)
    mass = None
    for va, vb, ma, mb, za, zb in (
        (a, b, 0, 0, near, away),
        (ax, ay, x, y, near, near),
        (bx, by, x, y, away, away),
        (axy, byx, x | y, x | y, near, away),
    ):
        places = (pair_places(ma, *za), pair_places(mb, *zb))
        mass = add_masses(documents, mass, (va, vb), places, devices)
        other = send(jnp.concatenate([va, vb], axis=0), core)
        places = (pair_places(ma | core, *za) + pair_places(mb | core, *zb),)
        mass = add_masses(documents, mass, (other,), places, devices)
    return score(2, 16, True, documents[-1], mass)


def whole_body(hidden, segment, counts, w_proj, seeds):
    own = lax.all_gather(unit_rows(seeds), "shard", axis=1, tiled=True)
    every = lax.all_gather(own, "loop", axis=0, tiled=True)
    tokens = every.shape[1]
    every = every.reshape(-1, every.shape[-1])
    pieces = every.shape[0] // PIECE
    documents = regroup_documents(hidden, counts, w_proj)
    mass = None
    for first in range(0, pieces, 4):
        places = (tuple(range(first, first + 4)),)
        chunk = every[first * PIECE : (first + 4) * PIECE]
        mass = add_masses(documents, mass, (chunk,), places, pieces)
    return score(1, tokens, False, documents[-1], mass)


def solution(mesh):
    in_specs = (
        P(("shard", "loop"), None),
        P(("shard", "loop")),
        P(("shard", "loop")),
        P(),
        P("loop", "shard", None),
    )
    out_specs = P(("shard", "loop"), None)
    paired = mesh.shape["shard"] == 2 and mesh.shape["loop"] == 16
    body = pair_body if paired else whole_body
    return jax.shard_map(body, mesh=mesh, in_specs=in_specs, out_specs=out_specs, check_vma=False)
```

time: 50.3 us -> 38.3 us (0.76)
  Pallas kernels: 20.1 us -> 13.6 us
  waiting for transfers between devices: 11.7 us -> 6.14 us
  local copies, waits for them, and re-layouts: 4.28 us -> 3.42 us
    ppermute x17 -> x13, waiting for transfers between devices: 11.7 us -> 6.14 us  [swap(): lax.ppermute(values, ('shard', 'loop'), [(i, i ^ mask) for i in range(dev...]
    pallas_call x8, Pallas kernels: 14.9 us -> 10.7 us  [add_masses(): pl.pallas_call(functools.partial(mass_kernel, places), out_shape=jax.Shap...]
    pallas_call x1, Pallas kernels: 3.49 us -> 1.65 us  [regroup_documents(): pl.pallas_call(docs_kernel, out_shape=(jax.ShapeDtypeStruct((docs * GROUP...]
    unnamed x10 -> x8, local copies, waits for them, and re-layouts: 4.26 us -> 3.42 us
    pallas_call x1, Pallas kernels: 1.49 us -> 0.94 us  [score(): pl.pallas_call(functools.partial(score_kernel, parts, tokens, relative),...]
    ppermute x17 -> x13, starting transfers between devices: 13.9 us -> 14.4 us  [swap(): lax.ppermute(values, ('shard', 'loop'), [(i, i ^ mask) for i in range(dev...]
  transfers between devices with their start and end apart: 17 -> 13, of which waited for: 7 -> 4; matrix products, arithmetic and copies ran while one was open for 0% -> 0% of each run, Pallas kernels for 33% -> 30%
where the time goes in v2:
time: 38.3 us; the launch traced here: 37.8 us
  starting transfers between devices  14.4 us (38%)
  Pallas kernels  13.6 us (36%)
  waiting for transfers between devices  6.14 us (16%)
  local copies, waits for them, and re-layouts  3.42 us (9%)
    ppermute x13, starting transfers between devices, swap(): lax.ppermute(values, ('shard', 'loop'), [(i, i ^ mask) for i in range(dev...  14.4 us
    pallas_call x8, Pallas kernels, add_masses(): pl.pallas_call(functools.partial(mass_kernel, places), out_shape=jax.Shap...  10.7 us
    ppermute x13, waiting for transfers between devices, swap(): lax.ppermute(values, ('shard', 'loop'), [(i, i ^ mask) for i in range(dev...  6.14 us
    unnamed x8, local copies, waits for them, and re-layouts  3.42 us
    pallas_call x1, Pallas kernels, regroup_documents(): pl.pallas_call(docs_kernel, out_shape=(jax.ShapeDtypeStruct((docs * GROUP...  1.65 us
    pallas_call x1, Pallas kernels, score(): pl.pallas_call(functools.partial(score_kernel, parts, tokens, relative),...  0.94 us
  transfers between devices with their start and end apart: 13, of which 4 were waited for; matrix products, arithmetic and copies ran while one was open for 0% of the time, Pallas kernels for 30%

profile of v2, /device:TPU:0, one launch (start us, length us, event | category | flops | bytes accessed | tf_op | source)
XLA Modules:
  0.0 37.8 jit_solution(13860072141110054268)
XLA Ops:
  0.0 4.0 %collective-permute-start.1 = (bf16[16,16,128]{2,1,0:T(8,128)(2,1)}, bf16[16,16,128]{2,1,0:T(8,128)(2,1)S(1)}, u32[]{:S(2)}, u32[]{:S(2)}) collective-permute-start(bf16[16,16,128]{2,1,0:T(8,128)(2,1)} %refs_0_.1), channel_id=1, source_target_pairs={{0,8},{1,9},{2,10},{3,11},{4,12},{5,13},{6,14},{7,15},{8,0},{9,1},... | collective-permute-start | bytes 196616 | tf_op jit(solution)/shard_map/ppermute | solution.py:237
  4.0 1.6 %collective-permute-start = (bf16[16,16,128]{2,1,0:T(8,128)(2,1)}, bf16[16,16,128]{2,1,0:T(8,128)(2,1)S(1)}, u32[]{:S(2)}, u32[]{:S(2)}) collective-permute-start(bf16[16,16,128]{2,1,0:T(8,128)(2,1)} %refs_0_.1), channel_id=1, source_target_pairs={{0,4},{1,5},{2,6},{3,7},{4,0},{5,1},{6,2},{7,3},{8,12},{9,13},{10,... | collective-permute-start | bytes 196616 | tf_op jit(solution)/shard_map/ppermute | solution.py:237
  5.6 1.7 %collective-permute-done.1.refs_0_ = bf16[16,16,128]{2,1,0:T(8,128)(2,1)S(1)} collective-permute-done((bf16[16,16,128]{2,1,0:T(8,128)(2,1)}, bf16[16,16,128]{2,1,0:T(8,128)(2,1)S(1)}, u32[]{:S(2)}, u32[]{:S(2)}) %collective-permute-start.1) | collective-permute-done | bytes 65568 | tf_op jit(solution)/shard_map/ppermute | solution.py:237
  7.3 1.4 %collective-permute-start.2 = (bf16[16,16,128]{2,1,0:T(8,128)(2,1)S(1)}, bf16[16,16,128]{2,1,0:T(8,128)(2,1)S(1)}, u32[]{:S(2)}, u32[]{:S(2)}) collective-permute-start(bf16[16,16,128]{2,1,0:T(8,128)(2,1)S(1)} %collective-permute-done.1.refs_0_), channel_id=1, source_target_pairs={{0,4},{1,5},{2,6},{3,7},{4,0},{5,1},{6,2},{7,3},{8,12},{9,13},{10,... | collective-permute-start | bytes 196616 | tf_op jit(solution)/shard_map/ppermute | solution.py:237
  8.7 1.8 %copy-done = bf16[1920,768]{1,0:T(8,128)(2,1)S(1)} copy-done((bf16[1920,768]{1,0:T(8,128)(2,1)S(1)}, bf16[1920,768]{1,0:T(8,128)(2,1)}, u32[]{:S(2)}) %copy-start) | copy-done | bytes 2949144
  10.5 0.9 %copy-done.1 = bf16[768,128]{1,0:T(8,128)(2,1)S(1)} copy-done((bf16[768,128]{1,0:T(8,128)(2,1)S(1)}, bf16[768,128]{1,0:T(8,128)(2,1)}, u32[]{:S(2)}) %copy-start.1) | copy-done | bytes 196632
  11.4 0.7 %copy-done.3 = s32[8]{0:T(128)S(1)} copy-done((s32[8]{0:T(128)S(1)}, s32[8]{0:T(128)}, u32[]{:S(2)}) %copy-start.3) | copy-done | bytes 56
  12.1 1.7 %documents.1 = (bf16[2048,128]{1,0:T(8,128)(2,1)S(1)}, f32[128,128]{1,0:T(8,128)S(1)}, f32[120,128]{1,0:T(8,128)S(1)}, s32[8,128]{1,0:T(8,128)S(1)}, f32[8,128]{1,0:T(8,128)S(1)}) custom-call(s32[8]{0:T(128)S(1)} %copy-done.3, bf16[1920,768]{1,0:T(8,128)(2,1)S(1)} %copy-done, bf16[768,128]{1,0:T(8,128)(2,1)S(1)} %copy-done.1), custom_call_target="tpu_custom_call" | custom-call | flops 3000000000 | tf_op jit(solution)/shard_map/documents/pallas_call | solution.py:88
  13.7 0.0 collective-permute-done.refs_1_
  13.8 0.2 unit_pieces.2.refs_0_
  13.9 1.7 %collective-permute-start.4 = (bf16[512,128]{1,0:T(8,128)(2,1)S(1)}, bf16[512,128]{1,0:T(8,128)(2,1)S(1)}, u32[]{:S(2)}, u32[]{:S(2)}) collective-permute-start(bf16[512,128]{1,0:T(8,128)(2,1)S(1)} %unit_pieces.2.refs_0_), channel_id=1, source_target_pairs={{0,2},{1,3},{2,0},{3,1},{4,6},{5,7},{6,4},{7,5},{8,10},{9,11},{10,... | collective-permute-start | bytes 393224 | tf_op jit(solution)/shard_map/ppermute | solution.py:237
  15.6 1.3 %collective-permute-start.5 = (bf16[512,128]{1,0:T(8,128)(2,1)S(1)}, bf16[512,128]{1,0:T(8,128)(2,1)S(1)}, u32[]{:S(2)}, u32[]{:S(2)}) collective-permute-start(bf16[512,128]{1,0:T(8,128)(2,1)S(1)} %unit_pieces.2.refs_0_), channel_id=1, source_target_pairs={{0,16},{1,17},{2,18},{3,19},{4,20},{5,21},{6,22},{7,23},{8,24},{9,... | collective-permute-start | bytes 393224 | tf_op jit(solution)/shard_map/ppermute | solution.py:237
  16.9 0.1 unit_pieces.3.refs_1_
  17.1 0.8 %collective-permute-start.8 = (bf16[512,128]{1,0:T(8,128)(2,1)S(1)}, bf16[512,128]{1,0:T(8,128)(2,1)S(1)}, u32[]{:S(2)}, u32[]{:S(2)}) collective-permute-start(bf16[512,128]{1,0:T(8,128)(2,1)S(1)} %unit_pieces.3.refs_1_), channel_id=1, source_target_pairs={{0,16},{1,17},{2,18},{3,19},{4,20},{5,21},{6,22},{7,23},{8,24},{9,... | collective-permute-start | bytes 393224 | tf_op jit(solution)/shard_map/ppermute | solution.py:237
  17.9 0.5 %collective-permute-start.7 = (bf16[512,128]{1,0:T(8,128)(2,1)S(1)}, bf16[512,128]{1,0:T(8,128)(2,1)S(1)}, u32[]{:S(2)}, u32[]{:S(2)}) collective-permute-start(bf16[512,128]{1,0:T(8,128)(2,1)S(1)} %unit_pieces.3.refs_1_), channel_id=1, source_target_pairs={{0,2},{1,3},{2,0},{3,1},{4,6},{5,7},{6,4},{7,5},{8,10},{9,11},{10,... | collective-permute-start | bytes 393224 | tf_op jit(solution)/shard_map/ppermute | solution.py:237
  18.4 1.3 %masses.8.refs_0_ = f32[32,8,256]{2,1,0:T(8,128)S(1)} custom-call(bf16[2048,128]{1,0:T(8,128)(2,1)S(1)} %get-tuple-element.11.rows, f32[128,128]{1,0:T(8,128)S(1)} %get-tuple-element.12.inside, f32[120,128]{1,0:T(8,128)S(1)} %get-tuple-element.13.keep, s32[8,128]{1,0:T(8,128)S(1)} %get-tuple-element.14.last, bf16[512,128]{1,0:T(8,128)(2,1)S(1)} %unit_pieces.2.refs_0_, ...), custom_call_target="tpu_custom_call" | custom-call | flops 1200000000 | tf_op jit(solution)/shard_map/masses/pallas_call | solution.py:179
  19.7 1.7 %collective-permute-start.10 = (bf16[512,128]{1,0:T(8,128)(2,1)S(1)}, bf16[512,128]{1,0:T(8,128)(2,1)S(1)}, u32[]{:S(2)}, u32[]{:S(2)}) collective-permute-start(bf16[512,128]{1,0:T(8,128)(2,1)S(1)} %collective-permute-done.4.refs_1_), channel_id=1, source_target_pairs={{0,16},{1,17},{2,18},{3,19},{4,20},{5,21},{6,22},{7,23},{8,24},{9,... | collective-permute-start | bytes 393224 | tf_op jit(solution)/shard_map/ppermute | solution.py:237
  21.4 1.0 %collective-permute-done.8.refs_2_ = bf16[512,128]{1,0:T(8,128)(2,1)S(1)} collective-permute-done((bf16[512,128]{1,0:T(8,128)(2,1)S(1)}, bf16[512,128]{1,0:T(8,128)(2,1)S(1)}, u32[]{:S(2)}, u32[]{:S(2)}) %collective-permute-start.8) | collective-permute-done | bytes 131104 | tf_op jit(solution)/shard_map/ppermute | solution.py:237
  22.4 0.8 %collective-permute-start.11 = (bf16[512,128]{1,0:T(8,128)(2,1)S(1)}, bf16[512,128]{1,0:T(8,128)(2,1)S(1)}, u32[]{:S(2)}, u32[]{:S(2)}) collective-permute-start(bf16[512,128]{1,0:T(8,128)(2,1)S(1)} %collective-permute-done.8.refs_2_), channel_id=1, source_target_pairs={{0,2},{1,3},{2,0},{3,1},{4,6},{5,7},{6,4},{7,5},{8,10},{9,11},{10,... | collective-permute-start | bytes 393224 | tf_op jit(solution)/shard_map/ppermute | solution.py:237
  23.2 0.1 collective-permute-start.6
  23.3 0.5 %collective-permute-start.9 = (bf16[1024,128]{1,0:T(8,128)(2,1)S(1)}, bf16[1024,128]{1,0:T(8,128)(2,1)S(1)}, u32[]{:S(2)}, u32[]{:S(2)}) collective-permute-start(bf16[1024,128]{1,0:T(8,128)(2,1)S(1)} %pad_maximum_fusion.2), channel_id=1, source_target_pairs={{0,1},{1,0},{2,3},{3,2},{4,5},{5,4},{6,7},{7,6},{8,9},{9,8},{10,11... | collective-permute-start | bytes 786440 | tf_op jit(solution)/shard_map/ppermute | solution.py:237
  23.9 1.8 %collective-permute-done.10.refs_1_ = bf16[512,128]{1,0:T(8,128)(2,1)S(1)} collective-permute-done((bf16[512,128]{1,0:T(8,128)(2,1)S(1)}, bf16[512,128]{1,0:T(8,128)(2,1)S(1)}, u32[]{:S(2)}, u32[]{:S(2)}) %collective-permute-start.10) | collective-permute-done | bytes 131104 | tf_op jit(solution)/shard_map/ppermute | solution.py:237
  25.7 1.7 %collective-permute-done.11.refs_2_ = bf16[512,128]{1,0:T(8,128)(2,1)S(1)} collective-permute-done((bf16[512,128]{1,0:T(8,128)(2,1)S(1)}, bf16[512,128]{1,0:T(8,128)(2,1)S(1)}, u32[]{:S(2)}, u32[]{:S(2)}) %collective-permute-start.11) | collective-permute-done | bytes 131104 | tf_op jit(solution)/shard_map/ppermute | solution.py:237
  27.4 0.1 collective-permute-start.12
  27.4 1.3 %masses.9.refs_0_ = f32[32,8,256]{2,1,0:T(8,128)S(1)} custom-call(bf16[2048,128]{1,0:T(8,128)(2,1)S(1)} %get-tuple-element.11.rows, f32[128,128]{1,0:T(8,128)S(1)} %get-tuple-element.12.inside, f32[120,128]{1,0:T(8,128)S(1)} %get-tuple-element.13.keep, s32[8,128]{1,0:T(8,128)S(1)} %get-tuple-element.14.last, ...), custom_call_target="tpu_custom_call", output_to_operand_aliasing={{}: (4, {})} | custom-call | flops 1200000000 | tf_op jit(solution)/shard_map/masses/pallas_call | solution.py:179
  28.8 1.3 %masses.10.refs_0_ = f32[32,8,256]{2,1,0:T(8,128)S(1)} custom-call(bf16[2048,128]{1,0:T(8,128)(2,1)S(1)} %get-tuple-element.11.rows, f32[128,128]{1,0:T(8,128)S(1)} %get-tuple-element.12.inside, f32[120,128]{1,0:T(8,128)S(1)} %get-tuple-element.13.keep, s32[8,128]{1,0:T(8,128)S(1)} %get-tuple-element.14.last, ...), custom_call_target="tpu_custom_call", output_to_operand_aliasing={{}: (4, {})} | custom-call | flops 1200000000 | tf_op jit(solution)/shard_map/masses/pallas_call | solution.py:179
  30.1 1.3 %masses.11.refs_0_ = f32[32,8,256]{2,1,0:T(8,128)S(1)} custom-call(bf16[2048,128]{1,0:T(8,128)(2,1)S(1)} %get-tuple-element.11.rows, f32[128,128]{1,0:T(8,128)S(1)} %get-tuple-element.12.inside, f32[120,128]{1,0:T(8,128)S(1)} %get-tuple-element.13.keep, s32[8,128]{1,0:T(8,128)S(1)} %get-tuple-element.14.last, ...), custom_call_target="tpu_custom_call", output_to_operand_aliasing={{}: (4, {})} | custom-call | flops 1200000000 | tf_op jit(solution)/shard_map/masses/pallas_call | solution.py:179
  31.5 1.3 %masses.12.refs_0_ = f32[32,8,256]{2,1,0:T(8,128)S(1)} custom-call(bf16[2048,128]{1,0:T(8,128)(2,1)S(1)} %get-tuple-element.11.rows, f32[128,128]{1,0:T(8,128)S(1)} %get-tuple-element.12.inside, f32[120,128]{1,0:T(8,128)S(1)} %get-tuple-element.13.keep, s32[8,128]{1,0:T(8,128)S(1)} %get-tuple-element.14.last, ...), custom_call_target="tpu_custom_call", output_to_operand_aliasing={{}: (4, {})} | custom-call | flops 1200000000 | tf_op jit(solution)/shard_map/masses/pallas_call | solution.py:179
  32.8 1.3 %masses.13.refs_0_ = f32[32,8,256]{2,1,0:T(8,128)S(1)} custom-call(bf16[2048,128]{1,0:T(8,128)(2,1)S(1)} %get-tuple-element.11.rows, f32[128,128]{1,0:T(8,128)S(1)} %get-tuple-element.12.inside, f32[120,128]{1,0:T(8,128)S(1)} %get-tuple-element.13.keep, s32[8,128]{1,0:T(8,128)S(1)} %get-tuple-element.14.last, ...), custom_call_target="tpu_custom_call", output_to_operand_aliasing={{}: (4, {})} | custom-call | flops 1200000000 | tf_op jit(solution)/shard_map/masses/pallas_call | solution.py:179
  34.2 1.3 %masses.14.refs_0_ = f32[32,8,256]{2,1,0:T(8,128)S(1)} custom-call(bf16[2048,128]{1,0:T(8,128)(2,1)S(1)} %get-tuple-element.11.rows, f32[128,128]{1,0:T(8,128)S(1)} %get-tuple-element.12.inside, f32[120,128]{1,0:T(8,128)S(1)} %get-tuple-element.13.keep, s32[8,128]{1,0:T(8,128)S(1)} %get-tuple-element.14.last, ...), custom_call_target="tpu_custom_call", output_to_operand_aliasing={{}: (4, {})} | custom-call | flops 1200000000 | tf_op jit(solution)/shard_map/masses/pallas_call | solution.py:179
  35.5 1.3 %masses.15.mass = f32[32,8,256]{2,1,0:T(8,128)S(1)} custom-call(bf16[2048,128]{1,0:T(8,128)(2,1)S(1)} %get-tuple-element.11.rows, f32[128,128]{1,0:T(8,128)S(1)} %get-tuple-element.12.inside, f32[120,128]{1,0:T(8,128)S(1)} %get-tuple-element.13.keep, s32[8,128]{1,0:T(8,128)S(1)} %get-tuple-element.14.last, ...), custom_call_target="tpu_custom_call", output_to_operand_aliasing={{}: (4, {})} | custom-call | flops 1200000000 | tf_op jit(solution)/shard_map/masses/pallas_call | solution.py:179
  36.9 0.9 %scores.1 = f32[8,256]{1,0:T(8,128)} custom-call(f32[8,128]{1,0:T(8,128)S(1)} %get-tuple-element.10.lengths, f32[32,8,256]{2,1,0:T(8,128)S(1)} %masses.15.mass), custom_call_target="tpu_custom_call" | custom-call | flops 1000000000 | tf_op jit(solution)/shard_map/scores/pallas_call | solution.py:225
  (18 shorter events, 0.1 us)
Async XLA Ops:
  0.0 7.3 %collective-permute-start.1 = (bf16[16,16,128]{2,1,0:T(8,128)(2,1)}, bf16[16,16,128]{2,1,0:T(8,128)(2,1)S(1)}, u32[]{:S(2)}, u32[]{:S(2)}) collective-permute-start(bf16[16,16,128]{2,1,0:T(8,128)(2,1)} %refs_0_.1), channel_id=1, source_target_pairs={{0,8},{1,9},{2,10},{3,11},{4,12},{5,13},{6,14},{7,15},{8,0},{9,1},... | collective-permute-start | bytes 196616 | tf_op jit(solution)/shard_map/ppermute | solution.py:237
  4.0 9.7 %collective-permute-start = (bf16[16,16,128]{2,1,0:T(8,128)(2,1)}, bf16[16,16,128]{2,1,0:T(8,128)(2,1)S(1)}, u32[]{:S(2)}, u32[]{:S(2)}) collective-permute-start(bf16[16,16,128]{2,1,0:T(8,128)(2,1)} %refs_0_.1), channel_id=1, source_target_pairs={{0,4},{1,5},{2,6},{3,7},{4,0},{5,1},{6,2},{7,3},{8,12},{9,13},{10,... | collective-permute-start | bytes 196616 | tf_op jit(solution)/shard_map/ppermute | solution.py:237
  7.3 9.6 %collective-permute-start.2 = (bf16[16,16,128]{2,1,0:T(8,128)(2,1)S(1)}, bf16[16,16,128]{2,1,0:T(8,128)(2,1)S(1)}, u32[]{:S(2)}, u32[]{:S(2)}) collective-permute-start(bf16[16,16,128]{2,1,0:T(8,128)(2,1)S(1)} %collective-permute-done.1.refs_0_), channel_id=1, source_target_pairs={{0,4},{1,5},{2,6},{3,7},{4,0},{5,1},{6,2},{7,3},{8,12},{9,13},{10,... | collective-permute-start | bytes 196616 | tf_op jit(solution)/shard_map/ppermute | solution.py:237
  8.7 1.8 %copy-start = (bf16[1920,768]{1,0:T(8,128)(2,1)S(1)}, bf16[1920,768]{1,0:T(8,128)(2,1)}, u32[]{:S(2)}) copy-start(bf16[1920,768]{1,0:T(8,128)(2,1)} %hidden.1) | copy-start | bytes 8847364
  10.5 0.9 %copy-start.1 = (bf16[768,128]{1,0:T(8,128)(2,1)S(1)}, bf16[768,128]{1,0:T(8,128)(2,1)}, u32[]{:S(2)}) copy-start(bf16[768,128]{1,0:T(8,128)(2,1)} %w_proj.1) | copy-start | bytes 589828
  11.4 0.7 %copy-start.3 = (s32[8]{0:T(128)S(1)}, s32[8]{0:T(128)}, u32[]{:S(2)}) copy-start(s32[8]{0:T(128)} %counts_hbm.1) | copy-start | bytes 100
  12.1 1.7 %copy-start.2 = (bf16[16,16,128]{2,1,0:T(8,128)(2,1)S(1)}, bf16[16,16,128]{2,1,0:T(8,128)(2,1)}, u32[]{:S(2)}) copy-start(bf16[16,16,128]{2,1,0:T(8,128)(2,1)} %refs_0_.1) | copy-start | bytes 196612
  13.9 5.8 %collective-permute-start.4 = (bf16[512,128]{1,0:T(8,128)(2,1)S(1)}, bf16[512,128]{1,0:T(8,128)(2,1)S(1)}, u32[]{:S(2)}, u32[]{:S(2)}) collective-permute-start(bf16[512,128]{1,0:T(8,128)(2,1)S(1)} %unit_pieces.2.refs_0_), channel_id=1, source_target_pairs={{0,2},{1,3},{2,0},{3,1},{4,6},{5,7},{6,4},{7,5},{8,10},{9,11},{10,... | collective-permute-start | bytes 393224 | tf_op jit(solution)/shard_map/ppermute | solution.py:237
  15.6 7.6 %collective-permute-start.5 = (bf16[512,128]{1,0:T(8,128)(2,1)S(1)}, bf16[512,128]{1,0:T(8,128)(2,1)S(1)}, u32[]{:S(2)}, u32[]{:S(2)}) collective-permute-start(bf16[512,128]{1,0:T(8,128)(2,1)S(1)} %unit_pieces.2.refs_0_), channel_id=1, source_target_pairs={{0,16},{1,17},{2,18},{3,19},{4,20},{5,21},{6,22},{7,23},{8,24},{9,... | collective-permute-start | bytes 393224 | tf_op jit(solution)/shard_map/ppermute | solution.py:237
  17.1 5.3 %collective-permute-start.8 = (bf16[512,128]{1,0:T(8,128)(2,1)S(1)}, bf16[512,128]{1,0:T(8,128)(2,1)S(1)}, u32[]{:S(2)}, u32[]{:S(2)}) collective-permute-start(bf16[512,128]{1,0:T(8,128)(2,1)S(1)} %unit_pieces.3.refs_1_), channel_id=1, source_target_pairs={{0,16},{1,17},{2,18},{3,19},{4,20},{5,21},{6,22},{7,23},{8,24},{9,... | collective-permute-start | bytes 393224 | tf_op jit(solution)/shard_map/ppermute | solution.py:237
  17.9 5.4 %collective-permute-start.7 = (bf16[512,128]{1,0:T(8,128)(2,1)S(1)}, bf16[512,128]{1,0:T(8,128)(2,1)S(1)}, u32[]{:S(2)}, u32[]{:S(2)}) collective-permute-start(bf16[512,128]{1,0:T(8,128)(2,1)S(1)} %unit_pieces.3.refs_1_), channel_id=1, source_target_pairs={{0,2},{1,3},{2,0},{3,1},{4,6},{5,7},{6,4},{7,5},{8,10},{9,11},{10,... | collective-permute-start | bytes 393224 | tf_op jit(solution)/shard_map/ppermute | solution.py:237
  18.4 9.1 %collective-permute-start.3 = (bf16[1024,128]{1,0:T(8,128)(2,1)S(1)}, bf16[1024,128]{1,0:T(8,128)(2,1)S(1)}, u32[]{:S(2)}, u32[]{:S(2)}) collective-permute-start(bf16[1024,128]{1,0:T(8,128)(2,1)S(1)} %pad_maximum_fusion), channel_id=1, source_target_pairs={{0,1},{1,0},{2,3},{3,2},{4,5},{5,4},{6,7},{7,6},{8,9},{9,8},{10,11... | collective-permute-start | bytes 786440 | tf_op jit(solution)/shard_map/ppermute | solution.py:237
  19.7 6.0 %collective-permute-start.10 = (bf16[512,128]{1,0:T(8,128)(2,1)S(1)}, bf16[512,128]{1,0:T(8,128)(2,1)S(1)}, u32[]{:S(2)}, u32[]{:S(2)}) collective-permute-start(bf16[512,128]{1,0:T(8,128)(2,1)S(1)} %collective-permute-done.4.refs_1_), channel_id=1, source_target_pairs={{0,16},{1,17},{2,18},{3,19},{4,20},{5,21},{6,22},{7,23},{8,24},{9,... | collective-permute-start | bytes 393224 | tf_op jit(solution)/shard_map/ppermute | solution.py:237
  22.4 5.0 %collective-permute-start.11 = (bf16[512,128]{1,0:T(8,128)(2,1)S(1)}, bf16[512,128]{1,0:T(8,128)(2,1)S(1)}, u32[]{:S(2)}, u32[]{:S(2)}) collective-permute-start(bf16[512,128]{1,0:T(8,128)(2,1)S(1)} %collective-permute-done.8.refs_2_), channel_id=1, source_target_pairs={{0,2},{1,3},{2,0},{3,1},{4,6},{5,7},{6,4},{7,5},{8,10},{9,11},{10,... | collective-permute-start | bytes 393224 | tf_op jit(solution)/shard_map/ppermute | solution.py:237
  23.2 6.9 %collective-permute-start.6 = (bf16[1024,128]{1,0:T(8,128)(2,1)S(1)}, bf16[1024,128]{1,0:T(8,128)(2,1)S(1)}, u32[]{:S(2)}, u32[]{:S(2)}) collective-permute-start(bf16[1024,128]{1,0:T(8,128)(2,1)S(1)} %pad_maximum_fusion.1), channel_id=1, source_target_pairs={{0,1},{1,0},{2,3},{3,2},{4,5},{5,4},{6,7},{7,6},{8,9},{9,8},{10,11... | collective-permute-start | bytes 786440 | tf_op jit(solution)/shard_map/ppermute | solution.py:237
  23.3 9.5 %collective-permute-start.9 = (bf16[1024,128]{1,0:T(8,128)(2,1)S(1)}, bf16[1024,128]{1,0:T(8,128)(2,1)S(1)}, u32[]{:S(2)}, u32[]{:S(2)}) collective-permute-start(bf16[1024,128]{1,0:T(8,128)(2,1)S(1)} %pad_maximum_fusion.2), channel_id=1, source_target_pairs={{0,1},{1,0},{2,3},{3,2},{4,5},{5,4},{6,7},{7,6},{8,9},{9,8},{10,11... | collective-permute-start | bytes 786440 | tf_op jit(solution)/shard_map/ppermute | solution.py:237
  27.4 8.2 %collective-permute-start.12 = (bf16[1024,128]{1,0:T(8,128)(2,1)S(1)}, bf16[1024,128]{1,0:T(8,128)(2,1)S(1)}, u32[]{:S(2)}, u32[]{:S(2)}) collective-permute-start(bf16[1024,128]{1,0:T(8,128)(2,1)S(1)} %pad_maximum_fusion.3), channel_id=1, source_target_pairs={{0,1},{1,0},{2,3},{3,2},{4,5},{5,4},{6,7},{7,6},{8,9},{9,8},{10,11... | collective-permute-start | bytes 786440 | tf_op jit(solution)/shard_map/ppermute | solution.py:237

commit v3 on v2

--- a/solution.py
+++ b/solution.py
@@ -30,24 +30,13 @@
 
 
 def cost(micros):
-    return pl.CostEstimate(flops=int(micros * 1e9), bytes_accessed=0, transcendentals=0)
-
-
-def docs_kernel(counts_hbm, hidden, w_proj, rows_out, inside, keep, last, lengths, vectors, counts, sem):
-    docs = last.shape[0]
-    rows = hidden.shape[0]
-    groups = rows // GROUP
-    tail = docs * GROUP
-    fetch = pltpu.make_async_copy(counts_hbm, counts, sem)
+    return pl.CostEstimate(flops=int(micros * 1e6), bytes_accessed=0, transcendentals=0)
+
+
+def layout_kernel(counts_any, inside, keep, last, lengths, counts, sem):
+    docs, groups = last.shape[0], keep.shape[0]
+    fetch = pltpu.make_async_copy(counts_any, counts, sem)
     fetch.start()
-    step = 384 if rows % 384 == 0 else rows
-    for lo in range(0, rows, step):
-        projected = jnp.dot(
-            hidden[lo : lo + step, :], w_proj[...], preferred_element_type=jnp.float32
-        )
-        vectors[lo : lo + step, :] = unit_rows(projected).astype(jnp.float32)
-    vectors[rows:, :] = jnp.zeros_like(vectors[rows:, :])
-    rows_out[tail:, :] = jnp.zeros_like(rows_out[tail:, :])
     fetch.wait()
     group = lax.broadcasted_iota(jnp.int32, keep.shape, 0)
     document = lax.broadcasted_iota(jnp.int32, last.shape, 0)
@@ -55,6 +44,53 @@
     keeps = jnp.ones(keep.shape, jnp.float32)
     lasts = jnp.zeros(last.shape, jnp.int32)
     sizes = jnp.zeros(last.shape, jnp.float32)
+    first = jnp.int32(0)
+    for d in range(docs):
+        count = counts[d]
+        full = count // GROUP
+        inside[d * GROUP : (d + 1) * GROUP, :] = (place < count - full * GROUP).astype(jnp.float32)
+        keeps = jnp.where(group == jnp.where(full > 0, first, groups), 0.0, keeps)
+        lasts = jnp.where(document == d, jnp.where(full > 0, first + full - 1, groups), lasts)
+        sizes = jnp.where(document == d, count.astype(jnp.float32), sizes)
+        first = first + full
+    keep[...] = keeps
+    last[...] = lasts
+    lengths[...] = sizes
+
+
+def document_layout(counts, rows):
+    docs, groups = counts.shape[0], rows // GROUP
+    return pl.pallas_call(
+        layout_kernel,
+        out_shape=(
+            jax.ShapeDtypeStruct((docs * GROUP, LANES), jnp.float32),
+            jax.ShapeDtypeStruct((groups, LANES), jnp.float32),
+            jax.ShapeDtypeStruct((docs, LANES), jnp.int32),
+            jax.ShapeDtypeStruct((docs, LANES), jnp.float32),
+        ),
+        in_specs=[ANY],
+        out_specs=(VMEM,) * 4,
+        scratch_shapes=[pltpu.SMEM((docs,), jnp.int32), pltpu.SemaphoreType.DMA],
+        compiler_params=params(4),
+        cost_estimate=cost(20000),
+        name="layout",
+    )(pltpu.with_memory_space_constraint(counts, pltpu.HBM))
+
+
+def docs_kernel(counts_any, hidden, w_proj, rows_out, vectors, counts, sem):
+    docs = counts.shape[0]
+    rows = hidden.shape[0]
+    tail = docs * GROUP
+    fetch = pltpu.make_async_copy(counts_any, counts, sem)
+    fetch.start()
+    step = 384 if rows % 384 == 0 else rows
+    for lo in range(0, rows, step):
+        block = slice(lo, lo + step)
+        projected = jnp.dot(hidden[block, :], w_proj[...], preferred_element_type=jnp.float32)
+        vectors[block, :] = unit_rows(projected).astype(jnp.float32)
+    vectors[rows:, :] = jnp.zeros_like(vectors[rows:, :])
+    rows_out[tail:, :] = jnp.zeros_like(rows_out[tail:, :])
+    fetch.wait()
     start = jnp.int32(0)
     first = jnp.int32(0)
     for d in range(docs):
@@ -70,41 +106,27 @@
         lax.fori_loop(0, full, move, 0)
         block = vectors[pl.ds(start + full * GROUP, GROUP), :]
         rows_out[d * GROUP : (d + 1) * GROUP, :] = block.astype(jnp.bfloat16)
-        inside[d * GROUP : (d + 1) * GROUP, :] = (place < count - full * GROUP).astype(jnp.float32)
-        keeps = jnp.where(group == jnp.where(full > 0, first, groups), 0.0, keeps)
-        lasts = jnp.where(document == d, jnp.where(full > 0, first + full - 1, groups), lasts)
-        sizes = jnp.where(document == d, count.astype(jnp.float32), sizes)
         start = start + count
         first = first + full
-    keep[...] = keeps
-    last[...] = lasts
-    lengths[...] = sizes
 
 
 def regroup_documents(hidden, counts, w_proj):
     rows, docs = hidden.shape[0], counts.shape[0]
     width = w_proj.shape[1]
-    groups = rows // GROUP
     return pl.pallas_call(
         docs_kernel,
-        out_shape=(
-            jax.ShapeDtypeStruct((docs * GROUP + rows, width), jnp.bfloat16),
-            jax.ShapeDtypeStruct((docs * GROUP, LANES), jnp.float32),
-            jax.ShapeDtypeStruct((groups, LANES), jnp.float32),
-            jax.ShapeDtypeStruct((docs, LANES), jnp.int32),
-            jax.ShapeDtypeStruct((docs, LANES), jnp.float32),
-        ),
+        out_shape=jax.ShapeDtypeStruct((docs * GROUP + rows, width), jnp.bfloat16),
         in_specs=[ANY, VMEM, VMEM],
-        out_specs=(VMEM,) * 5,
+        out_specs=VMEM,
         scratch_shapes=[
             pltpu.VMEM((rows + GROUP, width), jnp.float32),
             pltpu.SMEM((docs,), jnp.int32),
             pltpu.SemaphoreType.DMA,
         ],
         compiler_params=params(16),
-        cost_estimate=cost(3),
+        cost_estimate=cost(2.5),
         name="documents",
-    )(counts, hidden, w_proj)
+    )(pltpu.with_memory_space_constraint(counts, pltpu.HBM), hidden, w_proj)
 
 
 def unit_kernel(*refs):
@@ -144,7 +166,7 @@
 
     step = 24 if groups % 24 == 0 else groups
     ends = last[...]
-    for c, (chunk, place) in enumerate(zip(chunks, places)):
+    for c, chunk in enumerate(chunks):
         tokens = chunk[...]
         width = tokens.shape[0]
         block = weights(rows[:tail, :], tokens)
@@ -164,11 +186,13 @@
                 row = jnp.broadcast_to(keep[base + j : base + j + 1, :], (HALF, LANES))
                 total = total * wide(row, width) + (block[lo:mid] + block[mid:hi])
                 sums[c, base + j] = total
-    for c, (chunk, place) in enumerate(zip(chunks, places)):
+    odd = lax.axis_index("loop") % 2
+    for c, place in enumerate(places):
+        at = [even if even == other else jnp.where(odd == 0, even, other) for even, other in place]
         for d in range(docs):
             total = jnp.sum(sums[c, ends[d, 0]] + tail_sums[c, d], axis=0, keepdims=True)
-            for i, at in enumerate(place):
-                mass[at, d : d + 1, :] = total[:, i * PIECE : (i + 1) * PIECE]
+            for i, piece in enumerate(at):
+                mass[piece, d : d + 1, :] = total[:, i * PIECE : (i + 1) * PIECE]
 
 
 def add_masses(documents, mass, chunks, places, pieces):
@@ -187,7 +211,7 @@
             pltpu.VMEM((count, docs, HALF, width), jnp.float32),
         ],
         compiler_params=params(28),
-        cost_estimate=cost(1.2 * count * width / 1024),
+        cost_estimate=cost(20000),
         name="masses",
     )(rows, inside, keep, last, *before, *chunks)
 
@@ -233,40 +257,57 @@
     )(lengths, mass)
 
 
-def swap(values, mask, devices):
-    return lax.ppermute(values, ("shard", "loop"), [(i, i ^ mask) for i in range(devices)])
-
-
-def pair_places(mask, *along_z):
-    return tuple(((mask & 15) ^ bits) * 2 + (mask >> 4) for bits in along_z)
+def swap(values, even, odd=None):
+    odd = even if odd is None else odd
+    pairs = [(i, i ^ (even if i % 2 == 0 else odd)) for i in range(32)]
+    return lax.ppermute(values, ("shard", "loop"), pairs)
 
 
 def pair_body(hidden, segment, counts, w_proj, seeds):
     devices = 32
     core, x, z, far, y = 1, 2, 4, 8, 16
-    near, away = (0, z), (far, z | far)
-    send = functools.partial(swap, devices=devices)
-    raw_far = send(seeds, far)
-    raw_z = send(seeds, z)
-    documents = regroup_documents(hidden, counts, w_proj)
-    a = unit_pieces(seeds, raw_z)
-    raw_both = send(raw_far, z)
-    ax, ay = send(a, x), send(a, y)
-    b = unit_pieces(raw_far, raw_both)
-    bx, by = send(b, x), send(b, y)
-    axy, byx = send(ax, y), send(by, x)
-    mass = None
-    for va, vb, ma, mb, za, zb in (
-        (a, b, 0, 0, near, away),
-        (ax, ay, x, y, near, near),
-        (bx, by, x, y, away, away),
-        (axy, byx, x | y, x | y, near, away),
-    ):
-        places = (pair_places(ma, *za), pair_places(mb, *zb))
-        mass = add_masses(documents, mass, (va, vb), places, devices)
-        other = send(jnp.concatenate([va, vb], axis=0), core)
-        places = (pair_places(ma | core, *za) + pair_places(mb | core, *zb),)
-        mass = add_masses(documents, mass, (other,), places, devices)
+    after = lax.optimization_barrier
+    raw_far = swap(seeds, far)
+    raw_z = swap(seeds, z)
+    layout = document_layout(counts, hidden.shape[0])
+    raw_far, layout = after((raw_far, layout))
+    raw_both = swap(raw_far, z)
+    near = unit_pieces(seeds, raw_z)
+    first_near = swap(near, x, y)
+    away = unit_pieces(raw_far, raw_both)
+    first_away = swap(away, x, y)
+    own = jnp.concatenate([near, away], axis=0)
+    own_core = swap(own, core)
+    hidden, away = after((hidden, away))
+    rows = regroup_documents(hidden, counts, w_proj)
+    documents = (rows, *layout)
+
+    def add(mass, chunk, masks, through_core):
+        if through_core:
+            masks = (masks[1] ^ core, masks[0] ^ core)
+        place = tuple(
+            tuple(((mask & 15) ^ bits) * 2 + (mask >> 4) for mask in masks)
+            for bits in (0, z, far, z | far)
+        )
+        return add_masses(documents, mass, (chunk,), (place,), devices)
+
+    mass = add(None, own, (0, 0), False)
+    first_near, first_away, own, mass = after((first_near, first_away, own, mass))
+    first = jnp.concatenate([first_near, first_away], axis=0)
+    third = swap(first, y, x)
+    second = swap(own, y, x)
+    first_core = swap(first, core)
+    mass = add(mass, own_core, (0, 0), True)
+    mass = add(mass, first, (x, y), False)
+    mass = add(mass, first_core, (x, y), True)
+    third, mass = after((third, mass))
+    third_core = swap(third, core)
+    mass = add(mass, third, (x | y, x | y), False)
+    mass = add(mass, third_core, (x | y, x | y), True)
+    second, mass = after((second, mass))
+    second_core = swap(second, core)
+    mass = add(mass, second, (y, x), False)
+    mass = add(mass, second_core, (y, x), True)
     return score(2, 16, True, documents[-1], mass)
 
 
@@ -276,10 +317,11 @@
     tokens = every.shape[1]
     every = every.reshape(-1, every.shape[-1])
     pieces = every.shape[0] // PIECE
-    documents = regroup_documents(hidden, counts, w_proj)
+    layout = document_layout(counts, hidden.shape[0])
+    documents = (regroup_documents(hidden, counts, w_proj), *layout)
     mass = None
     for first in range(0, pieces, 4):
-        places = (tuple(range(first, first + 4)),)
+        places = (tuple((piece, piece) for piece in range(first, first + 4)),)
         chunk = every[first * PIECE : (first + 4) * PIECE]
         mass = add_masses(documents, mass, (chunk,), places, pieces)
     return score(1, tokens, False, documents[-1], mass)

time: 38.3 us -> 31.2 us (0.81)
  waiting for transfers between devices: 6.14 us -> 2.6 us
  local copies, waits for them, and re-layouts: 3.42 us -> 0.04 us
  Pallas kernels: 13.6 us -> 14.9 us
  starting transfers between devices: 14.4 us -> 13.4 us
    ppermute x13 -> x11, waiting for transfers between devices: 6.14 us -> 2.6 us  [swap(): return lax.ppermute(values, ('shard', 'loop'), pairs)]
    unnamed x8 -> x7, local copies, waits for them, and re-layouts: 3.42 us -> 0.02 us
    pallas_call x1 -> x2, Pallas kernels: 1.65 us -> 2.9 us  [the longest x1 2.04 us: regroup_documents(): pl.pallas_call(docs_kernel, out_shape=jax.ShapeDtypeStruct((docs * GROUP...]
    ppermute x13 -> x11, starting transfers between devices: 14.4 us -> 13.4 us  [swap(): return lax.ppermute(values, ('shard', 'loop'), pairs)]
  transfers between devices with their start and end apart: 13 -> 11, of which waited for: 4 -> 4; matrix products, arithmetic and copies ran while one was open for 0% -> 0% of each run, Pallas kernels for 30% -> 40%
where the time goes in v3:
time: 31.2 us; the launch traced here: 31.1 us
  Pallas kernels  14.9 us (48%)
  starting transfers between devices  13.4 us (43%)
  waiting for transfers between devices  2.6 us (8%)
    ppermute x11, starting transfers between devices, swap(): return lax.ppermute(values, ('shard', 'loop'), pairs)  13.4 us
    pallas_call x8, Pallas kernels, add_masses(): pl.pallas_call(functools.partial(mass_kernel, places), out_shape=jax.Shap...  10.7 us
    ppermute x11, waiting for transfers between devices, swap(): return lax.ppermute(values, ('shard', 'loop'), pairs)  2.6 us
    pallas_call x1, Pallas kernels, regroup_documents(): pl.pallas_call(docs_kernel, out_shape=jax.ShapeDtypeStruct((docs * GROUP...  2.04 us
    pallas_call x1, Pallas kernels, score(): pl.pallas_call(functools.partial(score_kernel, parts, tokens, relative),...  0.94 us
    pallas_call x1, Pallas kernels, document_layout(): pl.pallas_call(layout_kernel, out_shape=(jax.ShapeDtypeStruct((docs * GRO...  0.87 us
  transfers between devices with their start and end apart: 11, of which 4 were waited for; matrix products, arithmetic and copies ran while one was open for 0% of the time, Pallas kernels for 40%

profile of v3, /device:TPU:0, one launch (start us, length us, event | category | flops | bytes accessed | tf_op | source)
XLA Modules:
  0.0 31.1 jit_solution(5329505727767979016)
XLA Ops:
  0.0 4.0 %collective-permute-start = (bf16[16,16,128]{2,1,0:T(8,128)(2,1)}, bf16[16,16,128]{2,1,0:T(8,128)(2,1)S(1)}, u32[]{:S(2)}, u32[]{:S(2)}) collective-permute-start(bf16[16,16,128]{2,1,0:T(8,128)(2,1)} %refs_0_.1), channel_id=1, source_target_pairs={{0,8},{1,9},{2,10},{3,11},{4,12},{5,13},{6,14},{7,15},{8,0},{9,1},... | collective-permute-start | bytes 196616 | tf_op jit(solution)/shard_map/ppermute | solution.py:263
  4.0 1.6 %collective-permute-start.2 = (bf16[16,16,128]{2,1,0:T(8,128)(2,1)}, bf16[16,16,128]{2,1,0:T(8,128)(2,1)S(1)}, u32[]{:S(2)}, u32[]{:S(2)}) collective-permute-start(bf16[16,16,128]{2,1,0:T(8,128)(2,1)} %refs_0_.1), channel_id=1, source_target_pairs={{0,4},{1,5},{2,6},{3,7},{4,0},{5,1},{6,2},{7,3},{8,12},{9,13},{10,... | collective-permute-start | bytes 196616 | tf_op jit(solution)/shard_map/ppermute | solution.py:263
  5.6 0.9 %layout.1 = (f32[128,128]{1,0:T(8,128)S(1)}, f32[120,128]{1,0:T(8,128)S(1)}, s32[8,128]{1,0:T(8,128)S(1)}, f32[8,128]{1,0:T(8,128)S(1)}) custom-call(s32[8]{0:T(128)} %counts_any.3), custom_call_target="tpu_custom_call" | custom-call | flops 20000000000 | tf_op jit(solution)/shard_map/layout/pallas_call | solution.py:63
  6.5 0.9 %collective-permute-done.refs_0_ = bf16[16,16,128]{2,1,0:T(8,128)(2,1)S(1)} collective-permute-done((bf16[16,16,128]{2,1,0:T(8,128)(2,1)}, bf16[16,16,128]{2,1,0:T(8,128)(2,1)S(1)}, u32[]{:S(2)}, u32[]{:S(2)}) %collective-permute-start) | collective-permute-done | bytes 65568 | tf_op jit(solution)/shard_map/ppermute | solution.py:263
  7.4 1.3 %collective-permute-start.1 = (bf16[16,16,128]{2,1,0:T(8,128)(2,1)S(1)}, bf16[16,16,128]{2,1,0:T(8,128)(2,1)S(1)}, u32[]{:S(2)}, u32[]{:S(2)}) collective-permute-start(bf16[16,16,128]{2,1,0:T(8,128)(2,1)S(1)} %collective-permute-done.refs_0_), channel_id=1, source_target_pairs={{0,4},{1,5},{2,6},{3,7},{4,0},{5,1},{6,2},{7,3},{8,12},{9,13},{10,... | collective-permute-start | bytes 196616 | tf_op jit(solution)/shard_map/ppermute | solution.py:263
  8.7 0.0 collective-permute-done.2.refs_1_
  8.7 0.1 unit_pieces.3
  8.9 1.6 %collective-permute-start.3 = (bf16[512,128]{1,0:T(8,128)(2,1)S(1)}, bf16[512,128]{1,0:T(8,128)(2,1)S(1)}, u32[]{:S(2)}, u32[]{:S(2)}) collective-permute-start(bf16[512,128]{1,0:T(8,128)(2,1)S(1)} %unit_pieces.3), channel_id=1, source_target_pairs={{0,2},{1,17},{2,0},{3,19},{4,6},{5,21},{6,4},{7,23},{8,10},{9,25},... | collective-permute-start | bytes 393224 | tf_op jit(solution)/shard_map/ppermute | solution.py:263
  10.4 1.2 %collective-permute-done.1.refs_1_ = bf16[16,16,128]{2,1,0:T(8,128)(2,1)S(1)} collective-permute-done((bf16[16,16,128]{2,1,0:T(8,128)(2,1)S(1)}, bf16[16,16,128]{2,1,0:T(8,128)(2,1)S(1)}, u32[]{:S(2)}, u32[]{:S(2)}) %collective-permute-start.1) | collective-permute-done | bytes 65568 | tf_op jit(solution)/shard_map/ppermute | solution.py:263
  11.6 0.1 unit_pieces.2
  11.8 1.9 %collective-permute-start.4 = (bf16[512,128]{1,0:T(8,128)(2,1)S(1)}, bf16[512,128]{1,0:T(8,128)(2,1)S(1)}, u32[]{:S(2)}, u32[]{:S(2)}) collective-permute-start(bf16[512,128]{1,0:T(8,128)(2,1)S(1)} %unit_pieces.2), channel_id=1, source_target_pairs={{0,2},{1,17},{2,0},{3,19},{4,6},{5,21},{6,4},{7,23},{8,10},{9,25},... | collective-permute-start | bytes 393224 | tf_op jit(solution)/shard_map/ppermute | solution.py:263
  13.7 0.1 collective-permute-start.7
  13.8 2.0 %documents.1.rows = bf16[2048,128]{1,0:T(8,128)(2,1)S(1)} custom-call(s32[8]{0:T(128)} %counts_any.3, bf16[1920,768]{1,0:T(8,128)(2,1)S(1)} %copy-done, bf16[768,128]{1,0:T(8,128)(2,1)S(1)} %copy-done.1), custom_call_target="tpu_custom_call" | custom-call | flops 2500000 | tf_op jit(solution)/shard_map/documents/pallas_call | solution.py:116
  15.8 1.3 %masses.8.refs_0_ = f32[32,8,256]{2,1,0:T(8,128)S(1)} custom-call(bf16[2048,128]{1,0:T(8,128)(2,1)S(1)} %documents.1.rows, f32[128,128]{1,0:T(8,128)S(1)} %get-tuple-element.30.inside, f32[120,128]{1,0:T(8,128)S(1)} %get-tuple-element.31.keep, s32[8,128]{1,0:T(8,128)S(1)} %get-tuple-element.32.last, bf16[1024,128]{1,0:T(8,128)(2,1)S(1)} %pad_maximum_fusion.refs_0_), custom_call_target="tpu_custom_call" | custom-call | flops 20000000000 | tf_op jit(solution)/shard_map/masses/pallas_call | solution.py:203
  17.2 0.0 collective-permute-done.3
  17.2 0.0 collective-permute-done.4
  17.2 0.6 %collective-permute-start.8 = (bf16[1024,128]{1,0:T(8,128)(2,1)S(1)}, bf16[1024,128]{1,0:T(8,128)(2,1)S(1)}, u32[]{:S(2)}, u32[]{:S(2)}) collective-permute-start(bf16[1024,128]{1,0:T(8,128)(2,1)S(1)} %constant_dynamic-update-slice_fusion.refs_1_), channel_id=1, source_target_pairs={{0,1},{1,0},{2,3},{3,2},{4,5},{5,4},{6,7},{7,6},{8,9},{9,8},{10,11... | collective-permute-start | bytes 786440 | tf_op jit(solution)/shard_map/ppermute | solution.py:263
  17.8 1.4 %collective-permute-start.6 = (bf16[1024,128]{1,0:T(8,128)(2,1)S(1)}, bf16[1024,128]{1,0:T(8,128)(2,1)S(1)}, u32[]{:S(2)}, u32[]{:S(2)}) collective-permute-start(bf16[1024,128]{1,0:T(8,128)(2,1)S(1)} %constant_dynamic-update-slice_fusion.refs_1_), channel_id=1, source_target_pairs={{0,16},{1,3},{2,18},{3,1},{4,20},{5,7},{6,22},{7,5},{8,24},{9,11},... | collective-permute-start | bytes 786440 | tf_op jit(solution)/shard_map/ppermute | solution.py:263
  19.2 0.6 %collective-permute-start.5 = (bf16[1024,128]{1,0:T(8,128)(2,1)S(1)}, bf16[1024,128]{1,0:T(8,128)(2,1)S(1)}, u32[]{:S(2)}, u32[]{:S(2)}) collective-permute-start(bf16[1024,128]{1,0:T(8,128)(2,1)S(1)} %pad_maximum_fusion.refs_0_), channel_id=1, source_target_pairs={{0,16},{1,3},{2,18},{3,1},{4,20},{5,7},{6,22},{7,5},{8,24},{9,11},... | collective-permute-start | bytes 786440 | tf_op jit(solution)/shard_map/ppermute | solution.py:263
  19.8 0.0 collective-permute-done.7.refs_1_
  19.8 1.4 %masses.9.refs_0_ = f32[32,8,256]{2,1,0:T(8,128)S(1)} custom-call(bf16[2048,128]{1,0:T(8,128)(2,1)S(1)} %documents.1.rows, f32[128,128]{1,0:T(8,128)S(1)} %get-tuple-element.30.inside, f32[120,128]{1,0:T(8,128)S(1)} %get-tuple-element.31.keep, s32[8,128]{1,0:T(8,128)S(1)} %get-tuple-element.32.last, ...), custom_call_target="tpu_custom_call", output_to_operand_aliasing={{}: (4, {})} | custom-call | flops 20000000000 | tf_op jit(solution)/shard_map/masses/pallas_call | solution.py:203
  21.2 1.3 %masses.10.refs_0_ = f32[32,8,256]{2,1,0:T(8,128)S(1)} custom-call(bf16[2048,128]{1,0:T(8,128)(2,1)S(1)} %documents.1.rows, f32[128,128]{1,0:T(8,128)S(1)} %get-tuple-element.30.inside, f32[120,128]{1,0:T(8,128)S(1)} %get-tuple-element.31.keep, s32[8,128]{1,0:T(8,128)S(1)} %get-tuple-element.32.last, ...), custom_call_target="tpu_custom_call", output_to_operand_aliasing={{}: (4, {})} | custom-call | flops 20000000000 | tf_op jit(solution)/shard_map/masses/pallas_call | solution.py:203
  22.5 1.3 %masses.11.refs_0_ = f32[32,8,256]{2,1,0:T(8,128)S(1)} custom-call(bf16[2048,128]{1,0:T(8,128)(2,1)S(1)} %documents.1.rows, f32[128,128]{1,0:T(8,128)S(1)} %get-tuple-element.30.inside, f32[120,128]{1,0:T(8,128)S(1)} %get-tuple-element.31.keep, s32[8,128]{1,0:T(8,128)S(1)} %get-tuple-element.32.last, ...), custom_call_target="tpu_custom_call", output_to_operand_aliasing={{}: (4, {})} | custom-call | flops 20000000000 | tf_op jit(solution)/shard_map/masses/pallas_call | solution.py:203
  23.9 0.3 collective-permute-done.6.refs_1_
  24.2 1.4 %masses.12.refs_0_ = f32[32,8,256]{2,1,0:T(8,128)S(1)} custom-call(bf16[2048,128]{1,0:T(8,128)(2,1)S(1)} %documents.1.rows, f32[128,128]{1,0:T(8,128)S(1)} %get-tuple-element.30.inside, f32[120,128]{1,0:T(8,128)S(1)} %get-tuple-element.31.keep, s32[8,128]{1,0:T(8,128)S(1)} %get-tuple-element.32.last, ...), custom_call_target="tpu_custom_call", output_to_operand_aliasing={{}: (4, {})} | custom-call | flops 20000000000 | tf_op jit(solution)/shard_map/masses/pallas_call | solution.py:203
  25.5 0.2 collective-permute-done.9.refs_1_
  25.7 1.3 %masses.13.refs_0_ = f32[32,8,256]{2,1,0:T(8,128)S(1)} custom-call(bf16[2048,128]{1,0:T(8,128)(2,1)S(1)} %documents.1.rows, f32[128,128]{1,0:T(8,128)S(1)} %get-tuple-element.30.inside, f32[120,128]{1,0:T(8,128)S(1)} %get-tuple-element.31.keep, s32[8,128]{1,0:T(8,128)S(1)} %get-tuple-element.32.last, ...), custom_call_target="tpu_custom_call", output_to_operand_aliasing={{}: (4, {})} | custom-call | flops 20000000000 | tf_op jit(solution)/shard_map/masses/pallas_call | solution.py:203
  27.1 0.0 collective-permute-done.5.refs_1_
  27.1 0.4 %collective-permute-start.10 = (bf16[1024,128]{1,0:T(8,128)(2,1)S(1)}, bf16[1024,128]{1,0:T(8,128)(2,1)S(1)}, u32[]{:S(2)}, u32[]{:S(2)}) collective-permute-start(bf16[1024,128]{1,0:T(8,128)(2,1)S(1)} %collective-permute-done.5.refs_1_), channel_id=1, source_target_pairs={{0,1},{1,0},{2,3},{3,2},{4,5},{5,4},{6,7},{7,6},{8,9},{9,8},{10,11... | collective-permute-start | bytes 786440 | tf_op jit(solution)/shard_map/ppermute | solution.py:263
  27.5 1.3 %masses.14.refs_0_ = f32[32,8,256]{2,1,0:T(8,128)S(1)} custom-call(bf16[2048,128]{1,0:T(8,128)(2,1)S(1)} %documents.1.rows, f32[128,128]{1,0:T(8,128)S(1)} %get-tuple-element.30.inside, f32[120,128]{1,0:T(8,128)S(1)} %get-tuple-element.31.keep, s32[8,128]{1,0:T(8,128)S(1)} %get-tuple-element.32.last, ...), custom_call_target="tpu_custom_call", output_to_operand_aliasing={{}: (4, {})} | custom-call | flops 20000000000 | tf_op jit(solution)/shard_map/masses/pallas_call | solution.py:203
  28.8 1.3 %masses.15.mass = f32[32,8,256]{2,1,0:T(8,128)S(1)} custom-call(bf16[2048,128]{1,0:T(8,128)(2,1)S(1)} %documents.1.rows, f32[128,128]{1,0:T(8,128)S(1)} %get-tuple-element.30.inside, f32[120,128]{1,0:T(8,128)S(1)} %get-tuple-element.31.keep, s32[8,128]{1,0:T(8,128)S(1)} %get-tuple-element.32.last, ...), custom_call_target="tpu_custom_call", output_to_operand_aliasing={{}: (4, {})} | custom-call | flops 20000000000 | tf_op jit(solution)/shard_map/masses/pallas_call | solution.py:203
  30.2 0.9 %scores.1 = f32[8,256]{1,0:T(8,128)} custom-call(f32[8,128]{1,0:T(8,128)S(1)} %get-tuple-element.27.lengths, f32[32,8,256]{2,1,0:T(8,128)S(1)} %masses.15.mass), custom_call_target="tpu_custom_call" | custom-call | flops 1000000 | tf_op jit(solution)/shard_map/scores/pallas_call | solution.py:249
  (12 shorter events, 0.1 us)
Async XLA Ops:
  0.0 8.7 %copy-start.2 = (bf16[16,16,128]{2,1,0:T(8,128)(2,1)S(1)}, bf16[16,16,128]{2,1,0:T(8,128)(2,1)}, u32[]{:S(2)}) copy-start(bf16[16,16,128]{2,1,0:T(8,128)(2,1)} %refs_0_.1) | copy-start | bytes 196612
  0.0 13.8 %copy-start.1 = (bf16[768,128]{1,0:T(8,128)(2,1)S(1)}, bf16[768,128]{1,0:T(8,128)(2,1)}, u32[]{:S(2)}) copy-start(bf16[768,128]{1,0:T(8,128)(2,1)} %w_proj.1) | copy-start | bytes 589828
  0.0 7.4 %collective-permute-start = (bf16[16,16,128]{2,1,0:T(8,128)(2,1)}, bf16[16,16,128]{2,1,0:T(8,128)(2,1)S(1)}, u32[]{:S(2)}, u32[]{:S(2)}) collective-permute-start(bf16[16,16,128]{2,1,0:T(8,128)(2,1)} %refs_0_.1), channel_id=1, source_target_pairs={{0,8},{1,9},{2,10},{3,11},{4,12},{5,13},{6,14},{7,15},{8,0},{9,1},... | collective-permute-start | bytes 196616 | tf_op jit(solution)/shard_map/ppermute | solution.py:263
  4.0 4.7 %collective-permute-start.2 = (bf16[16,16,128]{2,1,0:T(8,128)(2,1)}, bf16[16,16,128]{2,1,0:T(8,128)(2,1)S(1)}, u32[]{:S(2)}, u32[]{:S(2)}) collective-permute-start(bf16[16,16,128]{2,1,0:T(8,128)(2,1)} %refs_0_.1), channel_id=1, source_target_pairs={{0,4},{1,5},{2,6},{3,7},{4,0},{5,1},{6,2},{7,3},{8,12},{9,13},{10,... | collective-permute-start | bytes 196616 | tf_op jit(solution)/shard_map/ppermute | solution.py:263
  5.6 8.2 %copy-start = (bf16[1920,768]{1,0:T(8,128)(2,1)S(1)}, bf16[1920,768]{1,0:T(8,128)(2,1)}, u32[]{:S(2)}) copy-start(bf16[1920,768]{1,0:T(8,128)(2,1)} %hidden) | copy-start | bytes 8847364
  7.4 4.3 %collective-permute-start.1 = (bf16[16,16,128]{2,1,0:T(8,128)(2,1)S(1)}, bf16[16,16,128]{2,1,0:T(8,128)(2,1)S(1)}, u32[]{:S(2)}, u32[]{:S(2)}) collective-permute-start(bf16[16,16,128]{2,1,0:T(8,128)(2,1)S(1)} %collective-permute-done.refs_0_), channel_id=1, source_target_pairs={{0,4},{1,5},{2,6},{3,7},{4,0},{5,1},{6,2},{7,3},{8,12},{9,13},{10,... | collective-permute-start | bytes 196616 | tf_op jit(solution)/shard_map/ppermute | solution.py:263
  8.9 8.3 %collective-permute-start.3 = (bf16[512,128]{1,0:T(8,128)(2,1)S(1)}, bf16[512,128]{1,0:T(8,128)(2,1)S(1)}, u32[]{:S(2)}, u32[]{:S(2)}) collective-permute-start(bf16[512,128]{1,0:T(8,128)(2,1)S(1)} %unit_pieces.3), channel_id=1, source_target_pairs={{0,2},{1,17},{2,0},{3,19},{4,6},{5,21},{6,4},{7,23},{8,10},{9,25},... | collective-permute-start | bytes 393224 | tf_op jit(solution)/shard_map/ppermute | solution.py:263
  11.8 5.4 %collective-permute-start.4 = (bf16[512,128]{1,0:T(8,128)(2,1)S(1)}, bf16[512,128]{1,0:T(8,128)(2,1)S(1)}, u32[]{:S(2)}, u32[]{:S(2)}) collective-permute-start(bf16[512,128]{1,0:T(8,128)(2,1)S(1)} %unit_pieces.2), channel_id=1, source_target_pairs={{0,2},{1,17},{2,0},{3,19},{4,6},{5,21},{6,4},{7,23},{8,10},{9,25},... | collective-permute-start | bytes 393224 | tf_op jit(solution)/shard_map/ppermute | solution.py:263
  13.7 6.2 %collective-permute-start.7 = (bf16[1024,128]{1,0:T(8,128)(2,1)S(1)}, bf16[1024,128]{1,0:T(8,128)(2,1)S(1)}, u32[]{:S(2)}, u32[]{:S(2)}) collective-permute-start(bf16[1024,128]{1,0:T(8,128)(2,1)S(1)} %pad_maximum_fusion.refs_0_), channel_id=1, source_target_pairs={{0,1},{1,0},{2,3},{3,2},{4,5},{5,4},{6,7},{7,6},{8,9},{9,8},{10,11... | collective-permute-start | bytes 786440 | tf_op jit(solution)/shard_map/ppermute | solution.py:263
  17.2 5.3 %collective-permute-start.8 = (bf16[1024,128]{1,0:T(8,128)(2,1)S(1)}, bf16[1024,128]{1,0:T(8,128)(2,1)S(1)}, u32[]{:S(2)}, u32[]{:S(2)}) collective-permute-start(bf16[1024,128]{1,0:T(8,128)(2,1)S(1)} %constant_dynamic-update-slice_fusion.refs_1_), channel_id=1, source_target_pairs={{0,1},{1,0},{2,3},{3,2},{4,5},{5,4},{6,7},{7,6},{8,9},{9,8},{10,11... | collective-permute-start | bytes 786440 | tf_op jit(solution)/shard_map/ppermute | solution.py:263
  17.8 6.4 %collective-permute-start.6 = (bf16[1024,128]{1,0:T(8,128)(2,1)S(1)}, bf16[1024,128]{1,0:T(8,128)(2,1)S(1)}, u32[]{:S(2)}, u32[]{:S(2)}) collective-permute-start(bf16[1024,128]{1,0:T(8,128)(2,1)S(1)} %constant_dynamic-update-slice_fusion.refs_1_), channel_id=1, source_target_pairs={{0,16},{1,3},{2,18},{3,1},{4,20},{5,7},{6,22},{7,5},{8,24},{9,11},... | collective-permute-start | bytes 786440 | tf_op jit(solution)/shard_map/ppermute | solution.py:263
  19.2 7.9 %collective-permute-start.5 = (bf16[1024,128]{1,0:T(8,128)(2,1)S(1)}, bf16[1024,128]{1,0:T(8,128)(2,1)S(1)}, u32[]{:S(2)}, u32[]{:S(2)}) collective-permute-start(bf16[1024,128]{1,0:T(8,128)(2,1)S(1)} %pad_maximum_fusion.refs_0_), channel_id=1, source_target_pairs={{0,16},{1,3},{2,18},{3,1},{4,20},{5,7},{6,22},{7,5},{8,24},{9,11},... | collective-permute-start | bytes 786440 | tf_op jit(solution)/shard_map/ppermute | solution.py:263
  24.2 1.5 %collective-permute-start.9 = (bf16[1024,128]{1,0:T(8,128)(2,1)S(1)}, bf16[1024,128]{1,0:T(8,128)(2,1)S(1)}, u32[]{:S(2)}, u32[]{:S(2)}) collective-permute-start(bf16[1024,128]{1,0:T(8,128)(2,1)S(1)} %collective-permute-done.6.refs_1_), channel_id=1, source_target_pairs={{0,1},{1,0},{2,3},{3,2},{4,5},{5,4},{6,7},{7,6},{8,9},{9,8},{10,11... | collective-permute-start | bytes 786440 | tf_op jit(solution)/shard_map/ppermute | solution.py:263
  27.1 1.7 %collective-permute-start.10 = (bf16[1024,128]{1,0:T(8,128)(2,1)S(1)}, bf16[1024,128]{1,0:T(8,128)(2,1)S(1)}, u32[]{:S(2)}, u32[]{:S(2)}) collective-permute-start(bf16[1024,128]{1,0:T(8,128)(2,1)S(1)} %collective-permute-done.5.refs_1_), channel_id=1, source_target_pairs={{0,1},{1,0},{2,3},{3,2},{4,5},{5,4},{6,7},{7,6},{8,9},{9,8},{10,11... | collective-permute-start | bytes 786440 | tf_op jit(solution)/shard_map/ppermute | solution.py:263

commit v4 on v3

--- a/solution.py
+++ b/solution.py
@@ -267,15 +267,15 @@
     devices = 32
     core, x, z, far, y = 1, 2, 4, 8, 16
     after = lax.optimization_barrier
-    raw_far = swap(seeds, far)
-    raw_z = swap(seeds, z)
+    raw_far = swap(seeds, far, x)
+    raw_z = swap(seeds, z, y)
     layout = document_layout(counts, hidden.shape[0])
     raw_far, layout = after((raw_far, layout))
-    raw_both = swap(raw_far, z)
+    raw_both = swap(raw_far, z, y)
     near = unit_pieces(seeds, raw_z)
-    first_near = swap(near, x, y)
+    first_near = swap(near, x, far)
     away = unit_pieces(raw_far, raw_both)
-    first_away = swap(away, x, y)
+    first_away = swap(away, x, far)
     own = jnp.concatenate([near, away], axis=0)
     own_core = swap(own, core)
     hidden, away = after((hidden, away))
@@ -283,31 +283,34 @@
     documents = (rows, *layout)
 
     def add(mass, chunk, masks, through_core):
+        lanes = [
+            [mask ^ bits for bits in (0, one, two, one | two)]
+            for mask, one, two in ((masks[0], z, far), (masks[1], y, x))
+        ]
         if through_core:
-            masks = (masks[1] ^ core, masks[0] ^ core)
+            lanes = [[mask ^ core for mask in lane] for lane in lanes[::-1]]
         place = tuple(
-            tuple(((mask & 15) ^ bits) * 2 + (mask >> 4) for mask in masks)
-            for bits in (0, z, far, z | far)
+            tuple((mask & 15) * 2 + (mask >> 4) for mask in pair) for pair in zip(*lanes)
         )
         return add_masses(documents, mass, (chunk,), (place,), devices)
 
     mass = add(None, own, (0, 0), False)
     first_near, first_away, own, mass = after((first_near, first_away, own, mass))
     first = jnp.concatenate([first_near, first_away], axis=0)
-    third = swap(first, y, x)
-    second = swap(own, y, x)
+    third = swap(first, y, z)
+    second = swap(own, y, z)
     first_core = swap(first, core)
     mass = add(mass, own_core, (0, 0), True)
-    mass = add(mass, first, (x, y), False)
-    mass = add(mass, first_core, (x, y), True)
+    mass = add(mass, first, (x, far), False)
+    mass = add(mass, first_core, (x, far), True)
     third, mass = after((third, mass))
     third_core = swap(third, core)
-    mass = add(mass, third, (x | y, x | y), False)
-    mass = add(mass, third_core, (x | y, x | y), True)
+    mass = add(mass, third, (x | y, z | far), False)
+    mass = add(mass, third_core, (x | y, z | far), True)
     second, mass = after((second, mass))
     second_core = swap(second, core)
-    mass = add(mass, second, (y, x), False)
-    mass = add(mass, second_core, (y, x), True)
+    mass = add(mass, second, (y, z), False)
+    mass = add(mass, second_core, (y, z), True)
     return score(2, 16, True, documents[-1], mass)
 
 

time: 31.2 us -> 30.7 us (0.984)
  waiting for transfers between devices: 2.6 us -> 2.22 us
    ppermute x11, waiting for transfers between devices: 2.6 us -> 2.22 us  [swap(): return lax.ppermute(values, ('shard', 'loop'), pairs)]
  transfers between devices with their start and end apart: 11 -> 11, of which waited for: 4 -> 6; matrix products, arithmetic and copies ran while one was open for 0% -> 0% of each run, Pallas kernels for 40% -> 41%
where the time goes in v4:
time: 30.7 us; the launch traced here: 30.6 us
  Pallas kernels  14.8 us (48%)
  starting transfers between devices  13.3 us (43%)
  waiting for transfers between devices  2.22 us (7%)
    ppermute x11, starting transfers between devices, swap(): return lax.ppermute(values, ('shard', 'loop'), pairs)  13.3 us
    pallas_call x8, Pallas kernels, add_masses(): pl.pallas_call(functools.partial(mass_kernel, places), out_shape=jax.Shap...  10.7 us
    ppermute x11, waiting for transfers between devices, swap(): return lax.ppermute(values, ('shard', 'loop'), pairs)  2.22 us
    pallas_call x1, Pallas kernels, regroup_documents(): pl.pallas_call(docs_kernel, out_shape=jax.ShapeDtypeStruct((docs * GROUP...  2 us
    pallas_call x1, Pallas kernels, score(): pl.pallas_call(functools.partial(score_kernel, parts, tokens, relative),...  0.94 us
    pallas_call x1, Pallas kernels, document_layout(): pl.pallas_call(layout_kernel, out_shape=(jax.ShapeDtypeStruct((docs * GRO...  0.87 us
  transfers between devices with their start and end apart: 11, of which 6 were waited for; matrix products, arithmetic and copies ran while one was open for 0% of the time, Pallas kernels for 41%

profile of v4, /device:TPU:0, one launch (start us, length us, event | category | flops | bytes accessed | tf_op | source)
XLA Modules:
  0.0 30.6 jit_solution(4339252371067061399)
XLA Ops:
  0.0 4.0 %collective-permute-start = (bf16[16,16,128]{2,1,0:T(8,128)(2,1)}, bf16[16,16,128]{2,1,0:T(8,128)(2,1)S(1)}, u32[]{:S(2)}, u32[]{:S(2)}) collective-permute-start(bf16[16,16,128]{2,1,0:T(8,128)(2,1)} %refs_0_.1), channel_id=1, source_target_pairs={{0,8},{1,3},{2,10},{3,1},{4,12},{5,7},{6,14},{7,5},{8,0},{9,11},{1... | collective-permute-start | bytes 196616 | tf_op jit(solution)/shard_map/ppermute | solution.py:263
  4.0 1.6 %collective-permute-start.2 = (bf16[16,16,128]{2,1,0:T(8,128)(2,1)}, bf16[16,16,128]{2,1,0:T(8,128)(2,1)S(1)}, u32[]{:S(2)}, u32[]{:S(2)}) collective-permute-start(bf16[16,16,128]{2,1,0:T(8,128)(2,1)} %refs_0_.1), channel_id=1, source_target_pairs={{0,4},{1,17},{2,6},{3,19},{4,0},{5,21},{6,2},{7,23},{8,12},{9,25},... | collective-permute-start | bytes 196616 | tf_op jit(solution)/shard_map/ppermute | solution.py:263
  5.6 0.9 %layout.1 = (f32[128,128]{1,0:T(8,128)S(1)}, f32[120,128]{1,0:T(8,128)S(1)}, s32[8,128]{1,0:T(8,128)S(1)}, f32[8,128]{1,0:T(8,128)S(1)}) custom-call(s32[8]{0:T(128)} %counts_any.3), custom_call_target="tpu_custom_call" | custom-call | flops 20000000000 | tf_op jit(solution)/shard_map/layout/pallas_call | solution.py:63
  6.5 0.1 collective-permute-done.refs_0_
  6.6 1.8 %collective-permute-start.1 = (bf16[16,16,128]{2,1,0:T(8,128)(2,1)S(1)}, bf16[16,16,128]{2,1,0:T(8,128)(2,1)S(1)}, u32[]{:S(2)}, u32[]{:S(2)}) collective-permute-start(bf16[16,16,128]{2,1,0:T(8,128)(2,1)S(1)} %collective-permute-done.refs_0_), channel_id=1, source_target_pairs={{0,4},{1,17},{2,6},{3,19},{4,0},{5,21},{6,2},{7,23},{8,12},{9,25},... | collective-permute-start | bytes 196616 | tf_op jit(solution)/shard_map/ppermute | solution.py:263
  8.4 0.1 collective-permute-done.2.refs_1_
  8.5 0.1 unit_pieces.3
  8.7 1.6 %collective-permute-start.3 = (bf16[512,128]{1,0:T(8,128)(2,1)S(1)}, bf16[512,128]{1,0:T(8,128)(2,1)S(1)}, u32[]{:S(2)}, u32[]{:S(2)}) collective-permute-start(bf16[512,128]{1,0:T(8,128)(2,1)S(1)} %unit_pieces.3), channel_id=1, source_target_pairs={{0,2},{1,9},{2,0},{3,11},{4,6},{5,13},{6,4},{7,15},{8,10},{9,1},{1... | collective-permute-start | bytes 393224 | tf_op jit(solution)/shard_map/ppermute | solution.py:263
  10.2 1.4 %collective-permute-done.1.refs_1_ = bf16[16,16,128]{2,1,0:T(8,128)(2,1)S(1)} collective-permute-done((bf16[16,16,128]{2,1,0:T(8,128)(2,1)S(1)}, bf16[16,16,128]{2,1,0:T(8,128)(2,1)S(1)}, u32[]{:S(2)}, u32[]{:S(2)}) %collective-permute-start.1) | collective-permute-done | bytes 65568 | tf_op jit(solution)/shard_map/ppermute | solution.py:263
  11.6 0.1 unit_pieces.2
  11.8 1.3 %collective-permute-start.4 = (bf16[512,128]{1,0:T(8,128)(2,1)S(1)}, bf16[512,128]{1,0:T(8,128)(2,1)S(1)}, u32[]{:S(2)}, u32[]{:S(2)}) collective-permute-start(bf16[512,128]{1,0:T(8,128)(2,1)S(1)} %unit_pieces.2), channel_id=1, source_target_pairs={{0,2},{1,9},{2,0},{3,11},{4,6},{5,13},{6,4},{7,15},{8,10},{9,1},{1... | collective-permute-start | bytes 393224 | tf_op jit(solution)/shard_map/ppermute | solution.py:263
  13.1 0.1 collective-permute-start.7
  13.2 2.0 %documents.1.rows = bf16[2048,128]{1,0:T(8,128)(2,1)S(1)} custom-call(s32[8]{0:T(128)} %counts_any.3, bf16[1920,768]{1,0:T(8,128)(2,1)S(1)} %copy-done, bf16[768,128]{1,0:T(8,128)(2,1)S(1)} %copy-done.1), custom_call_target="tpu_custom_call" | custom-call | flops 2500000 | tf_op jit(solution)/shard_map/documents/pallas_call | solution.py:116
  15.2 1.3 %masses.8.refs_0_ = f32[32,8,256]{2,1,0:T(8,128)S(1)} custom-call(bf16[2048,128]{1,0:T(8,128)(2,1)S(1)} %documents.1.rows, f32[128,128]{1,0:T(8,128)S(1)} %get-tuple-element.30.inside, f32[120,128]{1,0:T(8,128)S(1)} %get-tuple-element.31.keep, s32[8,128]{1,0:T(8,128)S(1)} %get-tuple-element.32.last, bf16[1024,128]{1,0:T(8,128)(2,1)S(1)} %pad_maximum_fusion.refs_0_), custom_call_target="tpu_custom_call" | custom-call | flops 20000000000 | tf_op jit(solution)/shard_map/masses/pallas_call | solution.py:203
  16.6 0.2 collective-permute-done.4
  16.8 0.4 %collective-permute-start.8 = (bf16[1024,128]{1,0:T(8,128)(2,1)S(1)}, bf16[1024,128]{1,0:T(8,128)(2,1)S(1)}, u32[]{:S(2)}, u32[]{:S(2)}) collective-permute-start(bf16[1024,128]{1,0:T(8,128)(2,1)S(1)} %constant_dynamic-update-slice_fusion.refs_1_), channel_id=1, source_target_pairs={{0,1},{1,0},{2,3},{3,2},{4,5},{5,4},{6,7},{7,6},{8,9},{9,8},{10,11... | collective-permute-start | bytes 786440 | tf_op jit(solution)/shard_map/ppermute | solution.py:263
  17.3 1.3 %collective-permute-start.6 = (bf16[1024,128]{1,0:T(8,128)(2,1)S(1)}, bf16[1024,128]{1,0:T(8,128)(2,1)S(1)}, u32[]{:S(2)}, u32[]{:S(2)}) collective-permute-start(bf16[1024,128]{1,0:T(8,128)(2,1)S(1)} %constant_dynamic-update-slice_fusion.refs_1_), channel_id=1, source_target_pairs={{0,16},{1,5},{2,18},{3,7},{4,20},{5,1},{6,22},{7,3},{8,24},{9,13},... | collective-permute-start | bytes 786440 | tf_op jit(solution)/shard_map/ppermute | solution.py:263
  18.6 0.7 %collective-permute-start.5 = (bf16[1024,128]{1,0:T(8,128)(2,1)S(1)}, bf16[1024,128]{1,0:T(8,128)(2,1)S(1)}, u32[]{:S(2)}, u32[]{:S(2)}) collective-permute-start(bf16[1024,128]{1,0:T(8,128)(2,1)S(1)} %pad_maximum_fusion.refs_0_), channel_id=1, source_target_pairs={{0,16},{1,5},{2,18},{3,7},{4,20},{5,1},{6,22},{7,3},{8,24},{9,13},... | collective-permute-start | bytes 786440 | tf_op jit(solution)/shard_map/ppermute | solution.py:263
  19.3 1.4 %masses.9.refs_0_ = f32[32,8,256]{2,1,0:T(8,128)S(1)} custom-call(bf16[2048,128]{1,0:T(8,128)(2,1)S(1)} %documents.1.rows, f32[128,128]{1,0:T(8,128)S(1)} %get-tuple-element.30.inside, f32[120,128]{1,0:T(8,128)S(1)} %get-tuple-element.31.keep, s32[8,128]{1,0:T(8,128)S(1)} %get-tuple-element.32.last, ...), custom_call_target="tpu_custom_call", output_to_operand_aliasing={{}: (4, {})} | custom-call | flops 20000000000 | tf_op jit(solution)/shard_map/masses/pallas_call | solution.py:203
  20.7 1.3 %masses.10.refs_0_ = f32[32,8,256]{2,1,0:T(8,128)S(1)} custom-call(bf16[2048,128]{1,0:T(8,128)(2,1)S(1)} %documents.1.rows, f32[128,128]{1,0:T(8,128)S(1)} %get-tuple-element.30.inside, f32[120,128]{1,0:T(8,128)S(1)} %get-tuple-element.31.keep, s32[8,128]{1,0:T(8,128)S(1)} %get-tuple-element.32.last, ...), custom_call_target="tpu_custom_call", output_to_operand_aliasing={{}: (4, {})} | custom-call | flops 20000000000 | tf_op jit(solution)/shard_map/masses/pallas_call | solution.py:203
  22.0 0.0 collective-permute-done.8.refs_1_
  22.0 1.4 %masses.11.refs_0_ = f32[32,8,256]{2,1,0:T(8,128)S(1)} custom-call(bf16[2048,128]{1,0:T(8,128)(2,1)S(1)} %documents.1.rows, f32[128,128]{1,0:T(8,128)S(1)} %get-tuple-element.30.inside, f32[120,128]{1,0:T(8,128)S(1)} %get-tuple-element.31.keep, s32[8,128]{1,0:T(8,128)S(1)} %get-tuple-element.32.last, ...), custom_call_target="tpu_custom_call", output_to_operand_aliasing={{}: (4, {})} | custom-call | flops 20000000000 | tf_op jit(solution)/shard_map/masses/pallas_call | solution.py:203
  23.4 0.3 collective-permute-done.6.refs_1_
  23.6 0.0 collective-permute-start.9
  23.6 1.3 %masses.12.refs_0_ = f32[32,8,256]{2,1,0:T(8,128)S(1)} custom-call(bf16[2048,128]{1,0:T(8,128)(2,1)S(1)} %documents.1.rows, f32[128,128]{1,0:T(8,128)S(1)} %get-tuple-element.30.inside, f32[120,128]{1,0:T(8,128)S(1)} %get-tuple-element.31.keep, s32[8,128]{1,0:T(8,128)S(1)} %get-tuple-element.32.last, ...), custom_call_target="tpu_custom_call", output_to_operand_aliasing={{}: (4, {})} | custom-call | flops 20000000000 | tf_op jit(solution)/shard_map/masses/pallas_call | solution.py:203
  25.0 0.2 collective-permute-done.9.refs_1_
  25.2 1.3 %masses.13.refs_0_ = f32[32,8,256]{2,1,0:T(8,128)S(1)} custom-call(bf16[2048,128]{1,0:T(8,128)(2,1)S(1)} %documents.1.rows, f32[128,128]{1,0:T(8,128)S(1)} %get-tuple-element.30.inside, f32[120,128]{1,0:T(8,128)S(1)} %get-tuple-element.31.keep, s32[8,128]{1,0:T(8,128)S(1)} %get-tuple-element.32.last, ...), custom_call_target="tpu_custom_call", output_to_operand_aliasing={{}: (4, {})} | custom-call | flops 20000000000 | tf_op jit(solution)/shard_map/masses/pallas_call | solution.py:203
  26.5 0.4 %collective-permute-start.10 = (bf16[1024,128]{1,0:T(8,128)(2,1)S(1)}, bf16[1024,128]{1,0:T(8,128)(2,1)S(1)}, u32[]{:S(2)}, u32[]{:S(2)}) collective-permute-start(bf16[1024,128]{1,0:T(8,128)(2,1)S(1)} %collective-permute-done.5.refs_1_), channel_id=1, source_target_pairs={{0,1},{1,0},{2,3},{3,2},{4,5},{5,4},{6,7},{7,6},{8,9},{9,8},{10,11... | collective-permute-start | bytes 786440 | tf_op jit(solution)/shard_map/ppermute | solution.py:263
  26.9 1.3 %masses.14.refs_0_ = f32[32,8,256]{2,1,0:T(8,128)S(1)} custom-call(bf16[2048,128]{1,0:T(8,128)(2,1)S(1)} %documents.1.rows, f32[128,128]{1,0:T(8,128)S(1)} %get-tuple-element.30.inside, f32[120,128]{1,0:T(8,128)S(1)} %get-tuple-element.31.keep, s32[8,128]{1,0:T(8,128)S(1)} %get-tuple-element.32.last, ...), custom_call_target="tpu_custom_call", output_to_operand_aliasing={{}: (4, {})} | custom-call | flops 20000000000 | tf_op jit(solution)/shard_map/masses/pallas_call | solution.py:203
  28.3 0.0 collective-permute-done.10.refs_1_
  28.3 1.3 %masses.15.mass = f32[32,8,256]{2,1,0:T(8,128)S(1)} custom-call(bf16[2048,128]{1,0:T(8,128)(2,1)S(1)} %documents.1.rows, f32[128,128]{1,0:T(8,128)S(1)} %get-tuple-element.30.inside, f32[120,128]{1,0:T(8,128)S(1)} %get-tuple-element.31.keep, s32[8,128]{1,0:T(8,128)S(1)} %get-tuple-element.32.last, ...), custom_call_target="tpu_custom_call", output_to_operand_aliasing={{}: (4, {})} | custom-call | flops 20000000000 | tf_op jit(solution)/shard_map/masses/pallas_call | solution.py:203
  29.6 0.9 %scores.1 = f32[8,256]{1,0:T(8,128)} custom-call(f32[8,128]{1,0:T(8,128)S(1)} %get-tuple-element.27.lengths, f32[32,8,256]{2,1,0:T(8,128)S(1)} %masses.15.mass), custom_call_target="tpu_custom_call" | custom-call | flops 1000000 | tf_op jit(solution)/shard_map/scores/pallas_call | solution.py:249
  (12 shorter events, 0.1 us)
Async XLA Ops:
  0.0 8.5 %copy-start.2 = (bf16[16,16,128]{2,1,0:T(8,128)(2,1)S(1)}, bf16[16,16,128]{2,1,0:T(8,128)(2,1)}, u32[]{:S(2)}) copy-start(bf16[16,16,128]{2,1,0:T(8,128)(2,1)} %refs_0_.1) | copy-start | bytes 196612
  0.0 13.2 %copy-start.1 = (bf16[768,128]{1,0:T(8,128)(2,1)S(1)}, bf16[768,128]{1,0:T(8,128)(2,1)}, u32[]{:S(2)}) copy-start(bf16[768,128]{1,0:T(8,128)(2,1)} %w_proj.1) | copy-start | bytes 589828
  0.0 6.6 %collective-permute-start = (bf16[16,16,128]{2,1,0:T(8,128)(2,1)}, bf16[16,16,128]{2,1,0:T(8,128)(2,1)S(1)}, u32[]{:S(2)}, u32[]{:S(2)}) collective-permute-start(bf16[16,16,128]{2,1,0:T(8,128)(2,1)} %refs_0_.1), channel_id=1, source_target_pairs={{0,8},{1,3},{2,10},{3,1},{4,12},{5,7},{6,14},{7,5},{8,0},{9,11},{1... | collective-permute-start | bytes 196616 | tf_op jit(solution)/shard_map/ppermute | solution.py:263
  4.0 4.5 %collective-permute-start.2 = (bf16[16,16,128]{2,1,0:T(8,128)(2,1)}, bf16[16,16,128]{2,1,0:T(8,128)(2,1)S(1)}, u32[]{:S(2)}, u32[]{:S(2)}) collective-permute-start(bf16[16,16,128]{2,1,0:T(8,128)(2,1)} %refs_0_.1), channel_id=1, source_target_pairs={{0,4},{1,17},{2,6},{3,19},{4,0},{5,21},{6,2},{7,23},{8,12},{9,25},... | collective-permute-start | bytes 196616 | tf_op jit(solution)/shard_map/ppermute | solution.py:263
  5.6 7.6 %copy-start = (bf16[1920,768]{1,0:T(8,128)(2,1)S(1)}, bf16[1920,768]{1,0:T(8,128)(2,1)}, u32[]{:S(2)}) copy-start(bf16[1920,768]{1,0:T(8,128)(2,1)} %hidden) | copy-start | bytes 8847364
  6.6 5.0 %collective-permute-start.1 = (bf16[16,16,128]{2,1,0:T(8,128)(2,1)S(1)}, bf16[16,16,128]{2,1,0:T(8,128)(2,1)S(1)}, u32[]{:S(2)}, u32[]{:S(2)}) collective-permute-start(bf16[16,16,128]{2,1,0:T(8,128)(2,1)S(1)} %collective-permute-done.refs_0_), channel_id=1, source_target_pairs={{0,4},{1,17},{2,6},{3,19},{4,0},{5,21},{6,2},{7,23},{8,12},{9,25},... | collective-permute-start | bytes 196616 | tf_op jit(solution)/shard_map/ppermute | solution.py:263
  8.7 7.9 %collective-permute-start.3 = (bf16[512,128]{1,0:T(8,128)(2,1)S(1)}, bf16[512,128]{1,0:T(8,128)(2,1)S(1)}, u32[]{:S(2)}, u32[]{:S(2)}) collective-permute-start(bf16[512,128]{1,0:T(8,128)(2,1)S(1)} %unit_pieces.3), channel_id=1, source_target_pairs={{0,2},{1,9},{2,0},{3,11},{4,6},{5,13},{6,4},{7,15},{8,10},{9,1},{1... | collective-permute-start | bytes 393224 | tf_op jit(solution)/shard_map/ppermute | solution.py:263
  11.8 5.0 %collective-permute-start.4 = (bf16[512,128]{1,0:T(8,128)(2,1)S(1)}, bf16[512,128]{1,0:T(8,128)(2,1)S(1)}, u32[]{:S(2)}, u32[]{:S(2)}) collective-permute-start(bf16[512,128]{1,0:T(8,128)(2,1)S(1)} %unit_pieces.2), channel_id=1, source_target_pairs={{0,2},{1,9},{2,0},{3,11},{4,6},{5,13},{6,4},{7,15},{8,10},{9,1},{1... | collective-permute-start | bytes 393224 | tf_op jit(solution)/shard_map/ppermute | solution.py:263
  13.1 6.2 %collective-permute-start.7 = (bf16[1024,128]{1,0:T(8,128)(2,1)S(1)}, bf16[1024,128]{1,0:T(8,128)(2,1)S(1)}, u32[]{:S(2)}, u32[]{:S(2)}) collective-permute-start(bf16[1024,128]{1,0:T(8,128)(2,1)S(1)} %pad_maximum_fusion.refs_0_), channel_id=1, source_target_pairs={{0,1},{1,0},{2,3},{3,2},{4,5},{5,4},{6,7},{7,6},{8,9},{9,8},{10,11... | collective-permute-start | bytes 786440 | tf_op jit(solution)/shard_map/ppermute | solution.py:263
  16.8 5.2 %collective-permute-start.8 = (bf16[1024,128]{1,0:T(8,128)(2,1)S(1)}, bf16[1024,128]{1,0:T(8,128)(2,1)S(1)}, u32[]{:S(2)}, u32[]{:S(2)}) collective-permute-start(bf16[1024,128]{1,0:T(8,128)(2,1)S(1)} %constant_dynamic-update-slice_fusion.refs_1_), channel_id=1, source_target_pairs={{0,1},{1,0},{2,3},{3,2},{4,5},{5,4},{6,7},{7,6},{8,9},{9,8},{10,11... | collective-permute-start | bytes 786440 | tf_op jit(solution)/shard_map/ppermute | solution.py:263
  17.3 6.4 %collective-permute-start.6 = (bf16[1024,128]{1,0:T(8,128)(2,1)S(1)}, bf16[1024,128]{1,0:T(8,128)(2,1)S(1)}, u32[]{:S(2)}, u32[]{:S(2)}) collective-permute-start(bf16[1024,128]{1,0:T(8,128)(2,1)S(1)} %constant_dynamic-update-slice_fusion.refs_1_), channel_id=1, source_target_pairs={{0,16},{1,5},{2,18},{3,7},{4,20},{5,1},{6,22},{7,3},{8,24},{9,13},... | collective-permute-start | bytes 786440 | tf_op jit(solution)/shard_map/ppermute | solution.py:263
  18.6 8.0 %collective-permute-start.5 = (bf16[1024,128]{1,0:T(8,128)(2,1)S(1)}, bf16[1024,128]{1,0:T(8,128)(2,1)S(1)}, u32[]{:S(2)}, u32[]{:S(2)}) collective-permute-start(bf16[1024,128]{1,0:T(8,128)(2,1)S(1)} %pad_maximum_fusion.refs_0_), channel_id=1, source_target_pairs={{0,16},{1,5},{2,18},{3,7},{4,20},{5,1},{6,22},{7,3},{8,24},{9,13},... | collective-permute-start | bytes 786440 | tf_op jit(solution)/shard_map/ppermute | solution.py:263
  23.6 1.5 %collective-permute-start.9 = (bf16[1024,128]{1,0:T(8,128)(2,1)S(1)}, bf16[1024,128]{1,0:T(8,128)(2,1)S(1)}, u32[]{:S(2)}, u32[]{:S(2)}) collective-permute-start(bf16[1024,128]{1,0:T(8,128)(2,1)S(1)} %collective-permute-done.6.refs_1_), channel_id=1, source_target_pairs={{0,1},{1,0},{2,3},{3,2},{4,5},{5,4},{6,7},{7,6},{8,9},{9,8},{10,11... | collective-permute-start | bytes 786440 | tf_op jit(solution)/shard_map/ppermute | solution.py:263
  26.5 1.7 %collective-permute-start.10 = (bf16[1024,128]{1,0:T(8,128)(2,1)S(1)}, bf16[1024,128]{1,0:T(8,128)(2,1)S(1)}, u32[]{:S(2)}, u32[]{:S(2)}) collective-permute-start(bf16[1024,128]{1,0:T(8,128)(2,1)S(1)} %collective-permute-done.5.refs_1_), channel_id=1, source_target_pairs={{0,1},{1,0},{2,3},{3,2},{4,5},{5,4},{6,7},{7,6},{8,9},{9,8},{10,11... | collective-permute-start | bytes 786440 | tf_op jit(solution)/shard_map/ppermute | solution.py:263

commit v5 on v4

--- a/solution.py
+++ b/solution.py
@@ -14,8 +14,12 @@
 HALF = GROUP // 2
 PIECE = 256
 LANES = 128
+STEP = 24
+SIZES = (84, 100)
+BLOCK = 64
 ANY = pl.BlockSpec(memory_space=pl.ANY)
 VMEM = pl.BlockSpec(memory_space=pltpu.VMEM)
+SMEM = pl.BlockSpec(memory_space=pltpu.SMEM)
 
 
 def unit_rows(values):
@@ -34,27 +38,30 @@
 
 
 def layout_kernel(counts_any, inside, keep, last, lengths, counts, sem):
-    docs, groups = last.shape[0], keep.shape[0]
+    docs, groups = counts.shape[0], keep.shape[0]
     fetch = pltpu.make_async_copy(counts_any, counts, sem)
     fetch.start()
     fetch.wait()
     group = lax.broadcasted_iota(jnp.int32, keep.shape, 0)
-    document = lax.broadcasted_iota(jnp.int32, last.shape, 0)
+    document = lax.broadcasted_iota(jnp.int32, lengths.shape, 0)
     place = lax.broadcasted_iota(jnp.int32, (GROUP, LANES), 0)
     keeps = jnp.ones(keep.shape, jnp.float32)
-    lasts = jnp.zeros(last.shape, jnp.int32)
-    sizes = jnp.zeros(last.shape, jnp.float32)
+    sizes = jnp.zeros(lengths.shape, jnp.float32)
     first = jnp.int32(0)
     for d in range(docs):
         count = counts[d]
         full = count // GROUP
         inside[d * GROUP : (d + 1) * GROUP, :] = (place < count - full * GROUP).astype(jnp.float32)
         keeps = jnp.where(group == jnp.where(full > 0, first, groups), 0.0, keeps)
-        lasts = jnp.where(document == d, jnp.where(full > 0, first + full - 1, groups), lasts)
         sizes = jnp.where(document == d, count.astype(jnp.float32), sizes)
         first = first + full
     keep[...] = keeps
-    last[...] = lasts
+    first = jnp.int32(0)
+    for d in range(docs):
+        full = counts[d] // GROUP
+        last[d] = jnp.where(full > 0, first + full - 1, groups)
+        first = first + full
+    last[docs] = first
     lengths[...] = sizes
 
 
@@ -65,11 +72,11 @@
         out_shape=(
             jax.ShapeDtypeStruct((docs * GROUP, LANES), jnp.float32),
             jax.ShapeDtypeStruct((groups, LANES), jnp.float32),
-            jax.ShapeDtypeStruct((docs, LANES), jnp.int32),
+            pltpu.SMEM((docs + 1,), jnp.int32),
             jax.ShapeDtypeStruct((docs, LANES), jnp.float32),
         ),
         in_specs=[ANY],
-        out_specs=(VMEM,) * 4,
+        out_specs=(VMEM, VMEM, SMEM, VMEM),
         scratch_shapes=[pltpu.SMEM((docs,), jnp.int32), pltpu.SemaphoreType.DMA],
         compiler_params=params(4),
         cost_estimate=cost(20000),
@@ -98,12 +105,12 @@
         full = count // GROUP
 
         def move(k, carry, start=start, first=first):
-            block = vectors[pl.ds(start + k * GROUP, GROUP), :]
-            at = pl.multiple_of(tail + (first + k) * GROUP, GROUP)
-            rows_out[pl.ds(at, GROUP), :] = block.astype(jnp.bfloat16)
+            block = vectors[pl.ds(start + k * BLOCK, BLOCK), :]
+            at = pl.multiple_of(tail + first * GROUP + k * BLOCK, GROUP)
+            rows_out[pl.ds(at, BLOCK), :] = block.astype(jnp.bfloat16)
             return carry
 
-        lax.fori_loop(0, full, move, 0)
+        lax.fori_loop(0, (full * GROUP + BLOCK - 1) // BLOCK, move, 0)
         block = vectors[pl.ds(start + full * GROUP, GROUP), :]
         rows_out[d * GROUP : (d + 1) * GROUP, :] = block.astype(jnp.bfloat16)
         start = start + count
@@ -115,11 +122,11 @@
     width = w_proj.shape[1]
     return pl.pallas_call(
         docs_kernel,
-        out_shape=jax.ShapeDtypeStruct((docs * GROUP + rows, width), jnp.bfloat16),
+        out_shape=jax.ShapeDtypeStruct((docs * GROUP + rows + BLOCK, width), jnp.bfloat16),
         in_specs=[ANY, VMEM, VMEM],
         out_specs=VMEM,
         scratch_shapes=[
-            pltpu.VMEM((rows + GROUP, width), jnp.float32),
+            pltpu.VMEM((rows + BLOCK, width), jnp.float32),
             pltpu.SMEM((docs,), jnp.int32),
             pltpu.SemaphoreType.DMA,
         ],
@@ -151,7 +158,7 @@
 def mass_kernel(places, rows, inside, keep, last, *refs):
     *chunks, mass, sums, tail_sums = refs
     chunks = chunks[-len(places) :]
-    docs = last.shape[0]
+    docs = last.shape[0] - 1
     groups = keep.shape[0]
     tail = docs * GROUP
 
@@ -164,46 +171,55 @@
     def wide(row, width):
         return jnp.concatenate([row] * (width // LANES), axis=1)
 
-    step = 24 if groups % 24 == 0 else groups
-    ends = last[...]
+    used = last[docs]
     for c, chunk in enumerate(chunks):
-        tokens = chunk[...]
-        width = tokens.shape[0]
-        block = weights(rows[:tail, :], tokens)
-        for d in range(docs):
-            lo = d * GROUP
-            mid, hi = lo + HALF, lo + GROUP
-            tail_sums[c, d] = block[lo:mid] * wide(inside[lo:mid, :], width) + block[
-                mid:hi
-            ] * wide(inside[mid:hi, :], width)
-        total = jnp.zeros((HALF, width), jnp.float32)
-        sums[c, groups] = total
-        for base in range(0, groups, step):
-            block = weights(rows[tail + base * GROUP : tail + (base + step) * GROUP, :], tokens)
-            for j in range(step):
-                lo = j * GROUP
+        width = chunk.shape[0]
+        sums[c, groups] = jnp.zeros((HALF, width), jnp.float32)
+
+    def run(size):
+        for c, chunk in enumerate(chunks):
+            tokens = chunk[...]
+            width = tokens.shape[0]
+            block = weights(rows[:tail, :], tokens)
+            for d in range(docs):
+                lo = d * GROUP
                 mid, hi = lo + HALF, lo + GROUP
-                row = jnp.broadcast_to(keep[base + j : base + j + 1, :], (HALF, LANES))
-                total = total * wide(row, width) + (block[lo:mid] + block[mid:hi])
-                sums[c, base + j] = total
+                tail_sums[c, d] = block[lo:mid] * wide(inside[lo:mid, :], width) + block[
+                    mid:hi
+                ] * wide(inside[mid:hi, :], width)
+            total = jnp.zeros((HALF, width), jnp.float32)
+            for base in range(0, size, STEP):
+                step = min(STEP, size - base)
+                block = weights(rows[tail + base * GROUP : tail + (base + step) * GROUP, :], tokens)
+                for j in range(step):
+                    lo = j * GROUP
+                    mid, hi = lo + HALF, lo + GROUP
+                    row = jnp.broadcast_to(keep[base + j : base + j + 1, :], (HALF, LANES))
+                    total = total * wide(row, width) + (block[lo:mid] + block[mid:hi])
+                    sums[c, base + j] = total
+
+    sizes = [size for size in SIZES if size < groups] + [groups]
+    for below, size in zip([-1] + sizes, sizes):
+        pl.when((used > below) & (used <= size))(functools.partial(run, size))
     odd = lax.axis_index("loop") % 2
     for c, place in enumerate(places):
         at = [even if even == other else jnp.where(odd == 0, even, other) for even, other in place]
         for d in range(docs):
-            total = jnp.sum(sums[c, ends[d, 0]] + tail_sums[c, d], axis=0, keepdims=True)
+            total = jnp.sum(sums[c, last[d]] + tail_sums[c, d], axis=0, keepdims=True)
             for i, piece in enumerate(at):
                 mass[piece, d : d + 1, :] = total[:, i * PIECE : (i + 1) * PIECE]
 
 
 def add_masses(documents, mass, chunks, places, pieces):
     rows, inside, keep, last, _ = documents
-    docs, groups = last.shape[0], keep.shape[0]
+    docs, groups = last.shape[0] - 1, keep.shape[0]
+    last = pltpu.with_memory_space_constraint(last, pltpu.SMEM)
     count, width = len(chunks), chunks[0].shape[0]
     before = () if mass is None else (mass,)
     return pl.pallas_call(
         functools.partial(mass_kernel, places),
         out_shape=jax.ShapeDtypeStruct((pieces, docs, PIECE), jnp.float32),
-        in_specs=[VMEM] * (4 + len(before) + count),
+        in_specs=[VMEM, VMEM, VMEM, SMEM] + [VMEM] * (len(before) + count),
         out_specs=VMEM,
         input_output_aliases={4: 0} if before else {},
         scratch_shapes=[

time: 30.7 us -> 29.8 us (0.971)
  Pallas kernels: 14.8 us -> 12.4 us
  waiting for transfers between devices: 2.22 us -> 4.26 us
  starting transfers between devices: 13.3 us -> 12.8 us
    pallas_call x8, Pallas kernels: 10.7 us -> 8.56 us  [add_masses(): pl.pallas_call(functools.partial(mass_kernel, places), out_shape=jax.Shap...]
    ppermute x11, waiting for transfers between devices: 2.22 us -> 4.26 us  [swap(): return lax.ppermute(values, ('shard', 'loop'), pairs)]
    ppermute x11, starting transfers between devices: 13.3 us -> 12.8 us  [swap(): return lax.ppermute(values, ('shard', 'loop'), pairs)]
  transfers between devices with their start and end apart: 11 -> 11, of which waited for: 6 -> 8; matrix products, arithmetic and copies ran while one was open for 0% -> 0% of each run, Pallas kernels for 41% -> 35%
where the time goes in v5:
time: 29.8 us; the launch traced here: 29.7 us
  starting transfers between devices  12.8 us (43%)
  Pallas kernels  12.4 us (42%)
  waiting for transfers between devices  4.26 us (14%)
    ppermute x11, starting transfers between devices, swap(): return lax.ppermute(values, ('shard', 'loop'), pairs)  12.8 us
    pallas_call x8, Pallas kernels, add_masses(): pl.pallas_call(functools.partial(mass_kernel, places), out_shape=jax.Shap...  8.56 us
    ppermute x11, waiting for transfers between devices, swap(): return lax.ppermute(values, ('shard', 'loop'), pairs)  4.26 us
    pallas_call x1, Pallas kernels, regroup_documents(): pl.pallas_call(docs_kernel, out_shape=jax.ShapeDtypeStruct((docs * GROUP...  1.73 us
    pallas_call x1, Pallas kernels, score(): pl.pallas_call(functools.partial(score_kernel, parts, tokens, relative),...  0.94 us
    pallas_call x1, Pallas kernels, document_layout(): pl.pallas_call(layout_kernel, out_shape=(jax.ShapeDtypeStruct((docs * GRO...  0.88 us
  transfers between devices with their start and end apart: 11, of which 8 were waited for; matrix products, arithmetic and copies ran while one was open for 0% of the time, Pallas kernels for 35%

profile of v5, /device:TPU:0, one launch (start us, length us, event | category | flops | bytes accessed | tf_op | source)
XLA Modules:
  0.0 29.7 jit_solution(4182778275705169650)
XLA Ops:
  0.0 4.0 %collective-permute-start = (bf16[16,16,128]{2,1,0:T(8,128)(2,1)}, bf16[16,16,128]{2,1,0:T(8,128)(2,1)S(1)}, u32[]{:S(2)}, u32[]{:S(2)}) collective-permute-start(bf16[16,16,128]{2,1,0:T(8,128)(2,1)} %refs_0_.1), channel_id=1, source_target_pairs={{0,8},{1,3},{2,10},{3,1},{4,12},{5,7},{6,14},{7,5},{8,0},{9,11},{1... | collective-permute-start | bytes 196616 | tf_op jit(solution)/shard_map/ppermute | solution.py:279
  4.0 1.6 %collective-permute-start.2 = (bf16[16,16,128]{2,1,0:T(8,128)(2,1)}, bf16[16,16,128]{2,1,0:T(8,128)(2,1)S(1)}, u32[]{:S(2)}, u32[]{:S(2)}) collective-permute-start(bf16[16,16,128]{2,1,0:T(8,128)(2,1)} %refs_0_.1), channel_id=1, source_target_pairs={{0,4},{1,17},{2,6},{3,19},{4,0},{5,21},{6,2},{7,23},{8,12},{9,25},... | collective-permute-start | bytes 196616 | tf_op jit(solution)/shard_map/ppermute | solution.py:279
  5.6 0.9 %layout.1 = (f32[128,128]{1,0:T(8,128)S(1)}, f32[120,128]{1,0:T(8,128)S(1)}, s32[9]{0:T(128)S(4)}, f32[8,128]{1,0:T(8,128)S(1)}) custom-call(s32[8]{0:T(128)} %counts_any.3), custom_call_target="tpu_custom_call" | custom-call | flops 20000000000 | tf_op jit(solution)/shard_map/layout/pallas_call | solution.py:70
  6.5 0.1 collective-permute-done.refs_0_
  6.6 1.8 %collective-permute-start.1 = (bf16[16,16,128]{2,1,0:T(8,128)(2,1)S(1)}, bf16[16,16,128]{2,1,0:T(8,128)(2,1)S(1)}, u32[]{:S(2)}, u32[]{:S(2)}) collective-permute-start(bf16[16,16,128]{2,1,0:T(8,128)(2,1)S(1)} %collective-permute-done.refs_0_), channel_id=1, source_target_pairs={{0,4},{1,17},{2,6},{3,19},{4,0},{5,21},{6,2},{7,23},{8,12},{9,25},... | collective-permute-start | bytes 196616 | tf_op jit(solution)/shard_map/ppermute | solution.py:279
  8.4 0.1 collective-permute-done.2.refs_1_
  8.5 0.1 unit_pieces.3
  8.7 1.6 %collective-permute-start.3 = (bf16[512,128]{1,0:T(8,128)(2,1)S(1)}, bf16[512,128]{1,0:T(8,128)(2,1)S(1)}, u32[]{:S(2)}, u32[]{:S(2)}) collective-permute-start(bf16[512,128]{1,0:T(8,128)(2,1)S(1)} %unit_pieces.3), channel_id=1, source_target_pairs={{0,2},{1,9},{2,0},{3,11},{4,6},{5,13},{6,4},{7,15},{8,10},{9,1},{1... | collective-permute-start | bytes 393224 | tf_op jit(solution)/shard_map/ppermute | solution.py:279
  10.2 1.4 %collective-permute-done.1.refs_1_ = bf16[16,16,128]{2,1,0:T(8,128)(2,1)S(1)} collective-permute-done((bf16[16,16,128]{2,1,0:T(8,128)(2,1)S(1)}, bf16[16,16,128]{2,1,0:T(8,128)(2,1)S(1)}, u32[]{:S(2)}, u32[]{:S(2)}) %collective-permute-start.1) | collective-permute-done | bytes 65568 | tf_op jit(solution)/shard_map/ppermute | solution.py:279
  11.6 0.1 unit_pieces.2
  11.8 1.3 %collective-permute-start.4 = (bf16[512,128]{1,0:T(8,128)(2,1)S(1)}, bf16[512,128]{1,0:T(8,128)(2,1)S(1)}, u32[]{:S(2)}, u32[]{:S(2)}) collective-permute-start(bf16[512,128]{1,0:T(8,128)(2,1)S(1)} %unit_pieces.2), channel_id=1, source_target_pairs={{0,2},{1,9},{2,0},{3,11},{4,6},{5,13},{6,4},{7,15},{8,10},{9,1},{1... | collective-permute-start | bytes 393224 | tf_op jit(solution)/shard_map/ppermute | solution.py:279
  13.1 0.1 collective-permute-start.7
  13.2 1.7 %documents.1.rows = bf16[2112,128]{1,0:T(8,128)(2,1)S(1)} custom-call(s32[8]{0:T(128)} %counts_any.3, bf16[1920,768]{1,0:T(8,128)(2,1)S(1)} %copy-done, bf16[768,128]{1,0:T(8,128)(2,1)S(1)} %copy-done.1), custom_call_target="tpu_custom_call" | custom-call | flops 2500000 | tf_op jit(solution)/shard_map/documents/pallas_call | solution.py:123
  15.0 1.0 %masses.8.refs_0_ = f32[32,8,256]{2,1,0:T(8,128)S(1)} custom-call(bf16[2112,128]{1,0:T(8,128)(2,1)S(1)} %documents.1.rows, f32[128,128]{1,0:T(8,128)S(1)} %get-tuple-element.30.inside, f32[120,128]{1,0:T(8,128)S(1)} %get-tuple-element.31.keep, s32[9]{0:T(128)S(4)} %get-tuple-element.32.last, bf16[1024,128]{1,0:T(8,128)(2,1)S(1)} %pad_maximum_fusion.refs_0_), custom_call_target="tpu_custom_call" | custom-call | flops 20000000000 | tf_op jit(solution)/shard_map/masses/pallas_call | solution.py:219
  16.0 0.8 %collective-permute-done.4 = bf16[512,128]{1,0:T(8,128)(2,1)S(1)} collective-permute-done((bf16[512,128]{1,0:T(8,128)(2,1)S(1)}, bf16[512,128]{1,0:T(8,128)(2,1)S(1)}, u32[]{:S(2)}, u32[]{:S(2)}) %collective-permute-start.4) | collective-permute-done | bytes 131104 | tf_op jit(solution)/shard_map/ppermute | solution.py:279
  16.8 0.1 collective-permute-start.8
  16.9 1.6 %collective-permute-start.6 = (bf16[1024,128]{1,0:T(8,128)(2,1)S(1)}, bf16[1024,128]{1,0:T(8,128)(2,1)S(1)}, u32[]{:S(2)}, u32[]{:S(2)}) collective-permute-start(bf16[1024,128]{1,0:T(8,128)(2,1)S(1)} %constant_dynamic-update-slice_fusion.refs_1_), channel_id=1, source_target_pairs={{0,16},{1,5},{2,18},{3,7},{4,20},{5,1},{6,22},{7,3},{8,24},{9,13},... | collective-permute-start | bytes 786440 | tf_op jit(solution)/shard_map/ppermute | solution.py:279
  18.5 0.5 %collective-permute-start.5 = (bf16[1024,128]{1,0:T(8,128)(2,1)S(1)}, bf16[1024,128]{1,0:T(8,128)(2,1)S(1)}, u32[]{:S(2)}, u32[]{:S(2)}) collective-permute-start(bf16[1024,128]{1,0:T(8,128)(2,1)S(1)} %pad_maximum_fusion.refs_0_), channel_id=1, source_target_pairs={{0,16},{1,5},{2,18},{3,7},{4,20},{5,1},{6,22},{7,3},{8,24},{9,13},... | collective-permute-start | bytes 786440 | tf_op jit(solution)/shard_map/ppermute | solution.py:279
  19.0 0.0 collective-permute-done.7.refs_1_
  19.0 1.0 %masses.9.refs_0_ = f32[32,8,256]{2,1,0:T(8,128)S(1)} custom-call(bf16[2112,128]{1,0:T(8,128)(2,1)S(1)} %documents.1.rows, f32[128,128]{1,0:T(8,128)S(1)} %get-tuple-element.30.inside, f32[120,128]{1,0:T(8,128)S(1)} %get-tuple-element.31.keep, s32[9]{0:T(128)S(4)} %get-tuple-element.32.last, ...), custom_call_target="tpu_custom_call", output_to_operand_aliasing={{}: (4, {})} | custom-call | flops 20000000000 | tf_op jit(solution)/shard_map/masses/pallas_call | solution.py:219
  20.1 1.2 %masses.10.refs_0_ = f32[32,8,256]{2,1,0:T(8,128)S(1)} custom-call(bf16[2112,128]{1,0:T(8,128)(2,1)S(1)} %documents.1.rows, f32[128,128]{1,0:T(8,128)S(1)} %get-tuple-element.30.inside, f32[120,128]{1,0:T(8,128)S(1)} %get-tuple-element.31.keep, s32[9]{0:T(128)S(4)} %get-tuple-element.32.last, ...), custom_call_target="tpu_custom_call", output_to_operand_aliasing={{}: (4, {})} | custom-call | flops 20000000000 | tf_op jit(solution)/shard_map/masses/pallas_call | solution.py:219
  21.3 1.1 %masses.11.refs_0_ = f32[32,8,256]{2,1,0:T(8,128)S(1)} custom-call(bf16[2112,128]{1,0:T(8,128)(2,1)S(1)} %documents.1.rows, f32[128,128]{1,0:T(8,128)S(1)} %get-tuple-element.30.inside, f32[120,128]{1,0:T(8,128)S(1)} %get-tuple-element.31.keep, s32[9]{0:T(128)S(4)} %get-tuple-element.32.last, ...), custom_call_target="tpu_custom_call", output_to_operand_aliasing={{}: (4, {})} | custom-call | flops 20000000000 | tf_op jit(solution)/shard_map/masses/pallas_call | solution.py:219
  22.4 1.0 %collective-permute-done.6.refs_1_ = bf16[1024,128]{1,0:T(8,128)(2,1)S(1)} collective-permute-done((bf16[1024,128]{1,0:T(8,128)(2,1)S(1)}, bf16[1024,128]{1,0:T(8,128)(2,1)S(1)}, u32[]{:S(2)}, u32[]{:S(2)}) %collective-permute-start.6) | collective-permute-done | bytes 262176 | tf_op jit(solution)/shard_map/ppermute | solution.py:279
  23.4 1.0 %masses.12.refs_0_ = f32[32,8,256]{2,1,0:T(8,128)S(1)} custom-call(bf16[2112,128]{1,0:T(8,128)(2,1)S(1)} %documents.1.rows, f32[128,128]{1,0:T(8,128)S(1)} %get-tuple-element.30.inside, f32[120,128]{1,0:T(8,128)S(1)} %get-tuple-element.31.keep, s32[9]{0:T(128)S(4)} %get-tuple-element.32.last, ...), custom_call_target="tpu_custom_call", output_to_operand_aliasing={{}: (4, {})} | custom-call | flops 20000000000 | tf_op jit(solution)/shard_map/masses/pallas_call | solution.py:219
  24.4 0.5 %collective-permute-done.9.refs_1_ = bf16[1024,128]{1,0:T(8,128)(2,1)S(1)} collective-permute-done((bf16[1024,128]{1,0:T(8,128)(2,1)S(1)}, bf16[1024,128]{1,0:T(8,128)(2,1)S(1)}, u32[]{:S(2)}, u32[]{:S(2)}) %collective-permute-start.9) | collective-permute-done | bytes 262176 | tf_op jit(solution)/shard_map/ppermute | solution.py:279
  24.9 1.0 %masses.13.refs_0_ = f32[32,8,256]{2,1,0:T(8,128)S(1)} custom-call(bf16[2112,128]{1,0:T(8,128)(2,1)S(1)} %documents.1.rows, f32[128,128]{1,0:T(8,128)S(1)} %get-tuple-element.30.inside, f32[120,128]{1,0:T(8,128)S(1)} %get-tuple-element.31.keep, s32[9]{0:T(128)S(4)} %get-tuple-element.32.last, ...), custom_call_target="tpu_custom_call", output_to_operand_aliasing={{}: (4, {})} | custom-call | flops 20000000000 | tf_op jit(solution)/shard_map/masses/pallas_call | solution.py:219
  25.9 0.2 collective-permute-done.5.refs_1_
  26.2 0.2 collective-permute-start.10
  26.4 1.0 %masses.14.refs_0_ = f32[32,8,256]{2,1,0:T(8,128)S(1)} custom-call(bf16[2112,128]{1,0:T(8,128)(2,1)S(1)} %documents.1.rows, f32[128,128]{1,0:T(8,128)S(1)} %get-tuple-element.30.inside, f32[120,128]{1,0:T(8,128)S(1)} %get-tuple-element.31.keep, s32[9]{0:T(128)S(4)} %get-tuple-element.32.last, ...), custom_call_target="tpu_custom_call", output_to_operand_aliasing={{}: (4, {})} | custom-call | flops 20000000000 | tf_op jit(solution)/shard_map/masses/pallas_call | solution.py:219
  27.4 0.3 collective-permute-done.10.refs_1_
  27.7 1.0 %masses.15.mass = f32[32,8,256]{2,1,0:T(8,128)S(1)} custom-call(bf16[2112,128]{1,0:T(8,128)(2,1)S(1)} %documents.1.rows, f32[128,128]{1,0:T(8,128)S(1)} %get-tuple-element.30.inside, f32[120,128]{1,0:T(8,128)S(1)} %get-tuple-element.31.keep, s32[9]{0:T(128)S(4)} %get-tuple-element.32.last, ...), custom_call_target="tpu_custom_call", output_to_operand_aliasing={{}: (4, {})} | custom-call | flops 20000000000 | tf_op jit(solution)/shard_map/masses/pallas_call | solution.py:219
  28.7 0.9 %scores.1 = f32[8,256]{1,0:T(8,128)} custom-call(f32[8,128]{1,0:T(8,128)S(1)} %get-tuple-element.27.lengths, f32[32,8,256]{2,1,0:T(8,128)S(1)} %masses.15.mass), custom_call_target="tpu_custom_call" | custom-call | flops 1000000 | tf_op jit(solution)/shard_map/scores/pallas_call | solution.py:265
  (12 shorter events, 0.1 us)
Async XLA Ops:
  0.0 8.5 %copy-start.2 = (bf16[16,16,128]{2,1,0:T(8,128)(2,1)S(1)}, bf16[16,16,128]{2,1,0:T(8,128)(2,1)}, u32[]{:S(2)}) copy-start(bf16[16,16,128]{2,1,0:T(8,128)(2,1)} %refs_0_.1) | copy-start | bytes 196612
  0.0 13.2 %copy-start.1 = (bf16[768,128]{1,0:T(8,128)(2,1)S(1)}, bf16[768,128]{1,0:T(8,128)(2,1)}, u32[]{:S(2)}) copy-start(bf16[768,128]{1,0:T(8,128)(2,1)} %w_proj.1) | copy-start | bytes 589828
  0.0 6.6 %collective-permute-start = (bf16[16,16,128]{2,1,0:T(8,128)(2,1)}, bf16[16,16,128]{2,1,0:T(8,128)(2,1)S(1)}, u32[]{:S(2)}, u32[]{:S(2)}) collective-permute-start(bf16[16,16,128]{2,1,0:T(8,128)(2,1)} %refs_0_.1), channel_id=1, source_target_pairs={{0,8},{1,3},{2,10},{3,1},{4,12},{5,7},{6,14},{7,5},{8,0},{9,11},{1... | collective-permute-start | bytes 196616 | tf_op jit(solution)/shard_map/ppermute | solution.py:279
  4.0 4.5 %collective-permute-start.2 = (bf16[16,16,128]{2,1,0:T(8,128)(2,1)}, bf16[16,16,128]{2,1,0:T(8,128)(2,1)S(1)}, u32[]{:S(2)}, u32[]{:S(2)}) collective-permute-start(bf16[16,16,128]{2,1,0:T(8,128)(2,1)} %refs_0_.1), channel_id=1, source_target_pairs={{0,4},{1,17},{2,6},{3,19},{4,0},{5,21},{6,2},{7,23},{8,12},{9,25},... | collective-permute-start | bytes 196616 | tf_op jit(solution)/shard_map/ppermute | solution.py:279
  5.6 7.6 %copy-start = (bf16[1920,768]{1,0:T(8,128)(2,1)S(1)}, bf16[1920,768]{1,0:T(8,128)(2,1)}, u32[]{:S(2)}) copy-start(bf16[1920,768]{1,0:T(8,128)(2,1)} %hidden) | copy-start | bytes 8847364
  6.6 5.0 %collective-permute-start.1 = (bf16[16,16,128]{2,1,0:T(8,128)(2,1)S(1)}, bf16[16,16,128]{2,1,0:T(8,128)(2,1)S(1)}, u32[]{:S(2)}, u32[]{:S(2)}) collective-permute-start(bf16[16,16,128]{2,1,0:T(8,128)(2,1)S(1)} %collective-permute-done.refs_0_), channel_id=1, source_target_pairs={{0,4},{1,17},{2,6},{3,19},{4,0},{5,21},{6,2},{7,23},{8,12},{9,25},... | collective-permute-start | bytes 196616 | tf_op jit(solution)/shard_map/ppermute | solution.py:279
  8.7 7.3 %collective-permute-start.3 = (bf16[512,128]{1,0:T(8,128)(2,1)S(1)}, bf16[512,128]{1,0:T(8,128)(2,1)S(1)}, u32[]{:S(2)}, u32[]{:S(2)}) collective-permute-start(bf16[512,128]{1,0:T(8,128)(2,1)S(1)} %unit_pieces.3), channel_id=1, source_target_pairs={{0,2},{1,9},{2,0},{3,11},{4,6},{5,13},{6,4},{7,15},{8,10},{9,1},{1... | collective-permute-start | bytes 393224 | tf_op jit(solution)/shard_map/ppermute | solution.py:279
  11.8 5.0 %collective-permute-start.4 = (bf16[512,128]{1,0:T(8,128)(2,1)S(1)}, bf16[512,128]{1,0:T(8,128)(2,1)S(1)}, u32[]{:S(2)}, u32[]{:S(2)}) collective-permute-start(bf16[512,128]{1,0:T(8,128)(2,1)S(1)} %unit_pieces.2), channel_id=1, source_target_pairs={{0,2},{1,9},{2,0},{3,11},{4,6},{5,13},{6,4},{7,15},{8,10},{9,1},{1... | collective-permute-start | bytes 393224 | tf_op jit(solution)/shard_map/ppermute | solution.py:279
  13.1 5.9 %collective-permute-start.7 = (bf16[1024,128]{1,0:T(8,128)(2,1)S(1)}, bf16[1024,128]{1,0:T(8,128)(2,1)S(1)}, u32[]{:S(2)}, u32[]{:S(2)}) collective-permute-start(bf16[1024,128]{1,0:T(8,128)(2,1)S(1)} %pad_maximum_fusion.refs_0_), channel_id=1, source_target_pairs={{0,1},{1,0},{2,3},{3,2},{4,5},{5,4},{6,7},{7,6},{8,9},{9,8},{10,11... | collective-permute-start | bytes 786440 | tf_op jit(solution)/shard_map/ppermute | solution.py:279
  16.8 4.5 %collective-permute-start.8 = (bf16[1024,128]{1,0:T(8,128)(2,1)S(1)}, bf16[1024,128]{1,0:T(8,128)(2,1)S(1)}, u32[]{:S(2)}, u32[]{:S(2)}) collective-permute-start(bf16[1024,128]{1,0:T(8,128)(2,1)S(1)} %constant_dynamic-update-slice_fusion.refs_1_), channel_id=1, source_target_pairs={{0,1},{1,0},{2,3},{3,2},{4,5},{5,4},{6,7},{7,6},{8,9},{9,8},{10,11... | collective-permute-start | bytes 786440 | tf_op jit(solution)/shard_map/ppermute | solution.py:279
  16.9 6.4 %collective-permute-start.6 = (bf16[1024,128]{1,0:T(8,128)(2,1)S(1)}, bf16[1024,128]{1,0:T(8,128)(2,1)S(1)}, u32[]{:S(2)}, u32[]{:S(2)}) collective-permute-start(bf16[1024,128]{1,0:T(8,128)(2,1)S(1)} %constant_dynamic-update-slice_fusion.refs_1_), channel_id=1, source_target_pairs={{0,16},{1,5},{2,18},{3,7},{4,20},{5,1},{6,22},{7,3},{8,24},{9,13},... | collective-permute-start | bytes 786440 | tf_op jit(solution)/shard_map/ppermute | solution.py:279
  18.5 7.7 %collective-permute-start.5 = (bf16[1024,128]{1,0:T(8,128)(2,1)S(1)}, bf16[1024,128]{1,0:T(8,128)(2,1)S(1)}, u32[]{:S(2)}, u32[]{:S(2)}) collective-permute-start(bf16[1024,128]{1,0:T(8,128)(2,1)S(1)} %pad_maximum_fusion.refs_0_), channel_id=1, source_target_pairs={{0,16},{1,5},{2,18},{3,7},{4,20},{5,1},{6,22},{7,3},{8,24},{9,13},... | collective-permute-start | bytes 786440 | tf_op jit(solution)/shard_map/ppermute | solution.py:279
  23.3 1.5 %collective-permute-start.9 = (bf16[1024,128]{1,0:T(8,128)(2,1)S(1)}, bf16[1024,128]{1,0:T(8,128)(2,1)S(1)}, u32[]{:S(2)}, u32[]{:S(2)}) collective-permute-start(bf16[1024,128]{1,0:T(8,128)(2,1)S(1)} %collective-permute-done.6.refs_1_), channel_id=1, source_target_pairs={{0,1},{1,0},{2,3},{3,2},{4,5},{5,4},{6,7},{7,6},{8,9},{9,8},{10,11... | collective-permute-start | bytes 786440 | tf_op jit(solution)/shard_map/ppermute | solution.py:279
  26.2 1.5 %collective-permute-start.10 = (bf16[1024,128]{1,0:T(8,128)(2,1)S(1)}, bf16[1024,128]{1,0:T(8,128)(2,1)S(1)}, u32[]{:S(2)}, u32[]{:S(2)}) collective-permute-start(bf16[1024,128]{1,0:T(8,128)(2,1)S(1)} %collective-permute-done.5.refs_1_), channel_id=1, source_target_pairs={{0,1},{1,0},{2,3},{3,2},{4,5},{5,4},{6,7},{7,6},{8,9},{9,8},{10,11... | collective-permute-start | bytes 786440 | tf_op jit(solution)/shard_map/ppermute | solution.py:279

commit v6 on v5

--- a/solution.py
+++ b/solution.py
@@ -315,8 +315,9 @@
     first = jnp.concatenate([first_near, first_away], axis=0)
     third = swap(first, y, z)
     second = swap(own, y, z)
+    mass = add(mass, own_core, (0, 0), True)
+    first, mass = after((first, mass))
     first_core = swap(first, core)
-    mass = add(mass, own_core, (0, 0), True)
     mass = add(mass, first, (x, far), False)
     mass = add(mass, first_core, (x, far), True)
     third, mass = after((third, mass))

time: 29.8 us -> 29.8 us (level)
  transfers between devices with their start and end apart: 11 -> 11, of which waited for: 8 -> 9; matrix products, arithmetic and copies ran while one was open for 0% -> 0% of each run, Pallas kernels for 35% -> 36%
where the time goes in v6:
time: 29.8 us; the launch traced here: 29.6 us
  starting transfers between devices  12.6 us (42%)
  Pallas kernels  12.5 us (42%)
  waiting for transfers between devices  4.3 us (14%)
    ppermute x11, starting transfers between devices, swap(): return lax.ppermute(values, ('shard', 'loop'), pairs)  12.6 us
    pallas_call x8, Pallas kernels, add_masses(): pl.pallas_call(functools.partial(mass_kernel, places), out_shape=jax.Shap...  8.66 us
    ppermute x11, waiting for transfers between devices, swap(): return lax.ppermute(values, ('shard', 'loop'), pairs)  4.3 us
    pallas_call x1, Pallas kernels, regroup_documents(): pl.pallas_call(docs_kernel, out_shape=jax.ShapeDtypeStruct((docs * GROUP...  1.73 us
    pallas_call x1, Pallas kernels, score(): pl.pallas_call(functools.partial(score_kernel, parts, tokens, relative),...  0.94 us
    pallas_call x1, Pallas kernels, document_layout(): pl.pallas_call(layout_kernel, out_shape=(jax.ShapeDtypeStruct((docs * GRO...  0.88 us
  transfers between devices with their start and end apart: 11, of which 9 were waited for; matrix products, arithmetic and copies ran while one was open for 0% of the time, Pallas kernels for 36%

profile of v6, /device:TPU:0, one launch (start us, length us, event | category | flops | bytes accessed | tf_op | source)
XLA Modules:
  0.0 29.6 jit_solution(8762345953191489543)
XLA Ops:
  0.0 4.0 %collective-permute-start = (bf16[16,16,128]{2,1,0:T(8,128)(2,1)}, bf16[16,16,128]{2,1,0:T(8,128)(2,1)S(1)}, u32[]{:S(2)}, u32[]{:S(2)}) collective-permute-start(bf16[16,16,128]{2,1,0:T(8,128)(2,1)} %refs_0_.1), channel_id=1, source_target_pairs={{0,8},{1,3},{2,10},{3,1},{4,12},{5,7},{6,14},{7,5},{8,0},{9,11},{1... | collective-permute-start | bytes 196616 | tf_op jit(solution)/shard_map/ppermute | solution.py:279
  4.0 1.6 %collective-permute-start.2 = (bf16[16,16,128]{2,1,0:T(8,128)(2,1)}, bf16[16,16,128]{2,1,0:T(8,128)(2,1)S(1)}, u32[]{:S(2)}, u32[]{:S(2)}) collective-permute-start(bf16[16,16,128]{2,1,0:T(8,128)(2,1)} %refs_0_.1), channel_id=1, source_target_pairs={{0,4},{1,17},{2,6},{3,19},{4,0},{5,21},{6,2},{7,23},{8,12},{9,25},... | collective-permute-start | bytes 196616 | tf_op jit(solution)/shard_map/ppermute | solution.py:279
  5.6 0.9 %layout.1 = (f32[128,128]{1,0:T(8,128)S(1)}, f32[120,128]{1,0:T(8,128)S(1)}, s32[9]{0:T(128)S(4)}, f32[8,128]{1,0:T(8,128)S(1)}) custom-call(s32[8]{0:T(128)} %counts_any.3), custom_call_target="tpu_custom_call" | custom-call | flops 20000000000 | tf_op jit(solution)/shard_map/layout/pallas_call | solution.py:70
  6.5 0.1 collective-permute-done.refs_0_
  6.6 1.8 %collective-permute-start.1 = (bf16[16,16,128]{2,1,0:T(8,128)(2,1)S(1)}, bf16[16,16,128]{2,1,0:T(8,128)(2,1)S(1)}, u32[]{:S(2)}, u32[]{:S(2)}) collective-permute-start(bf16[16,16,128]{2,1,0:T(8,128)(2,1)S(1)} %collective-permute-done.refs_0_), channel_id=1, source_target_pairs={{0,4},{1,17},{2,6},{3,19},{4,0},{5,21},{6,2},{7,23},{8,12},{9,25},... | collective-permute-start | bytes 196616 | tf_op jit(solution)/shard_map/ppermute | solution.py:279
  8.4 0.1 collective-permute-done.2.refs_1_
  8.5 0.1 unit_pieces.3
  8.7 1.6 %collective-permute-start.3 = (bf16[512,128]{1,0:T(8,128)(2,1)S(1)}, bf16[512,128]{1,0:T(8,128)(2,1)S(1)}, u32[]{:S(2)}, u32[]{:S(2)}) collective-permute-start(bf16[512,128]{1,0:T(8,128)(2,1)S(1)} %unit_pieces.3), channel_id=1, source_target_pairs={{0,2},{1,9},{2,0},{3,11},{4,6},{5,13},{6,4},{7,15},{8,10},{9,1},{1... | collective-permute-start | bytes 393224 | tf_op jit(solution)/shard_map/ppermute | solution.py:279
  10.2 1.4 %collective-permute-done.1.refs_1_ = bf16[16,16,128]{2,1,0:T(8,128)(2,1)S(1)} collective-permute-done((bf16[16,16,128]{2,1,0:T(8,128)(2,1)S(1)}, bf16[16,16,128]{2,1,0:T(8,128)(2,1)S(1)}, u32[]{:S(2)}, u32[]{:S(2)}) %collective-permute-start.1) | collective-permute-done | bytes 65568 | tf_op jit(solution)/shard_map/ppermute | solution.py:279
  11.6 0.1 unit_pieces.2
  11.8 1.3 %collective-permute-start.4 = (bf16[512,128]{1,0:T(8,128)(2,1)S(1)}, bf16[512,128]{1,0:T(8,128)(2,1)S(1)}, u32[]{:S(2)}, u32[]{:S(2)}) collective-permute-start(bf16[512,128]{1,0:T(8,128)(2,1)S(1)} %unit_pieces.2), channel_id=1, source_target_pairs={{0,2},{1,9},{2,0},{3,11},{4,6},{5,13},{6,4},{7,15},{8,10},{9,1},{1... | collective-permute-start | bytes 393224 | tf_op jit(solution)/shard_map/ppermute | solution.py:279
  13.1 0.1 collective-permute-start.7
  13.2 1.7 %documents.1.rows = bf16[2112,128]{1,0:T(8,128)(2,1)S(1)} custom-call(s32[8]{0:T(128)} %counts_any.3, bf16[1920,768]{1,0:T(8,128)(2,1)S(1)} %copy-done, bf16[768,128]{1,0:T(8,128)(2,1)S(1)} %copy-done.1), custom_call_target="tpu_custom_call" | custom-call | flops 2500000 | tf_op jit(solution)/shard_map/documents/pallas_call | solution.py:123
  15.0 1.1 %masses.8.refs_0_ = f32[32,8,256]{2,1,0:T(8,128)S(1)} custom-call(bf16[2112,128]{1,0:T(8,128)(2,1)S(1)} %documents.1.rows, f32[128,128]{1,0:T(8,128)S(1)} %get-tuple-element.32.inside, f32[120,128]{1,0:T(8,128)S(1)} %get-tuple-element.33.keep, s32[9]{0:T(128)S(4)} %get-tuple-element.34.last, bf16[1024,128]{1,0:T(8,128)(2,1)S(1)} %pad_maximum_fusion.refs_0_), custom_call_target="tpu_custom_call" | custom-call | flops 20000000000 | tf_op jit(solution)/shard_map/masses/pallas_call | solution.py:219
  16.0 0.0 collective-permute-done.3
  16.0 0.8 %collective-permute-done.4 = bf16[512,128]{1,0:T(8,128)(2,1)S(1)} collective-permute-done((bf16[512,128]{1,0:T(8,128)(2,1)S(1)}, bf16[512,128]{1,0:T(8,128)(2,1)S(1)}, u32[]{:S(2)}, u32[]{:S(2)}) %collective-permute-start.4) | collective-permute-done | bytes 131104 | tf_op jit(solution)/shard_map/ppermute | solution.py:279
  16.8 1.6 %collective-permute-start.6 = (bf16[1024,128]{1,0:T(8,128)(2,1)S(1)}, bf16[1024,128]{1,0:T(8,128)(2,1)S(1)}, u32[]{:S(2)}, u32[]{:S(2)}) collective-permute-start(bf16[1024,128]{1,0:T(8,128)(2,1)S(1)} %constant_dynamic-update-slice_fusion.refs_1_), channel_id=1, source_target_pairs={{0,16},{1,5},{2,18},{3,7},{4,20},{5,1},{6,22},{7,3},{8,24},{9,13},... | collective-permute-start | bytes 786440 | tf_op jit(solution)/shard_map/ppermute | solution.py:279
  18.4 0.5 %collective-permute-start.5 = (bf16[1024,128]{1,0:T(8,128)(2,1)S(1)}, bf16[1024,128]{1,0:T(8,128)(2,1)S(1)}, u32[]{:S(2)}, u32[]{:S(2)}) collective-permute-start(bf16[1024,128]{1,0:T(8,128)(2,1)S(1)} %pad_maximum_fusion.refs_0_), channel_id=1, source_target_pairs={{0,16},{1,5},{2,18},{3,7},{4,20},{5,1},{6,22},{7,3},{8,24},{9,13},... | collective-permute-start | bytes 786440 | tf_op jit(solution)/shard_map/ppermute | solution.py:279
  18.9 1.0 %masses.9.refs_0_ = f32[32,8,256]{2,1,0:T(8,128)S(1)} custom-call(bf16[2112,128]{1,0:T(8,128)(2,1)S(1)} %documents.1.rows, f32[128,128]{1,0:T(8,128)S(1)} %get-tuple-element.32.inside, f32[120,128]{1,0:T(8,128)S(1)} %get-tuple-element.33.keep, s32[9]{0:T(128)S(4)} %get-tuple-element.34.last, ...), custom_call_target="tpu_custom_call", output_to_operand_aliasing={{}: (4, {})} | custom-call | flops 20000000000 | tf_op jit(solution)/shard_map/masses/pallas_call | solution.py:219
  20.0 0.1 collective-permute-start.8
  20.1 1.2 %masses.10.refs_0_ = f32[32,8,256]{2,1,0:T(8,128)S(1)} custom-call(bf16[2112,128]{1,0:T(8,128)(2,1)S(1)} %documents.1.rows, f32[128,128]{1,0:T(8,128)S(1)} %get-tuple-element.32.inside, f32[120,128]{1,0:T(8,128)S(1)} %get-tuple-element.33.keep, s32[9]{0:T(128)S(4)} %get-tuple-element.34.last, ...), custom_call_target="tpu_custom_call", output_to_operand_aliasing={{}: (4, {})} | custom-call | flops 20000000000 | tf_op jit(solution)/shard_map/masses/pallas_call | solution.py:219
  21.3 0.3 collective-permute-done.8.refs_1_
  21.6 1.0 %masses.11.refs_0_ = f32[32,8,256]{2,1,0:T(8,128)S(1)} custom-call(bf16[2112,128]{1,0:T(8,128)(2,1)S(1)} %documents.1.rows, f32[128,128]{1,0:T(8,128)S(1)} %get-tuple-element.32.inside, f32[120,128]{1,0:T(8,128)S(1)} %get-tuple-element.33.keep, s32[9]{0:T(128)S(4)} %get-tuple-element.34.last, ...), custom_call_target="tpu_custom_call", output_to_operand_aliasing={{}: (4, {})} | custom-call | flops 20000000000 | tf_op jit(solution)/shard_map/masses/pallas_call | solution.py:219
  22.6 0.6 %collective-permute-done.6.refs_1_ = bf16[1024,128]{1,0:T(8,128)(2,1)S(1)} collective-permute-done((bf16[1024,128]{1,0:T(8,128)(2,1)S(1)}, bf16[1024,128]{1,0:T(8,128)(2,1)S(1)}, u32[]{:S(2)}, u32[]{:S(2)}) %collective-permute-start.6) | collective-permute-done | bytes 262176 | tf_op jit(solution)/shard_map/ppermute | solution.py:279
  23.3 1.0 %masses.12.refs_0_ = f32[32,8,256]{2,1,0:T(8,128)S(1)} custom-call(bf16[2112,128]{1,0:T(8,128)(2,1)S(1)} %documents.1.rows, f32[128,128]{1,0:T(8,128)S(1)} %get-tuple-element.32.inside, f32[120,128]{1,0:T(8,128)S(1)} %get-tuple-element.33.keep, s32[9]{0:T(128)S(4)} %get-tuple-element.34.last, ...), custom_call_target="tpu_custom_call", output_to_operand_aliasing={{}: (4, {})} | custom-call | flops 20000000000 | tf_op jit(solution)/shard_map/masses/pallas_call | solution.py:219
  24.3 0.5 %collective-permute-done.9.refs_1_ = bf16[1024,128]{1,0:T(8,128)(2,1)S(1)} collective-permute-done((bf16[1024,128]{1,0:T(8,128)(2,1)S(1)}, bf16[1024,128]{1,0:T(8,128)(2,1)S(1)}, u32[]{:S(2)}, u32[]{:S(2)}) %collective-permute-start.9) | collective-permute-done | bytes 262176 | tf_op jit(solution)/shard_map/ppermute | solution.py:279
  24.8 1.0 %masses.13.refs_0_ = f32[32,8,256]{2,1,0:T(8,128)S(1)} custom-call(bf16[2112,128]{1,0:T(8,128)(2,1)S(1)} %documents.1.rows, f32[128,128]{1,0:T(8,128)S(1)} %get-tuple-element.32.inside, f32[120,128]{1,0:T(8,128)S(1)} %get-tuple-element.33.keep, s32[9]{0:T(128)S(4)} %get-tuple-element.34.last, ...), custom_call_target="tpu_custom_call", output_to_operand_aliasing={{}: (4, {})} | custom-call | flops 20000000000 | tf_op jit(solution)/shard_map/masses/pallas_call | solution.py:219
  25.9 0.2 collective-permute-done.5.refs_1_
  26.1 1.2 %masses.14.refs_0_ = f32[32,8,256]{2,1,0:T(8,128)S(1)} custom-call(bf16[2112,128]{1,0:T(8,128)(2,1)S(1)} %documents.1.rows, f32[128,128]{1,0:T(8,128)S(1)} %get-tuple-element.32.inside, f32[120,128]{1,0:T(8,128)S(1)} %get-tuple-element.33.keep, s32[9]{0:T(128)S(4)} %get-tuple-element.34.last, ...), custom_call_target="tpu_custom_call", output_to_operand_aliasing={{}: (4, {})} | custom-call | flops 20000000000 | tf_op jit(solution)/shard_map/masses/pallas_call | solution.py:219
  27.3 0.4 %collective-permute-done.10.refs_1_ = bf16[1024,128]{1,0:T(8,128)(2,1)S(1)} collective-permute-done((bf16[1024,128]{1,0:T(8,128)(2,1)S(1)}, bf16[1024,128]{1,0:T(8,128)(2,1)S(1)}, u32[]{:S(2)}, u32[]{:S(2)}) %collective-permute-start.10) | collective-permute-done | bytes 262176 | tf_op jit(solution)/shard_map/ppermute | solution.py:279
  27.6 1.0 %masses.15.mass = f32[32,8,256]{2,1,0:T(8,128)S(1)} custom-call(bf16[2112,128]{1,0:T(8,128)(2,1)S(1)} %documents.1.rows, f32[128,128]{1,0:T(8,128)S(1)} %get-tuple-element.32.inside, f32[120,128]{1,0:T(8,128)S(1)} %get-tuple-element.33.keep, s32[9]{0:T(128)S(4)} %get-tuple-element.34.last, ...), custom_call_target="tpu_custom_call", output_to_operand_aliasing={{}: (4, {})} | custom-call | flops 20000000000 | tf_op jit(solution)/shard_map/masses/pallas_call | solution.py:219
  28.7 0.9 %scores.1 = f32[8,256]{1,0:T(8,128)} custom-call(f32[8,128]{1,0:T(8,128)S(1)} %get-tuple-element.29.lengths, f32[32,8,256]{2,1,0:T(8,128)S(1)} %masses.15.mass), custom_call_target="tpu_custom_call" | custom-call | flops 1000000 | tf_op jit(solution)/shard_map/scores/pallas_call | solution.py:265
  (12 shorter events, 0.1 us)
Async XLA Ops:
  0.0 8.5 %copy-start.2 = (bf16[16,16,128]{2,1,0:T(8,128)(2,1)S(1)}, bf16[16,16,128]{2,1,0:T(8,128)(2,1)}, u32[]{:S(2)}) copy-start(bf16[16,16,128]{2,1,0:T(8,128)(2,1)} %refs_0_.1) | copy-start | bytes 196612
  0.0 13.2 %copy-start.1 = (bf16[768,128]{1,0:T(8,128)(2,1)S(1)}, bf16[768,128]{1,0:T(8,128)(2,1)}, u32[]{:S(2)}) copy-start(bf16[768,128]{1,0:T(8,128)(2,1)} %w_proj.1) | copy-start | bytes 589828
  0.0 6.6 %collective-permute-start = (bf16[16,16,128]{2,1,0:T(8,128)(2,1)}, bf16[16,16,128]{2,1,0:T(8,128)(2,1)S(1)}, u32[]{:S(2)}, u32[]{:S(2)}) collective-permute-start(bf16[16,16,128]{2,1,0:T(8,128)(2,1)} %refs_0_.1), channel_id=1, source_target_pairs={{0,8},{1,3},{2,10},{3,1},{4,12},{5,7},{6,14},{7,5},{8,0},{9,11},{1... | collective-permute-start | bytes 196616 | tf_op jit(solution)/shard_map/ppermute | solution.py:279
  4.0 4.5 %collective-permute-start.2 = (bf16[16,16,128]{2,1,0:T(8,128)(2,1)}, bf16[16,16,128]{2,1,0:T(8,128)(2,1)S(1)}, u32[]{:S(2)}, u32[]{:S(2)}) collective-permute-start(bf16[16,16,128]{2,1,0:T(8,128)(2,1)} %refs_0_.1), channel_id=1, source_target_pairs={{0,4},{1,17},{2,6},{3,19},{4,0},{5,21},{6,2},{7,23},{8,12},{9,25},... | collective-permute-start | bytes 196616 | tf_op jit(solution)/shard_map/ppermute | solution.py:279
  5.6 7.6 %copy-start = (bf16[1920,768]{1,0:T(8,128)(2,1)S(1)}, bf16[1920,768]{1,0:T(8,128)(2,1)}, u32[]{:S(2)}) copy-start(bf16[1920,768]{1,0:T(8,128)(2,1)} %hidden) | copy-start | bytes 8847364
  6.6 5.0 %collective-permute-start.1 = (bf16[16,16,128]{2,1,0:T(8,128)(2,1)S(1)}, bf16[16,16,128]{2,1,0:T(8,128)(2,1)S(1)}, u32[]{:S(2)}, u32[]{:S(2)}) collective-permute-start(bf16[16,16,128]{2,1,0:T(8,128)(2,1)S(1)} %collective-permute-done.refs_0_), channel_id=1, source_target_pairs={{0,4},{1,17},{2,6},{3,19},{4,0},{5,21},{6,2},{7,23},{8,12},{9,25},... | collective-permute-start | bytes 196616 | tf_op jit(solution)/shard_map/ppermute | solution.py:279
  8.7 7.3 %collective-permute-start.3 = (bf16[512,128]{1,0:T(8,128)(2,1)S(1)}, bf16[512,128]{1,0:T(8,128)(2,1)S(1)}, u32[]{:S(2)}, u32[]{:S(2)}) collective-permute-start(bf16[512,128]{1,0:T(8,128)(2,1)S(1)} %unit_pieces.3), channel_id=1, source_target_pairs={{0,2},{1,9},{2,0},{3,11},{4,6},{5,13},{6,4},{7,15},{8,10},{9,1},{1... | collective-permute-start | bytes 393224 | tf_op jit(solution)/shard_map/ppermute | solution.py:279
  11.8 5.0 %collective-permute-start.4 = (bf16[512,128]{1,0:T(8,128)(2,1)S(1)}, bf16[512,128]{1,0:T(8,128)(2,1)S(1)}, u32[]{:S(2)}, u32[]{:S(2)}) collective-permute-start(bf16[512,128]{1,0:T(8,128)(2,1)S(1)} %unit_pieces.2), channel_id=1, source_target_pairs={{0,2},{1,9},{2,0},{3,11},{4,6},{5,13},{6,4},{7,15},{8,10},{9,1},{1... | collective-permute-start | bytes 393224 | tf_op jit(solution)/shard_map/ppermute | solution.py:279
  13.1 5.8 %collective-permute-start.7 = (bf16[1024,128]{1,0:T(8,128)(2,1)S(1)}, bf16[1024,128]{1,0:T(8,128)(2,1)S(1)}, u32[]{:S(2)}, u32[]{:S(2)}) collective-permute-start(bf16[1024,128]{1,0:T(8,128)(2,1)S(1)} %pad_maximum_fusion.refs_0_), channel_id=1, source_target_pairs={{0,1},{1,0},{2,3},{3,2},{4,5},{5,4},{6,7},{7,6},{8,9},{9,8},{10,11... | collective-permute-start | bytes 786440 | tf_op jit(solution)/shard_map/ppermute | solution.py:279
  16.8 6.4 %collective-permute-start.6 = (bf16[1024,128]{1,0:T(8,128)(2,1)S(1)}, bf16[1024,128]{1,0:T(8,128)(2,1)S(1)}, u32[]{:S(2)}, u32[]{:S(2)}) collective-permute-start(bf16[1024,128]{1,0:T(8,128)(2,1)S(1)} %constant_dynamic-update-slice_fusion.refs_1_), channel_id=1, source_target_pairs={{0,16},{1,5},{2,18},{3,7},{4,20},{5,1},{6,22},{7,3},{8,24},{9,13},... | collective-permute-start | bytes 786440 | tf_op jit(solution)/shard_map/ppermute | solution.py:279
  18.4 7.7 %collective-permute-start.5 = (bf16[1024,128]{1,0:T(8,128)(2,1)S(1)}, bf16[1024,128]{1,0:T(8,128)(2,1)S(1)}, u32[]{:S(2)}, u32[]{:S(2)}) collective-permute-start(bf16[1024,128]{1,0:T(8,128)(2,1)S(1)} %pad_maximum_fusion.refs_0_), channel_id=1, source_target_pairs={{0,16},{1,5},{2,18},{3,7},{4,20},{5,1},{6,22},{7,3},{8,24},{9,13},... | collective-permute-start | bytes 786440 | tf_op jit(solution)/shard_map/ppermute | solution.py:279
  20.0 1.6 %collective-permute-start.8 = (bf16[1024,128]{1,0:T(8,128)(2,1)S(1)}, bf16[1024,128]{1,0:T(8,128)(2,1)S(1)}, u32[]{:S(2)}, u32[]{:S(2)}) collective-permute-start(bf16[1024,128]{1,0:T(8,128)(2,1)S(1)} %constant_dynamic-update-slice_fusion.refs_1_), channel_id=1, source_target_pairs={{0,1},{1,0},{2,3},{3,2},{4,5},{5,4},{6,7},{7,6},{8,9},{9,8},{10,11... | collective-permute-start | bytes 786440 | tf_op jit(solution)/shard_map/ppermute | solution.py:279
  23.3 1.5 %collective-permute-start.9 = (bf16[1024,128]{1,0:T(8,128)(2,1)S(1)}, bf16[1024,128]{1,0:T(8,128)(2,1)S(1)}, u32[]{:S(2)}, u32[]{:S(2)}) collective-permute-start(bf16[1024,128]{1,0:T(8,128)(2,1)S(1)} %collective-permute-done.6.refs_1_), channel_id=1, source_target_pairs={{0,1},{1,0},{2,3},{3,2},{4,5},{5,4},{6,7},{7,6},{8,9},{9,8},{10,11... | collective-permute-start | bytes 786440 | tf_op jit(solution)/shard_map/ppermute | solution.py:279
  26.1 1.5 %collective-permute-start.10 = (bf16[1024,128]{1,0:T(8,128)(2,1)S(1)}, bf16[1024,128]{1,0:T(8,128)(2,1)S(1)}, u32[]{:S(2)}, u32[]{:S(2)}) collective-permute-start(bf16[1024,128]{1,0:T(8,128)(2,1)S(1)} %collective-permute-done.5.refs_1_), channel_id=1, source_target_pairs={{0,1},{1,0},{2,3},{3,2},{4,5},{5,4},{6,7},{7,6},{8,9},{9,8},{10,11... | collective-permute-start | bytes 786440 | tf_op jit(solution)/shard_map/ppermute | solution.py:279

commit v7 on v6

--- a/solution.py
+++ b/solution.py
@@ -247,10 +247,13 @@
         logs = []
         for tile in range(tiles):
             at = ((tile * per_tile + i) ^ own) * parts
-            logs.append(sum(jnp.log(mass[at + part] / sizes) for part in range(parts)))
+            ratio = mass[at] / sizes
+            for part in range(1, parts):
+                ratio = ratio * (mass[at + part] / sizes)
+            logs.append(jnp.log(ratio))
         rest = jnp.concatenate(logs, axis=0)
         pick = (column == place + i * queries).astype(jnp.bfloat16)
-        for _ in range(3):
+        for _ in range(2):
             head = rest.astype(jnp.bfloat16)
             total = total + jnp.dot(head, pick, preferred_element_type=jnp.float32)
             rest = rest - head.astype(jnp.float32)

time: 29.8 us -> 29.7 us (level)
  no operation moved by 1% of the time
where the time goes in v7:
time: 29.7 us; the launch traced here: 29.5 us
  starting transfers between devices  12.6 us (42%)
  Pallas kernels  12.4 us (42%)
  waiting for transfers between devices  4.3 us (14%)
    ppermute x11, starting transfers between devices, swap(): return lax.ppermute(values, ('shard', 'loop'), pairs)  12.6 us
    pallas_call x8, Pallas kernels, add_masses(): pl.pallas_call(functools.partial(mass_kernel, places), out_shape=jax.Shap...  8.66 us
    ppermute x11, waiting for transfers between devices, swap(): return lax.ppermute(values, ('shard', 'loop'), pairs)  4.3 us
    pallas_call x1, Pallas kernels, regroup_documents(): pl.pallas_call(docs_kernel, out_shape=jax.ShapeDtypeStruct((docs * GROUP...  1.73 us
    pallas_call x1, Pallas kernels, document_layout(): pl.pallas_call(layout_kernel, out_shape=(jax.ShapeDtypeStruct((docs * GRO...  0.88 us
    pallas_call x1, Pallas kernels, score(): pl.pallas_call(functools.partial(score_kernel, parts, tokens, relative),...  0.87 us
  transfers between devices with their start and end apart: 11, of which 9 were waited for; matrix products, arithmetic and copies ran while one was open for 0% of the time, Pallas kernels for 36%

profile of v7, /device:TPU:0, one launch (start us, length us, event | category | flops | bytes accessed | tf_op | source)
XLA Modules:
  0.0 29.5 jit_solution(2764672970479871722)
XLA Ops:
  0.0 4.0 %collective-permute-start = (bf16[16,16,128]{2,1,0:T(8,128)(2,1)}, bf16[16,16,128]{2,1,0:T(8,128)(2,1)S(1)}, u32[]{:S(2)}, u32[]{:S(2)}) collective-permute-start(bf16[16,16,128]{2,1,0:T(8,128)(2,1)} %refs_0_.1), channel_id=1, source_target_pairs={{0,8},{1,3},{2,10},{3,1},{4,12},{5,7},{6,14},{7,5},{8,0},{9,11},{1... | collective-permute-start | bytes 196616 | tf_op jit(solution)/shard_map/ppermute | solution.py:282
  4.0 1.6 %collective-permute-start.2 = (bf16[16,16,128]{2,1,0:T(8,128)(2,1)}, bf16[16,16,128]{2,1,0:T(8,128)(2,1)S(1)}, u32[]{:S(2)}, u32[]{:S(2)}) collective-permute-start(bf16[16,16,128]{2,1,0:T(8,128)(2,1)} %refs_0_.1), channel_id=1, source_target_pairs={{0,4},{1,17},{2,6},{3,19},{4,0},{5,21},{6,2},{7,23},{8,12},{9,25},... | collective-permute-start | bytes 196616 | tf_op jit(solution)/shard_map/ppermute | solution.py:282
  5.6 0.9 %layout.1 = (f32[128,128]{1,0:T(8,128)S(1)}, f32[120,128]{1,0:T(8,128)S(1)}, s32[9]{0:T(128)S(4)}, f32[8,128]{1,0:T(8,128)S(1)}) custom-call(s32[8]{0:T(128)} %counts_any.3), custom_call_target="tpu_custom_call" | custom-call | flops 20000000000 | tf_op jit(solution)/shard_map/layout/pallas_call | solution.py:70
  6.5 0.1 collective-permute-done.refs_0_
  6.6 1.8 %collective-permute-start.1 = (bf16[16,16,128]{2,1,0:T(8,128)(2,1)S(1)}, bf16[16,16,128]{2,1,0:T(8,128)(2,1)S(1)}, u32[]{:S(2)}, u32[]{:S(2)}) collective-permute-start(bf16[16,16,128]{2,1,0:T(8,128)(2,1)S(1)} %collective-permute-done.refs_0_), channel_id=1, source_target_pairs={{0,4},{1,17},{2,6},{3,19},{4,0},{5,21},{6,2},{7,23},{8,12},{9,25},... | collective-permute-start | bytes 196616 | tf_op jit(solution)/shard_map/ppermute | solution.py:282
  8.4 0.1 collective-permute-done.2.refs_1_
  8.5 0.1 unit_pieces.3
  8.7 1.6 %collective-permute-start.3 = (bf16[512,128]{1,0:T(8,128)(2,1)S(1)}, bf16[512,128]{1,0:T(8,128)(2,1)S(1)}, u32[]{:S(2)}, u32[]{:S(2)}) collective-permute-start(bf16[512,128]{1,0:T(8,128)(2,1)S(1)} %unit_pieces.3), channel_id=1, source_target_pairs={{0,2},{1,9},{2,0},{3,11},{4,6},{5,13},{6,4},{7,15},{8,10},{9,1},{1... | collective-permute-start | bytes 393224 | tf_op jit(solution)/shard_map/ppermute | solution.py:282
  10.2 1.4 %collective-permute-done.1.refs_1_ = bf16[16,16,128]{2,1,0:T(8,128)(2,1)S(1)} collective-permute-done((bf16[16,16,128]{2,1,0:T(8,128)(2,1)S(1)}, bf16[16,16,128]{2,1,0:T(8,128)(2,1)S(1)}, u32[]{:S(2)}, u32[]{:S(2)}) %collective-permute-start.1) | collective-permute-done | bytes 65568 | tf_op jit(solution)/shard_map/ppermute | solution.py:282
  11.6 0.1 unit_pieces.2
  11.8 1.3 %collective-permute-start.4 = (bf16[512,128]{1,0:T(8,128)(2,1)S(1)}, bf16[512,128]{1,0:T(8,128)(2,1)S(1)}, u32[]{:S(2)}, u32[]{:S(2)}) collective-permute-start(bf16[512,128]{1,0:T(8,128)(2,1)S(1)} %unit_pieces.2), channel_id=1, source_target_pairs={{0,2},{1,9},{2,0},{3,11},{4,6},{5,13},{6,4},{7,15},{8,10},{9,1},{1... | collective-permute-start | bytes 393224 | tf_op jit(solution)/shard_map/ppermute | solution.py:282
  13.1 0.1 collective-permute-start.7
  13.2 1.7 %documents.1.rows = bf16[2112,128]{1,0:T(8,128)(2,1)S(1)} custom-call(s32[8]{0:T(128)} %counts_any.3, bf16[1920,768]{1,0:T(8,128)(2,1)S(1)} %copy-done, bf16[768,128]{1,0:T(8,128)(2,1)S(1)} %copy-done.1), custom_call_target="tpu_custom_call" | custom-call | flops 2500000 | tf_op jit(solution)/shard_map/documents/pallas_call | solution.py:123
  15.0 1.1 %masses.8.refs_0_ = f32[32,8,256]{2,1,0:T(8,128)S(1)} custom-call(bf16[2112,128]{1,0:T(8,128)(2,1)S(1)} %documents.1.rows, f32[128,128]{1,0:T(8,128)S(1)} %get-tuple-element.32.inside, f32[120,128]{1,0:T(8,128)S(1)} %get-tuple-element.33.keep, s32[9]{0:T(128)S(4)} %get-tuple-element.34.last, bf16[1024,128]{1,0:T(8,128)(2,1)S(1)} %pad_maximum_fusion.refs_0_), custom_call_target="tpu_custom_call" | custom-call | flops 20000000000 | tf_op jit(solution)/shard_map/masses/pallas_call | solution.py:219
  16.0 0.8 %collective-permute-done.4 = bf16[512,128]{1,0:T(8,128)(2,1)S(1)} collective-permute-done((bf16[512,128]{1,0:T(8,128)(2,1)S(1)}, bf16[512,128]{1,0:T(8,128)(2,1)S(1)}, u32[]{:S(2)}, u32[]{:S(2)}) %collective-permute-start.4) | collective-permute-done | bytes 131104 | tf_op jit(solution)/shard_map/ppermute | solution.py:282
  16.8 1.6 %collective-permute-start.6 = (bf16[1024,128]{1,0:T(8,128)(2,1)S(1)}, bf16[1024,128]{1,0:T(8,128)(2,1)S(1)}, u32[]{:S(2)}, u32[]{:S(2)}) collective-permute-start(bf16[1024,128]{1,0:T(8,128)(2,1)S(1)} %constant_dynamic-update-slice_fusion.refs_1_), channel_id=1, source_target_pairs={{0,16},{1,5},{2,18},{3,7},{4,20},{5,1},{6,22},{7,3},{8,24},{9,13},... | collective-permute-start | bytes 786440 | tf_op jit(solution)/shard_map/ppermute | solution.py:282
  18.4 0.5 %collective-permute-start.5 = (bf16[1024,128]{1,0:T(8,128)(2,1)S(1)}, bf16[1024,128]{1,0:T(8,128)(2,1)S(1)}, u32[]{:S(2)}, u32[]{:S(2)}) collective-permute-start(bf16[1024,128]{1,0:T(8,128)(2,1)S(1)} %pad_maximum_fusion.refs_0_), channel_id=1, source_target_pairs={{0,16},{1,5},{2,18},{3,7},{4,20},{5,1},{6,22},{7,3},{8,24},{9,13},... | collective-permute-start | bytes 786440 | tf_op jit(solution)/shard_map/ppermute | solution.py:282
  18.9 1.0 %masses.9.refs_0_ = f32[32,8,256]{2,1,0:T(8,128)S(1)} custom-call(bf16[2112,128]{1,0:T(8,128)(2,1)S(1)} %documents.1.rows, f32[128,128]{1,0:T(8,128)S(1)} %get-tuple-element.32.inside, f32[120,128]{1,0:T(8,128)S(1)} %get-tuple-element.33.keep, s32[9]{0:T(128)S(4)} %get-tuple-element.34.last, ...), custom_call_target="tpu_custom_call", output_to_operand_aliasing={{}: (4, {})} | custom-call | flops 20000000000 | tf_op jit(solution)/shard_map/masses/pallas_call | solution.py:219
  20.0 0.1 collective-permute-start.8
  20.1 1.2 %masses.10.refs_0_ = f32[32,8,256]{2,1,0:T(8,128)S(1)} custom-call(bf16[2112,128]{1,0:T(8,128)(2,1)S(1)} %documents.1.rows, f32[128,128]{1,0:T(8,128)S(1)} %get-tuple-element.32.inside, f32[120,128]{1,0:T(8,128)S(1)} %get-tuple-element.33.keep, s32[9]{0:T(128)S(4)} %get-tuple-element.34.last, ...), custom_call_target="tpu_custom_call", output_to_operand_aliasing={{}: (4, {})} | custom-call | flops 20000000000 | tf_op jit(solution)/shard_map/masses/pallas_call | solution.py:219
  21.3 0.3 collective-permute-done.8.refs_1_
  21.6 1.0 %masses.11.refs_0_ = f32[32,8,256]{2,1,0:T(8,128)S(1)} custom-call(bf16[2112,128]{1,0:T(8,128)(2,1)S(1)} %documents.1.rows, f32[128,128]{1,0:T(8,128)S(1)} %get-tuple-element.32.inside, f32[120,128]{1,0:T(8,128)S(1)} %get-tuple-element.33.keep, s32[9]{0:T(128)S(4)} %get-tuple-element.34.last, ...), custom_call_target="tpu_custom_call", output_to_operand_aliasing={{}: (4, {})} | custom-call | flops 20000000000 | tf_op jit(solution)/shard_map/masses/pallas_call | solution.py:219
  22.6 0.6 %collective-permute-done.6.refs_1_ = bf16[1024,128]{1,0:T(8,128)(2,1)S(1)} collective-permute-done((bf16[1024,128]{1,0:T(8,128)(2,1)S(1)}, bf16[1024,128]{1,0:T(8,128)(2,1)S(1)}, u32[]{:S(2)}, u32[]{:S(2)}) %collective-permute-start.6) | collective-permute-done | bytes 262176 | tf_op jit(solution)/shard_map/ppermute | solution.py:282
  23.3 0.0 collective-permute-start.9
  23.3 1.0 %masses.12.refs_0_ = f32[32,8,256]{2,1,0:T(8,128)S(1)} custom-call(bf16[2112,128]{1,0:T(8,128)(2,1)S(1)} %documents.1.rows, f32[128,128]{1,0:T(8,128)S(1)} %get-tuple-element.32.inside, f32[120,128]{1,0:T(8,128)S(1)} %get-tuple-element.33.keep, s32[9]{0:T(128)S(4)} %get-tuple-element.34.last, ...), custom_call_target="tpu_custom_call", output_to_operand_aliasing={{}: (4, {})} | custom-call | flops 20000000000 | tf_op jit(solution)/shard_map/masses/pallas_call | solution.py:219
  24.3 0.5 %collective-permute-done.9.refs_1_ = bf16[1024,128]{1,0:T(8,128)(2,1)S(1)} collective-permute-done((bf16[1024,128]{1,0:T(8,128)(2,1)S(1)}, bf16[1024,128]{1,0:T(8,128)(2,1)S(1)}, u32[]{:S(2)}, u32[]{:S(2)}) %collective-permute-start.9) | collective-permute-done | bytes 262176 | tf_op jit(solution)/shard_map/ppermute | solution.py:282
  24.8 1.0 %masses.13.refs_0_ = f32[32,8,256]{2,1,0:T(8,128)S(1)} custom-call(bf16[2112,128]{1,0:T(8,128)(2,1)S(1)} %documents.1.rows, f32[128,128]{1,0:T(8,128)S(1)} %get-tuple-element.32.inside, f32[120,128]{1,0:T(8,128)S(1)} %get-tuple-element.33.keep, s32[9]{0:T(128)S(4)} %get-tuple-element.34.last, ...), custom_call_target="tpu_custom_call", output_to_operand_aliasing={{}: (4, {})} | custom-call | flops 20000000000 | tf_op jit(solution)/shard_map/masses/pallas_call | solution.py:219
  25.9 0.2 collective-permute-done.5.refs_1_
  26.1 1.2 %masses.14.refs_0_ = f32[32,8,256]{2,1,0:T(8,128)S(1)} custom-call(bf16[2112,128]{1,0:T(8,128)(2,1)S(1)} %documents.1.rows, f32[128,128]{1,0:T(8,128)S(1)} %get-tuple-element.32.inside, f32[120,128]{1,0:T(8,128)S(1)} %get-tuple-element.33.keep, s32[9]{0:T(128)S(4)} %get-tuple-element.34.last, ...), custom_call_target="tpu_custom_call", output_to_operand_aliasing={{}: (4, {})} | custom-call | flops 20000000000 | tf_op jit(solution)/shard_map/masses/pallas_call | solution.py:219
  27.3 0.4 %collective-permute-done.10.refs_1_ = bf16[1024,128]{1,0:T(8,128)(2,1)S(1)} collective-permute-done((bf16[1024,128]{1,0:T(8,128)(2,1)S(1)}, bf16[1024,128]{1,0:T(8,128)(2,1)S(1)}, u32[]{:S(2)}, u32[]{:S(2)}) %collective-permute-start.10) | collective-permute-done | bytes 262176 | tf_op jit(solution)/shard_map/ppermute | solution.py:282
  27.6 1.0 %masses.15.mass = f32[32,8,256]{2,1,0:T(8,128)S(1)} custom-call(bf16[2112,128]{1,0:T(8,128)(2,1)S(1)} %documents.1.rows, f32[128,128]{1,0:T(8,128)S(1)} %get-tuple-element.32.inside, f32[120,128]{1,0:T(8,128)S(1)} %get-tuple-element.33.keep, s32[9]{0:T(128)S(4)} %get-tuple-element.34.last, ...), custom_call_target="tpu_custom_call", output_to_operand_aliasing={{}: (4, {})} | custom-call | flops 20000000000 | tf_op jit(solution)/shard_map/masses/pallas_call | solution.py:219
  28.7 0.9 %scores.1 = f32[8,256]{1,0:T(8,128)} custom-call(f32[8,128]{1,0:T(8,128)S(1)} %get-tuple-element.29.lengths, f32[32,8,256]{2,1,0:T(8,128)S(1)} %masses.15.mass), custom_call_target="tpu_custom_call" | custom-call | flops 1000000 | tf_op jit(solution)/shard_map/scores/pallas_call | solution.py:268
  (12 shorter events, 0.1 us)
Async XLA Ops:
  0.0 8.5 %copy-start.2 = (bf16[16,16,128]{2,1,0:T(8,128)(2,1)S(1)}, bf16[16,16,128]{2,1,0:T(8,128)(2,1)}, u32[]{:S(2)}) copy-start(bf16[16,16,128]{2,1,0:T(8,128)(2,1)} %refs_0_.1) | copy-start | bytes 196612
  0.0 13.2 %copy-start.1 = (bf16[768,128]{1,0:T(8,128)(2,1)S(1)}, bf16[768,128]{1,0:T(8,128)(2,1)}, u32[]{:S(2)}) copy-start(bf16[768,128]{1,0:T(8,128)(2,1)} %w_proj.1) | copy-start | bytes 589828
  0.0 6.6 %collective-permute-start = (bf16[16,16,128]{2,1,0:T(8,128)(2,1)}, bf16[16,16,128]{2,1,0:T(8,128)(2,1)S(1)}, u32[]{:S(2)}, u32[]{:S(2)}) collective-permute-start(bf16[16,16,128]{2,1,0:T(8,128)(2,1)} %refs_0_.1), channel_id=1, source_target_pairs={{0,8},{1,3},{2,10},{3,1},{4,12},{5,7},{6,14},{7,5},{8,0},{9,11},{1... | collective-permute-start | bytes 196616 | tf_op jit(solution)/shard_map/ppermute | solution.py:282
  4.0 4.5 %collective-permute-start.2 = (bf16[16,16,128]{2,1,0:T(8,128)(2,1)}, bf16[16,16,128]{2,1,0:T(8,128)(2,1)S(1)}, u32[]{:S(2)}, u32[]{:S(2)}) collective-permute-start(bf16[16,16,128]{2,1,0:T(8,128)(2,1)} %refs_0_.1), channel_id=1, source_target_pairs={{0,4},{1,17},{2,6},{3,19},{4,0},{5,21},{6,2},{7,23},{8,12},{9,25},... | collective-permute-start | bytes 196616 | tf_op jit(solution)/shard_map/ppermute | solution.py:282
  5.6 7.6 %copy-start = (bf16[1920,768]{1,0:T(8,128)(2,1)S(1)}, bf16[1920,768]{1,0:T(8,128)(2,1)}, u32[]{:S(2)}) copy-start(bf16[1920,768]{1,0:T(8,128)(2,1)} %hidden) | copy-start | bytes 8847364
  6.6 5.0 %collective-permute-start.1 = (bf16[16,16,128]{2,1,0:T(8,128)(2,1)S(1)}, bf16[16,16,128]{2,1,0:T(8,128)(2,1)S(1)}, u32[]{:S(2)}, u32[]{:S(2)}) collective-permute-start(bf16[16,16,128]{2,1,0:T(8,128)(2,1)S(1)} %collective-permute-done.refs_0_), channel_id=1, source_target_pairs={{0,4},{1,17},{2,6},{3,19},{4,0},{5,21},{6,2},{7,23},{8,12},{9,25},... | collective-permute-start | bytes 196616 | tf_op jit(solution)/shard_map/ppermute | solution.py:282
  8.7 7.3 %collective-permute-start.3 = (bf16[512,128]{1,0:T(8,128)(2,1)S(1)}, bf16[512,128]{1,0:T(8,128)(2,1)S(1)}, u32[]{:S(2)}, u32[]{:S(2)}) collective-permute-start(bf16[512,128]{1,0:T(8,128)(2,1)S(1)} %unit_pieces.3), channel_id=1, source_target_pairs={{0,2},{1,9},{2,0},{3,11},{4,6},{5,13},{6,4},{7,15},{8,10},{9,1},{1... | collective-permute-start | bytes 393224 | tf_op jit(solution)/shard_map/ppermute | solution.py:282
  11.8 5.0 %collective-permute-start.4 = (bf16[512,128]{1,0:T(8,128)(2,1)S(1)}, bf16[512,128]{1,0:T(8,128)(2,1)S(1)}, u32[]{:S(2)}, u32[]{:S(2)}) collective-permute-start(bf16[512,128]{1,0:T(8,128)(2,1)S(1)} %unit_pieces.2), channel_id=1, source_target_pairs={{0,2},{1,9},{2,0},{3,11},{4,6},{5,13},{6,4},{7,15},{8,10},{9,1},{1... | collective-permute-start | bytes 393224 | tf_op jit(solution)/shard_map/ppermute | solution.py:282
  13.1 5.8 %collective-permute-start.7 = (bf16[1024,128]{1,0:T(8,128)(2,1)S(1)}, bf16[1024,128]{1,0:T(8,128)(2,1)S(1)}, u32[]{:S(2)}, u32[]{:S(2)}) collective-permute-start(bf16[1024,128]{1,0:T(8,128)(2,1)S(1)} %pad_maximum_fusion.refs_0_), channel_id=1, source_target_pairs={{0,1},{1,0},{2,3},{3,2},{4,5},{5,4},{6,7},{7,6},{8,9},{9,8},{10,11... | collective-permute-start | bytes 786440 | tf_op jit(solution)/shard_map/ppermute | solution.py:282
  16.8 6.4 %collective-permute-start.6 = (bf16[1024,128]{1,0:T(8,128)(2,1)S(1)}, bf16[1024,128]{1,0:T(8,128)(2,1)S(1)}, u32[]{:S(2)}, u32[]{:S(2)}) collective-permute-start(bf16[1024,128]{1,0:T(8,128)(2,1)S(1)} %constant_dynamic-update-slice_fusion.refs_1_), channel_id=1, source_target_pairs={{0,16},{1,5},{2,18},{3,7},{4,20},{5,1},{6,22},{7,3},{8,24},{9,13},... | collective-permute-start | bytes 786440 | tf_op jit(solution)/shard_map/ppermute | solution.py:282
  18.4 7.7 %collective-permute-start.5 = (bf16[1024,128]{1,0:T(8,128)(2,1)S(1)}, bf16[1024,128]{1,0:T(8,128)(2,1)S(1)}, u32[]{:S(2)}, u32[]{:S(2)}) collective-permute-start(bf16[1024,128]{1,0:T(8,128)(2,1)S(1)} %pad_maximum_fusion.refs_0_), channel_id=1, source_target_pairs={{0,16},{1,5},{2,18},{3,7},{4,20},{5,1},{6,22},{7,3},{8,24},{9,13},... | collective-permute-start | bytes 786440 | tf_op jit(solution)/shard_map/ppermute | solution.py:282
  20.0 1.6 %collective-permute-start.8 = (bf16[1024,128]{1,0:T(8,128)(2,1)S(1)}, bf16[1024,128]{1,0:T(8,128)(2,1)S(1)}, u32[]{:S(2)}, u32[]{:S(2)}) collective-permute-start(bf16[1024,128]{1,0:T(8,128)(2,1)S(1)} %constant_dynamic-update-slice_fusion.refs_1_), channel_id=1, source_target_pairs={{0,1},{1,0},{2,3},{3,2},{4,5},{5,4},{6,7},{7,6},{8,9},{9,8},{10,11... | collective-permute-start | bytes 786440 | tf_op jit(solution)/shard_map/ppermute | solution.py:282
  23.3 1.5 %collective-permute-start.9 = (bf16[1024,128]{1,0:T(8,128)(2,1)S(1)}, bf16[1024,128]{1,0:T(8,128)(2,1)S(1)}, u32[]{:S(2)}, u32[]{:S(2)}) collective-permute-start(bf16[1024,128]{1,0:T(8,128)(2,1)S(1)} %collective-permute-done.6.refs_1_), channel_id=1, source_target_pairs={{0,1},{1,0},{2,3},{3,2},{4,5},{5,4},{6,7},{7,6},{8,9},{9,8},{10,11... | collective-permute-start | bytes 786440 | tf_op jit(solution)/shard_map/ppermute | solution.py:282
  26.1 1.5 %collective-permute-start.10 = (bf16[1024,128]{1,0:T(8,128)(2,1)S(1)}, bf16[1024,128]{1,0:T(8,128)(2,1)S(1)}, u32[]{:S(2)}, u32[]{:S(2)}) collective-permute-start(bf16[1024,128]{1,0:T(8,128)(2,1)S(1)} %collective-permute-done.5.refs_1_), channel_id=1, source_target_pairs={{0,1},{1,0},{2,3},{3,2},{4,5},{5,4},{6,7},{7,6},{8,9},{9,8},{10,11... | collective-permute-start | bytes 786440 | tf_op jit(solution)/shard_map/ppermute | solution.py:282
